TPU v7x, 32 devices: a whole 2x2x4 slice. The times are simulated.
32 devices in a mesh: seq: 8 (over z, core), head: 4 (over y, x).
Axes of the slice: x: 2, y: 2, z: 4, core: 2. Of those that a mesh axis runs over, the one named last changes fastest.
Arguments:
- queries: bfloat16 [8192, 2048], P('seq', 'head'), may hold values from -1.5 to 1.5
- keys: bfloat16 [8192, 2048], P('seq', 'head'), may hold values from -1.5 to 1.5
- values: bfloat16 [8192, 2048], P('seq', 'head'), may hold values from -6 to 6
- log_decay: float32 [16, 8192], P('head', 'seq'), may hold values from -2 to 0, as said below
- out_weight: bfloat16 [2048, 2048], P(None, 'head'), may hold values from -0.125 to 0.125
- out_grad: bfloat16 [8192, 2048], P('seq', 'head'), may hold values from -0.75 to 0.75
Outputs:
- attended: bfloat16 [8192, 2048], P('seq', 'head')
- query_grad: bfloat16 [8192, 2048], P('seq', 'head')
- key_grad: bfloat16 [8192, 2048], P('seq', 'head')
- value_grad: bfloat16 [8192, 2048], P('seq', 'head')
- weight_grad: bfloat16 [2048, 2048], P('seq', 'head')
Inputs may be any that keep to these rules, and one draw needn't show every extreme that they name: `log_decay`: natural logarithm of the factor by which a head's state is multiplied before the token's own key and value are added; always negative.
All inputs are finite; a program needn't handle non-finite values.
Results may differ from a plain program's by a relative error of at most 0.0069.
Values may be sent and summed in bfloat16 or wider, within the bound.
No kernel may reach another device: no remote copies, remote signals or barrier semaphores. Data moves between devices by JAX's collectives and lax.ppermute only.
A program may use at most 64 MiB of HBM per device.

v0:
```python
import jax
import jax.numpy as jnp
from jax import lax
from jax.sharding import PartitionSpec as P

HIGH = lax.Precision.HIGHEST


def chain_weights(totals, position, upward):
    number = totals.shape[0]
    source = lax.broadcasted_iota(jnp.int32, (number, number), 0)
    middle = lax.broadcasted_iota(jnp.int32, (number, number), 1)
    column = lax.broadcasted_iota(jnp.int32, (number, 1), 0)
    if upward:
        between = (middle > position) & (middle < source)
        usable = column > position
    else:
        between = (middle > source) & (middle < position)
        usable = column < position
    span_sums = jnp.dot(between.astype(jnp.float32), totals, precision=HIGH)
    return jnp.where(usable, jnp.exp(span_sums), 0.0)


def weighted_sum(factor_table, shards):
    return jnp.sum(factor_table[:, :, None, None] * shards, axis=0)


def on_device(queries, keys, values, log_decay, out_weight, out_grad):
    length, columns = queries.shape
    heads_here = log_decay.shape[0]
    head_size = columns // heads_here
    shaped = (length, heads_here, head_size)
    query_rows = queries.reshape(shaped)
    key_rows = keys.reshape(shaped)
    value_rows = values.reshape(shaped)
    running = jnp.cumsum(log_decay, axis=1)
    totals = running[:, -1]
    row_index = lax.broadcasted_iota(jnp.int32, (length, length), 0)
    col_index = lax.broadcasted_iota(jnp.int32, (length, length), 1)
    causal = (row_index >= col_index)[None]
    spread = running[:, :, None] - running[:, None, :]
    decay = jnp.where(causal, jnp.exp(jnp.where(causal, spread, 0.0)), 0.0)
    scores = jnp.einsum("thd,shd->hts", query_rows, key_rows, preferred_element_type=jnp.float32)
    weights = (scores * decay).astype(jnp.bfloat16)
    growth = jnp.exp(running).T
    tail_decay = jnp.exp(totals[None, :] - running.T)
    key_tail = (key_rows * tail_decay[:, :, None]).astype(jnp.bfloat16)
    value_tail = (value_rows * tail_decay[:, :, None]).astype(jnp.bfloat16)
    query_grown = (query_rows * growth[:, :, None]).astype(jnp.bfloat16)
    update = jnp.einsum("thd,the->hde", key_tail, value_rows, preferred_element_type=jnp.float32)
    gathered = lax.all_gather(totals[None, :], "seq", axis=0, tiled=True)
    position = lax.axis_index("seq")
    before = chain_weights(gathered, position, False)
    incoming = weighted_sum(before, lax.all_gather(update[None], "seq", axis=0, tiled=True))
    incoming_low = incoming.astype(jnp.bfloat16)
    local_part = jnp.einsum("hts,she->the", weights, value_rows, preferred_element_type=jnp.float32)
    carried = jnp.einsum(
        "thd,hde->the", query_grown, incoming_low, preferred_element_type=jnp.float32
    )
    mixed = local_part + carried
    root_mean = jnp.sqrt(jnp.mean(mixed * mixed, axis=2, keepdims=True) + 1e-05)
    normed = mixed / root_mean
    attended = normed.astype(jnp.bfloat16)
    full_grad = lax.all_gather(out_grad, "head", axis=1, tiled=True)
    head_grad = jnp.dot(full_grad, out_weight, preferred_element_type=jnp.float32).reshape(shaped)
    norm_grad = (
        head_grad - normed * jnp.mean(head_grad * normed, axis=2, keepdims=True)
    ) / root_mean
    mixed_grad = norm_grad.astype(jnp.bfloat16)
    grad_grown = (mixed_grad * growth[:, :, None]).astype(jnp.bfloat16)
    pair_grad = jnp.einsum(
        "thd,shd->hts", mixed_grad, value_rows, preferred_element_type=jnp.float32
    )
    masked_grad = (pair_grad * decay).astype(jnp.bfloat16)
    back_update = jnp.einsum(
        "thd,the->hde", query_grown, mixed_grad, preferred_element_type=jnp.float32
    )
    after = chain_weights(gathered, position, True)
    outgoing = weighted_sum(after, lax.all_gather(back_update[None], "seq", axis=0, tiled=True))
    outgoing_low = outgoing.astype(jnp.bfloat16)
    query_grad = jnp.einsum(
        "hts,shd->thd", masked_grad, key_rows, preferred_element_type=jnp.float32
    ) + jnp.einsum("the,hde->thd", grad_grown, incoming_low, preferred_element_type=jnp.float32)
    key_grad = jnp.einsum(
        "hts,thd->shd", masked_grad, query_rows, preferred_element_type=jnp.float32
    ) + jnp.einsum("she,hde->shd", value_tail, outgoing_low, preferred_element_type=jnp.float32)
    value_grad = jnp.einsum(
        "hts,the->she", weights, mixed_grad, preferred_element_type=jnp.float32
    ) + jnp.einsum("shd,hde->she", key_tail, outgoing_low, preferred_element_type=jnp.float32)
    attended_flat = attended.reshape(length, columns)
    weight_grad = lax.psum_scatter(
        lax.dot_general(
            full_grad, attended_flat, (((0,), (0,)), ((), ())), preferred_element_type=jnp.float32
        ),
        "seq",
        scatter_dimension=0,
        tiled=True,
    )
    return (
        attended_flat,
        query_grad.astype(jnp.bfloat16).reshape(length, columns),
        key_grad.astype(jnp.bfloat16).reshape(length, columns),
        value_grad.astype(jnp.bfloat16).reshape(length, columns),
        weight_grad.astype(jnp.bfloat16),
    )


def solution(mesh):
    return jax.shard_map(
        on_device,
        mesh=mesh,
        in_specs=(
            P("seq", "head"),
            P("seq", "head"),
            P("seq", "head"),
            P("head", "seq"),
            P(None, "head"),
            P("seq", "head"),
        ),
        out_specs=(
            P("seq", "head"),
            P("seq", "head"),
            P("seq", "head"),
            P("seq", "head"),
            P("seq", "head"),
        ),
        check_vma=False,
    )
```

profile of v0, /device:TPU:0, one launch (start us, length us, event | category | flops | bytes accessed | tf_op | source)
XLA Modules:
  0.0 198.2 jit_solution(1714559132739994037)
XLA Ops:
  7.2 0.9 copy.135
  8.1 1.1 reduce-window.6
  9.9 3.6 %fusion.9 = f32[4,128,128]{2,1,0:T(8,128)} fusion(f32[1024,4]{0,1:T(4,128)S(1)} %get-tuple-element.22, bf16[1024,512]{1,0:T(8,128)(2,1)} %param.8, bf16[1024,512]{1,0:T(8,128)(2,1)} %param.7), kind=kOutput, calls=%fused_computation.29 | convolution fusion | flops 135790592 | bytes 2375680 | tf_op jit(solution)/shard_map/thd,the->hde/dot_general | solution.py:50
  13.6 0.7 all-gather.7.cloned.1.call-update
  15.7 18.4 %all-reduce = f32[32]{0:T(128)S(1)} all-reduce(f32[32]{0:T(128)S(1)} %bitcast_dynamic-update-slice_fusion), channel_id=2, replica_groups=mesh['seq'=8,'head'=4] {'seq'}, use_global_device_ids=true, to_apply=%add | all-reduce | flops 32 | bytes 256
  34.4 1.5 copy.59
  36.3 7.6 %multiply_convert_fusion.1 = bf16[4,1024,1024]{2,1,0:T(8,128)(2,1)S(1)} fusion(bf16[1024,4,128]{0,2,1:T(8,128)(2,1)S(1)} %bitcast.115, f32[4,1024]{1,0:T(4,128)S(1)} %bitcast.128, pred[1024,1024]{1,0:T(8,128)(4,1)S(1)} %iota_compare_fusion, bf16[1024,512]{1,0:T(8,128)(2,1)} %param.7), kind=kOutput, calls=%fused_computation.1 | convolution fusion | flops 1094713344 | bytes 11550720 | tf_op jit(solution)/shard_map/thd,shd->hts/dot_general | solution.py:43
  43.9 3.2 %copy-done.1 = bf16[4,1024,1024]{2,1,0:T(8,128)(2,1)} copy-done((bf16[4,1024,1024]{2,1,0:T(8,128)(2,1)}, bf16[4,1024,1024]{2,1,0:T(8,128)(2,1)S(1)}, u32[]{:S(2)}) %copy-start.1) | copy-done | bytes 8388632
  47.1 4.2 %fusion.5 = f32[4,1024,128]{1,2,0:T(8,128)} fusion(bf16[4,1024,1024]{2,1,0:T(8,128)(2,1)S(1)} %multiply_convert_fusion.1, bf16[1024,512]{1,0:T(8,128)(2,1)S(1)} %copy-done.8), kind=kOutput, calls=%fused_computation.25 | convolution fusion | flops 1073741824 | bytes 11534336 | tf_op jit(solution)/shard_map/hts,she->the/dot_general | solution.py:56
  51.3 2.0 multiply_reduce_fusion.3
  53.6 1.9 multiply_reduce_fusion.2
  55.6 44.0 %all-gather.7.cloned.1.call-done = bf16[1024,2048]{1,0:T(8,128)(2,1)} async-done(((bf16[1024,512]{1,0:T(8,128)(2,1)}), bf16[1024,2048]{1,0:T(8,128)(2,1)}) %all-gather.7.cloned.1.call-update) | async-done | bytes 4194320 | tf_op jit(solution)/shard_map/all_gather | solution.py:64
  99.5 5.4 %multiply_reduce_fusion.1 = (f32[1024,4]{0,1:T(4,128)S(1)}, f32[1024,512]{0,1:T(8,128)S(1)}) fusion(f32[1024,4,128]{0,2,1:T(8,128)} %get-tuple-element.25, f32[1024,4]{0,1:T(4,128)S(1)} %add_sqrt_fusion, bf16[1024,2048]{1,0:T(8,128)(2,1)} %all-gather.7.cloned.1.call-done, bf16[2048,512]{1,0:T(8,128)(2,1)S(1)} %copy-done), kind=kOutput, calls=%fused_computation.15 | convolution fusion | flops 2149052416 | bytes 10518528 | tf_op jit(solution)/shard_map/dot_general | solution.py:65
  104.9 1.6 divide_convert_fusion
  106.5 1.0 copy-done.4
  107.5 1.1 fusion.16
  108.9 6.8 %convolution_bitcast_fusion = f32[2048,512]{0,1:T(8,128)} fusion(bf16[1024,512]{0,1:T(8,128)(2,1)} %bitcast.120, bf16[1024,2048]{1,0:T(8,128)(2,1)} %all-gather.7.cloned.1.call-done), kind=kOutput, calls=%fused_computation.4 | convolution fusion | flops 2147483648 | bytes 9437184 | tf_op jit(solution)/shard_map/dot_general | solution.py:92
  116.0 2.3 %copy.78 = bf16[1024,512]{1,0:T(8,128)(2,1)} copy(bf16[1024,512]{0,1:T(8,128)(2,1)} %bitcast.121) | data formatting | bytes 2097152
  118.3 7.6 %multiply_convert_fusion = bf16[4,1024,1024]{2,1,0:T(8,128)(2,1)S(1)} fusion(bf16[1024,4,128]{0,2,1:T(8,128)(2,1)} %copy-done.4, f32[4,1024]{1,0:T(4,128)S(1)} %bitcast.129, pred[1024,1024]{1,0:T(8,128)(4,1)} %copy-done.10, bf16[1024,512]{1,0:T(8,128)(2,1)} %param.8), kind=kOutput, calls=%fused_computation | convolution fusion | flops 1094713344 | bytes 11550720 | tf_op jit(solution)/shard_map/thd,shd->hts/dot_general | solution.py:71
  125.9 2.9 %fusion.11 = f32[4,1024,128]{1,2,0:T(8,128)S(1)} fusion(bf16[4,1024,1024]{2,1,0:T(8,128)(2,1)S(1)} %multiply_convert_fusion, bf16[1024,512]{1,0:T(8,128)(2,1)S(1)} %copy-done.9), kind=kOutput, calls=%fused_computation.31 | convolution fusion | flops 1073741824 | bytes 11534336 | tf_op jit(solution)/shard_map/hts,shd->thd/dot_general | solution.py:81
  129.1 1.4 fusion.1
  130.5 2.3 %copy.79 = bf16[1024,512]{1,0:T(8,128)(2,1)} copy(bf16[1024,512]{0,1:T(8,128)(2,1)} %bitcast.122) | data formatting | bytes 2097152
  132.8 6.4 %fusion.36 = f32[4,128,1024]{2,1,0:T(8,128)} fusion(bf16[1024,4,128]{0,2,1:T(8,128)(2,1)} %copy-done.4, bf16[4,1024,1024]{2,1,0:T(8,128)(2,1)} %copy-done.1), kind=kOutput, calls=%fused_computation.68 | convolution fusion | flops 1073741824 | bytes 11534336 | tf_op jit(solution)/shard_map/hts,the->she/dot_general | solution.py:87
  139.2 2.0 multiply_reduce_fusion
  141.4 3.2 %add_convert_fusion = bf16[4,128,1024]{2,1,0:T(8,128)(2,1)} fusion(f32[4,128,1024]{2,1,0:T(8,128)S(1)} %copy-done.6, f32[1024,4]{0,1:T(4,128)S(1)} %get-tuple-element.22, bf16[4,128,128]{2,1,0:T(8,128)(2,1)S(1)} %multiply_reduce_fusion, bf16[1024,512]{1,0:T(8,128)(2,1)} %param.7), kind=kOutput, calls=%fused_computation.10 | convolution fusion | flops 136839168 | bytes 4341760 | tf_op jit(solution)/shard_map/shd,hde->she/dot_general | solution.py:89
  144.6 2.4 %copy.81 = bf16[1024,512]{1,0:T(8,128)(2,1)} copy(bf16[1024,512]{0,1:T(8,128)(2,1)} %bitcast.123) | data formatting | bytes 2097152
  147.0 2.2 %fusion.4 = f32[4,128,1024]{2,1,0:T(8,128)S(1)} fusion(f32[1024,4]{0,1:T(4,128)S(1)} %get-tuple-element.22, bf16[4,128,128]{2,1,0:T(8,128)(2,1)S(1)} %multiply_reduce_fusion, bf16[1024,512]{1,0:T(8,128)(2,1)} %param.8), kind=kOutput, calls=%fused_computation.24 | convolution fusion | flops 135790592 | bytes 3293184 | tf_op jit(solution)/shard_map/she,hde->shd/dot_general | solution.py:86
  149.2 5.7 %fusion = bf16[1024,4,128]{0,2,1:T(8,128)(2,1)} fusion(f32[4,128,1024]{2,1,0:T(8,128)S(1)} %fusion.4, bf16[1024,4,128]{0,2,1:T(8,128)(2,1)S(1)} %bitcast.118, bf16[4,1024,1024]{2,1,0:T(8,128)(2,1)} %copy-done.2), kind=kOutput, calls=%fused_computation.6 | convolution fusion | flops 1074790400 | bytes 12582912 | tf_op jit(solution)/shard_map/hts,thd->shd/dot_general | solution.py:84
  154.8 2.3 %copy.80 = bf16[1024,512]{1,0:T(8,128)(2,1)} copy(bf16[1024,512]{0,1:T(8,128)(2,1)} %bitcast.119) | data formatting | bytes 2097152
  157.1 32.6 %reduce-scatter.2.cloned.1.call-done = f32[256,512]{0,1:T(8,128)} async-done(((f32[2048,512]{0,1:T(8,128)}), f32[256,512]{0,1:T(8,128)}) %reduce-scatter.2.cloned.1.call-update) | async-done | bytes 524304 | tf_op jit(solution)/shard_map/reduce_scatter | solution.py:91
  189.7 1.1 convert_element_type.77
  190.8 0.8 copy.82
  (50 shorter events, 3.7 us)
Async XLA Ops:
  7.2 92.4 %copy-start = (bf16[2048,512]{1,0:T(8,128)(2,1)S(1)}, bf16[2048,512]{1,0:T(8,128)(2,1)}, u32[]{:S(2)}) copy-start(bf16[2048,512]{1,0:T(8,128)(2,1)} %param.10) | copy-start | bytes 6291460
  7.2 44.1 %all-gather.9.cloned.1.call-start = ((), (), s32[]{:S(2)}) async-start(), calls=%async_computation.3 | async-start | bytes 2359296 | tf_op jit(solution)/shard_map/all_gather | solution.py:54
  9.9 4.4 %copy-start.11 = (u32[32]{0:T(128)S(1)}, u32[32]{0:T(128)}, u32[]{:S(2)}) copy-start(u32[32]{0:T(128)} %constant.19) | copy-start | bytes 388
  13.5 86.0 %all-gather.7.cloned.1.call-start = ((), (), s32[]{:S(2)}) async-start(), calls=%async_computation.1 | async-start | bytes 5242880 | tf_op jit(solution)/shard_map/all_gather | solution.py:64
  14.3 124.9 %all-gather.11.cloned.1.call-start = ((), (), s32[]{:S(2)}) async-start(), calls=%async_computation.4 | async-start | bytes 2359296 | tf_op jit(solution)/shard_map/all_gather | solution.py:79
  36.2 7.6 %copy-start.10 = (pred[1024,1024]{1,0:T(8,128)(4,1)}, pred[1024,1024]{1,0:T(8,128)(4,1)S(1)}, u32[]{:S(2)}) copy-start(pred[1024,1024]{1,0:T(8,128)(4,1)S(1)} %iota_compare_fusion) | copy-start | bytes 3145732
  36.3 10.9 %copy-start.8 = (bf16[1024,512]{1,0:T(8,128)(2,1)S(1)}, bf16[1024,512]{1,0:T(8,128)(2,1)}, u32[]{:S(2)}) copy-start(bf16[1024,512]{1,0:T(8,128)(2,1)} %param.8) | copy-start | bytes 3145732
  43.9 3.2 %copy-start.1 = (bf16[4,1024,1024]{2,1,0:T(8,128)(2,1)}, bf16[4,1024,1024]{2,1,0:T(8,128)(2,1)S(1)}, u32[]{:S(2)}) copy-start(bf16[4,1024,1024]{2,1,0:T(8,128)(2,1)S(1)} %multiply_convert_fusion.1) | copy-start | bytes 25165828
  51.3 2.3 %copy-start.7 = (f32[4,1024,128]{1,2,0:T(8,128)S(1)}, f32[4,1024,128]{1,2,0:T(8,128)}, u32[]{:S(2)}) copy-start(f32[4,1024,128]{1,2,0:T(8,128)} %fusion.5) | copy-start | bytes 6291460
  99.5 5.4 %copy-start.3 = (f32[1024,4,128]{0,2,1:T(8,128)S(1)}, f32[1024,4,128]{0,2,1:T(8,128)}, u32[]{:S(2)}) copy-start(f32[1024,4,128]{0,2,1:T(8,128)} %get-tuple-element.25) | copy-start | bytes 6291460
  106.5 1.0 copy-start.4
  108.7 81.0 %reduce-scatter.2.cloned.1.call-start = ((), (), s32[]{:S(2)}) async-start(), calls=%async_computation.2 | async-start | bytes 4718592 | tf_op jit(solution)/shard_map/reduce_scatter | solution.py:91
  118.3 7.6 %copy-start.9 = (bf16[1024,512]{1,0:T(8,128)(2,1)S(1)}, bf16[1024,512]{1,0:T(8,128)(2,1)}, u32[]{:S(2)}) copy-start(bf16[1024,512]{1,0:T(8,128)(2,1)} %param.7) | copy-start | bytes 3145732
  125.9 3.2 %copy-start.2 = (bf16[4,1024,1024]{2,1,0:T(8,128)(2,1)}, bf16[4,1024,1024]{2,1,0:T(8,128)(2,1)S(1)}, u32[]{:S(2)}) copy-start(bf16[4,1024,1024]{2,1,0:T(8,128)(2,1)S(1)} %multiply_convert_fusion) | copy-start | bytes 25165828
  125.9 3.2 %copy-start.5 = (bf16[1024,4,128]{0,2,1:T(8,128)(2,1)S(1)}, bf16[1024,4,128]{0,2,1:T(8,128)(2,1)}, u32[]{:S(2)}) copy-start(bf16[1024,4,128]{0,2,1:T(8,128)(2,1)} %copy-done.4) | copy-start | bytes 3145732
  139.2 2.2 %copy-start.6 = (f32[4,128,1024]{2,1,0:T(8,128)S(1)}, f32[4,128,1024]{2,1,0:T(8,128)}, u32[]{:S(2)}) copy-start(f32[4,128,1024]{2,1,0:T(8,128)} %fusion.36) | copy-start | bytes 6291460
Sparse Core Ops, SparseCore 0:
  13.6 31.8 all-gather.8
  47.3 52.1 all-gather.6
  108.8 29.1 all-gather.10
  140.1 49.5 reduce-scatter.1
where the time goes:
time: 199 us; the launch traced here: 198 us
  waiting for transfers between devices  77.3 us (39%)
  matrix products  60.2 us (30%)
  local copies, waits for them, and re-layouts  18.9 us (9%)
  blocking collectives  18.4 us (9%)
  between operations  14.6 us (7%)
  other arithmetic  8.4 us (4%)
    all_gather x1, waiting for transfers between devices, on_device(): full_grad = lax.all_gather(out_grad, 'head', axis=1, tiled=True)  44 us
    reduce_scatter x1, waiting for transfers between devices, on_device(): lax.psum_scatter(lax.dot_general(full_grad, attended_flat, (((0,), (0,)),...  32.6 us
    unnamed x36, local copies, waits for them, and re-layouts  18.4 us
    unnamed x1, blocking collectives  18.4 us
    dot_general x1, matrix products, on_device(): jnp.einsum('thd,shd->hts', query_rows, key_rows, preferred_element_type=j...  7.6 us
    dot_general x1, matrix products, on_device(): jnp.einsum('thd,shd->hts', mixed_grad, value_rows, preferred_element_type...  7.55 us
    dot_general x1, matrix products, on_device(): lax.dot_general(full_grad, attended_flat, (((0,), (0,)), ((), ())), prefe...  6.78 us
    dot_general x1, matrix products, on_device(): jnp.einsum('hts,the->she', weights, mixed_grad, preferred_element_type=jn...  6.38 us
  transfers between devices with their start and end apart: 4, of which 2 were waited for; matrix products, arithmetic and copies ran while one was open for 33% of the time, Pallas kernels for 0%

commit v1 on v0

v1 whole, which is shorter than its diff:
```python
import functools

import jax
import jax.numpy as jnp
from jax import lax
from jax.experimental import pallas as pl
from jax.experimental.pallas import tpu as pltpu
from jax.sharding import PartitionSpec as P

HIGH = lax.Precision.HIGHEST
F32 = jnp.float32
BF16 = jnp.bfloat16
VMEM = pl.BlockSpec(memory_space=pltpu.VMEM)
SMEM = pl.BlockSpec(memory_space=pltpu.SMEM)
NN = (((1,), (0,)), ((), ()))
NT = (((1,), (1,)), ((), ()))
TN = (((0,), (0,)), ((), ()))


def mm(left, right, dims):
    return lax.dot_general(left, right, dims, preferred_element_type=F32)


def call(body, outs, specs, flops, *args):
    shapes = [jax.ShapeDtypeStruct(shape, dtype) for shape, dtype in outs]
    moved = sum(a.size * a.dtype.itemsize for a in list(args) + shapes)
    return pl.pallas_call(
        body,
        out_shape=shapes,
        in_specs=specs,
        out_specs=[VMEM] * len(shapes),
        compiler_params=pltpu.CompilerParams(vmem_limit_bytes=32 * 1024 * 1024),
        cost_estimate=pl.CostEstimate(flops=flops, bytes_accessed=moved, transcendentals=0),
    )(*args)


def state_body(keys, values, log_decay, run_row, run_col, states, update):
    chunks, heads, size = run_row.shape
    width = states.shape[-1]
    source = lax.broadcasted_iota(jnp.int32, (size, size), 0)
    target = lax.broadcasted_iota(jnp.int32, (size, size), 1)
    upper = (source <= target).astype(F32)
    lower = (source >= target).astype(F32)
    for j in range(chunks):
        piece = log_decay[:, j * size : (j + 1) * size]
        run_row[j] = lax.dot_general(piece, upper, NN, precision=HIGH, preferred_element_type=F32)
        run_col[j] = lax.dot_general(lower, piece, NT, precision=HIGH, preferred_element_type=F32)
    for h in range(heads):
        cols = slice(h * width, (h + 1) * width)
        state = jnp.zeros((width, width), F32)
        for j in range(chunks):
            rows = slice(j * size, (j + 1) * size)
            run = run_col[j, :, h : h + 1]
            total = run[size - 1 : size, :]
            tail = (keys[rows, cols] * jnp.exp(total - run)).astype(BF16)
            states[h, j] = state
            state = state * jnp.exp(total) + mm(tail, values[rows, cols], TN)
        update[h] = state


def decay_of(run_row, run_col, j, h, causal):
    spread = run_col[j, :, h : h + 1] - run_row[j, h : h + 1, :]
    return jnp.exp(jnp.where(causal, spread, -jnp.inf))


def causal_mask(size):
    return lax.broadcasted_iota(jnp.int32, (size, size), 0) >= lax.broadcasted_iota(
        jnp.int32, (size, size), 1
    )


def local_body(queries, keys, values, run_row, run_col, states, weights, mixed):
    chunks, heads, size = run_row.shape
    width = states.shape[-1]
    causal = causal_mask(size)
    for h in range(heads):
        cols = slice(h * width, (h + 1) * width)
        for j in range(chunks):
            rows = slice(j * size, (j + 1) * size)
            query = queries[rows, cols]
            scores = mm(query, keys[rows, cols], NT)
            weight = (scores * decay_of(run_row, run_col, j, h, causal)).astype(BF16)
            weights[h, j] = weight
            grown = (query * jnp.exp(run_col[j, :, h : h + 1])).astype(BF16)
            mixed[rows, cols] = mm(weight, values[rows, cols], NN) + mm(
                grown, states[h, j].astype(BF16), NN
            )


def norm_body(mixed, queries, run_col, incoming, normed, attended, inverse):
    chunks, size, heads = run_col.shape
    width = incoming.shape[-1]
    for h in range(heads):
        cols = slice(h * width, (h + 1) * width)
        state = incoming[h].astype(BF16)
        before = jnp.zeros((1, 1), F32)
        for j in range(chunks):
            rows = slice(j * size, (j + 1) * size)
            run = run_col[j, :, h : h + 1]
            grown = (queries[rows, cols] * jnp.exp(run + before)).astype(BF16)
            total = mixed[rows, cols] + mm(grown, state, NN)
            scale = lax.rsqrt(jnp.mean(total * total, axis=1, keepdims=True) + 1e-05)
            inverse[j, :, h : h + 1] = scale
            total = total * scale
            normed[rows, cols] = total
            attended[rows, cols] = total.astype(BF16)
            before = before + run[size - 1 : size, :]


def head_grad_body(size, number, *refs):
    starts, weight = refs[0], refs[1]
    pieces, out = refs[2 : 2 + number], refs[2 + number]
    for t in range(out.shape[0] // size):
        rows = slice(t * size, (t + 1) * size)
        total = None
        for i, piece in enumerate(pieces):
            depth = piece.shape[1]
            start = pl.multiple_of(starts[i] * 64, 64)
            term = mm(piece[rows, :], weight[pl.ds(start, depth), :], NN)
            total = term if total is None else total + term
        out[rows, :] = total


def mixed_grad_body(number, *refs):
    starts, weight = refs[0], refs[1]
    pieces = refs[2 : 2 + number]
    partial, normed, inverse, queries, run_col = refs[2 + number : 7 + number]
    mixed_grad, states, update = refs[7 + number :]
    chunks, size, heads = run_col.shape
    width = update.shape[-1]
    for j in range(chunks):
        rows = slice(j * size, (j + 1) * size)
        total = partial[rows, :]
        for i, piece in enumerate(pieces):
            depth = piece.shape[1]
            start = pl.multiple_of(starts[i] * 64, 64)
            total = total + mm(piece[rows, :], weight[pl.ds(start, depth), :], NN)
        for h in range(heads):
            cols = slice(h * width, (h + 1) * width)
            grad = total[:, cols]
            unit = normed[rows, cols]
            mean = jnp.mean(grad * unit, axis=1, keepdims=True)
            grad = ((grad - unit * mean) * inverse[j, :, h : h + 1]).astype(BF16)
            mixed_grad[rows, cols] = grad
            grown = (queries[rows, cols] * jnp.exp(run_col[j, :, h : h + 1])).astype(BF16)
            states[h, j] = mm(grown, grad, TN)
    for h in range(heads):
        state = jnp.zeros((width, width), F32)
        for j in reversed(range(chunks)):
            own = states[h, j]
            states[h, j] = state
            state = own + state * jnp.exp(run_col[j, size - 1 : size, h : h + 1])
        update[h] = state


def back_body(
    queries, keys, values, mixed_grad, weights, run_row, run_col, states, incoming, back_states,
    query_grad, key_grad, value_grad,
):
    chunks, heads, size = run_row.shape
    width = states.shape[-1]
    causal = causal_mask(size)
    for h in range(heads):
        cols = slice(h * width, (h + 1) * width)
        before = jnp.zeros((1, 1), F32)
        for j in range(chunks):
            rows = slice(j * size, (j + 1) * size)
            run = run_col[j, :, h : h + 1]
            total = run[size - 1 : size, :]
            grad = mixed_grad[rows, cols]
            key, value = keys[rows, cols], values[rows, cols]
            pair = mm(grad, value, NT)
            masked = (pair * decay_of(run_row, run_col, j, h, causal)).astype(BF16)
            state = (states[h, j] + incoming[h] * jnp.exp(before)).astype(BF16)
            back_state = back_states[h, j].astype(BF16)
            grown = (grad * jnp.exp(run)).astype(BF16)
            query_grad[rows, cols] = (mm(masked, key, NN) + mm(grown, state, NT)).astype(BF16)
            tail = jnp.exp(total - run)
            key_grad[rows, cols] = mm(masked, queries[rows, cols], TN) + mm(
                (value * tail).astype(BF16), back_state, NT
            )
            value_grad[rows, cols] = mm(weights[h, j], grad, TN) + mm(
                (key * tail).astype(BF16), back_state, NN
            )
            before = before + total


def final_body(keys, values, run_col, outgoing, key_part, value_part, key_grad, value_grad):
    chunks, size, heads = run_col.shape
    width = outgoing.shape[-1]
    for h in range(heads):
        cols = slice(h * width, (h + 1) * width)
        state = outgoing[h].astype(BF16)
        after = jnp.zeros((1, 1), F32)
        for j in reversed(range(chunks)):
            rows = slice(j * size, (j + 1) * size)
            run = run_col[j, :, h : h + 1]
            after = after + run[size - 1 : size, :]
            tail = jnp.exp(after - run)
            key_grad[rows, cols] = (
                key_part[rows, cols] + mm((values[rows, cols] * tail).astype(BF16), state, NT)
            ).astype(BF16)
            value_grad[rows, cols] = (
                value_part[rows, cols] + mm((keys[rows, cols] * tail).astype(BF16), state, NN)
            ).astype(BF16)


def weight_grad_body(number, *refs):
    core = refs[0][0]
    pieces, attended, out = refs[1 : 1 + number], refs[1 + number], refs[2 + number]
    for i, (side, slot, piece, span) in enumerate(pieces_of(number, refs)):
        out[lax.rem(side + core, 2), slot] = mm(piece[:, span], attended[...], TN).astype(BF16)


def pieces_of(number, refs):
    raise NotImplementedError


class Chain:
    def __init__(self, totals, size):
        index = lax.axis_index("seq")
        self.chips = size // 2
        self.chip, self.core = index // 2, index % 2
        self.totals = totals
        heads = totals.shape[0]
        self.other = self.swap(totals)
        first = jnp.where(self.core == 0, totals, self.other)
        second = jnp.where(self.core == 0, self.other, totals)
        chip_total = first + second
        back = [self.shift(chip_total, k) for k in range(1, self.chips)]
        zero = jnp.zeros((heads,), F32)
        self.incoming, self.outgoing = [None] * self.chips, [None] * self.chips
        span = zero
        for k in range(1, self.chips):
            self.incoming[k] = jnp.where(k <= self.chip, jnp.exp(span), 0.0)
            span = span + back[k - 1]
        span = zero
        for k in reversed(range(1, self.chips)):
            self.outgoing[k] = jnp.where(k > self.chip, jnp.exp(span), 0.0)
            span = span + back[k - 1]

    def swap(self, value):
        return lax.ppermute(value, "seq", [(i, i ^ 1) for i in range(2 * self.chips)])

    def shift(self, value, k):
        pairs = [
            (i, (i // 2 + k) % self.chips * 2 + i % 2) for i in range(2 * self.chips)
        ]
        return lax.ppermute(value, "seq", pairs)

    def run(self, update, forward):
        low = update.astype(BF16)
        other = self.swap(low).astype(F32)
        near, far = jnp.exp(self.totals), jnp.exp(self.other)
        wide = lambda factor: factor[:, None, None]
        late = self.core == (1 if forward else 0)
        chip = jnp.where(late, update + wide(near) * other, other + wide(far) * update)
        chip = chip.astype(BF16)
        heads, rows, cols = chip.shape
        halves = chip.reshape(2, heads * rows // 2, cols)
        half = lax.dynamic_index_in_dim(halves, self.core, 0, keepdims=False)
        factors = self.incoming if forward else self.outgoing
        total = jnp.zeros(half.shape, F32)
        for k in range(1, self.chips):
            weight = jnp.repeat(factors[k], rows).reshape(2, heads * rows // 2)
            weight = lax.dynamic_index_in_dim(weight, self.core, 0, keepdims=False)
            total = total + weight[:, None] * self.shift(half, k).astype(F32)
        total = total.astype(BF16)
        theirs = self.swap(total)
        low_half = jnp.where(self.core == 0, total, theirs)
        high_half = jnp.where(self.core == 0, theirs, total)
        entering = jnp.concatenate([low_half, high_half]).reshape(chip.shape).astype(F32)
        return jnp.where(late, other + wide(far) * entering, entering)


def gather_pieces(out_grad, count):
    half = out_grad.shape[1] // 2
    move = lambda a, k: lax.ppermute(a, "head", [(i, i ^ k) for i in range(count)])
    low, high = out_grad[:, :half], out_grad[:, half:]
    x_low, y_high = move(low, 1), move(high, 2)
    diagonal_high, diagonal_low = move(y_high, 1), move(x_low, 2)
    x_high, y_low = move(high, 1), move(low, 2)
    early = [(0, 0, low), (0, 1, high), (1, 0, x_low), (2, 1, y_high)]
    late = [(3, 0, diagonal_low), (3, 1, diagonal_high), (1, 1, x_high), (2, 0, y_low)]
    return early, late


def reduce_rows(attended, group, chips, count):
    seq, head = lax.axis_index("seq"), lax.axis_index("head")
    chip, core = seq // 2, seq % 2
    sides = [[p for p in group if p[1] == side] for side in range(2)]
    product = lambda a: mm(a, attended, TN).astype(BF16)
    parts = [jnp.stack([product(p[2]) for p in side]) for side in sides]
    mine = jnp.where(core == 0, parts[0], parts[1])
    theirs = jnp.where(core == 0, parts[1], parts[0])
    pairs = [(i, i ^ 1) for i in range(2 * chips)]
    held = (mine.astype(F32) + lax.ppermute(theirs, "seq", pairs).astype(F32)).astype(BF16)

    def target(slot, side, where):
        return where ^ sides[side][slot][0]

    total = jnp.zeros(held.shape[1:], F32)
    for slot in range(2):
        goal = jnp.where(core == 0, target(slot, 0, head), target(slot, 1, head))
        total = total + jnp.where(chip == goal, held[slot].astype(F32), 0.0)
    for step in range(1, 4):
        moves, picks = [], []
        for s in range(2 * chips):
            for y in range(count):
                first, second = target(0, s % 2, y), target(1, s % 2, y)
                apart = first ^ second
                z = s // 2
                if z == first or z == second:
                    if step == apart:
                        goal, slot = (second, 1) if z == first else (first, 0)
                    else:
                        continue
                elif z ^ first == step:
                    goal, slot = first, 0
                elif z ^ second == step:
                    goal, slot = second, 1
                else:
                    continue
                moves.append((s * count + y, (goal * 2 + s % 2) * count + y))
                picks.append((s * count + y, slot))
        first = jnp.where(core == 0, target(0, 0, head), target(0, 1, head))
        sent = jnp.where((chip ^ first) == step, held[0], held[1])
        total = total + lax.ppermute(sent, ("seq", "head"), moves).astype(F32)
    return total


def on_device(seq_size, head_size, queries, keys, values, log_decay, out_weight, out_grad):
    length, columns = queries.shape
    heads = log_decay.shape[0]
    width = columns // heads
    size = 256 if length % 256 == 0 else length
    chunks = length // size
    head = lax.axis_index("head")
    chips = seq_size // 2
    near = head_size == 4 and chips == 4
    if near:
        early, late = gather_pieces(out_grad, head_size)
    else:
        whole = lax.all_gather(out_grad, "head", axis=1, tiled=True)
        early, late = [], []
    chain = Chain(jnp.sum(log_decay, axis=1), seq_size)
    square = heads * chunks * size * width * width * 2
    pairs = heads * chunks * size * size * width * 2
    run_row, run_col, states, update = call(
        state_body,
        [((chunks, heads, size), F32), ((chunks, size, heads), F32),
         ((heads, chunks, width, width), F32), ((heads, width, width), F32)],
        [VMEM] * 3, square, keys, values, log_decay,
    )
    incoming = chain.run(update, True)
    weights, mixed = call(
        local_body,
        [((heads, chunks, size, size), BF16), ((length, columns), F32)],
        [VMEM] * 6, 2 * pairs + square, queries, keys, values, run_row, run_col, states,
    )
    normed, attended, inverse = call(
        norm_body,
        [((length, columns), F32), ((length, columns), BF16), ((chunks, size, heads), F32)],
        [VMEM] * 4, square, mixed, queries, run_col, incoming,
    )

    def starts_of(group):
        block = out_grad.shape[1]
        return jnp.stack(
            [((head ^ k) * block + side * (block // 2)) // 64 for k, side, _ in group]
        ).astype(jnp.int32)

    if near:
        first = early + late[:2]
        partial, = call(
            functools.partial(head_grad_body, size, len(first)),
            [((length, columns), F32)],
            [SMEM] + [VMEM] * (1 + len(first)),
            2 * length * columns * out_weight.shape[0] * 3 // 4,
            starts_of(first), out_weight, *[p[2] for p in first],
        )
        last = late[2:]
    else:
        last = []
        partial = jnp.dot(whole, out_weight, preferred_element_type=F32)
    mixed_grad, back_states, back_update = call(
        functools.partial(mixed_grad_body, len(last)),
        [((length, columns), BF16), ((heads, chunks, width, width), F32),
         ((heads, width, width), F32)],
        [SMEM] + [VMEM] * (6 + len(last)),
        square + 2 * length * columns * out_weight.shape[0] // 4,
        starts_of(last) if last else jnp.zeros((1,), jnp.int32), out_weight,
        *[p[2] for p in last], partial, normed, inverse, queries, run_col,
    )
    outgoing = chain.run(back_update, False)
    query_grad, key_part, value_part = call(
        back_body,
        [((length, columns), BF16), ((length, columns), F32), ((length, columns), F32)],
        [VMEM] * 10, 4 * pairs + 3 * square,
        queries, keys, values, mixed_grad, weights, run_row, run_col, states, incoming,
        back_states,
    )
    key_grad, value_grad = call(
        final_body,
        [((length, columns), BF16)] * 2,
        [VMEM] * 6, 2 * square, keys, values, run_col, outgoing, key_part, value_part,
    )
    if near:
        weight_grad = reduce_rows(attended, early, chips, head_size) + reduce_rows(
            attended, late, chips, head_size
        )
    else:
        weight_grad = lax.psum_scatter(
            mm(whole, attended, TN), "seq", scatter_dimension=0, tiled=True
        )
    return attended, query_grad, key_grad, value_grad, weight_grad.astype(BF16)


def solution(mesh):
    block = P("seq", "head")
    return jax.shard_map(
        functools.partial(on_device, mesh.shape["seq"], mesh.shape["head"]),
        mesh=mesh,
        in_specs=(block, block, block, P("head", "seq"), P(None, "head"), block),
        out_specs=(block,) * 5,
        check_vma=False,
    )
```

time: 199 us -> 118 us (0.59)
  the two profiles are of different devices: /device:TPU:0 before, /device:TPU:16 now
where the time goes in v1:
time: 118 us
  starting transfers between devices  37.1 us (31%)
  waiting for transfers between devices  30 us (25%)
  Pallas kernels  24.9 us (21%)
  local copies, waits for them, and re-layouts  12.4 us (11%)
  matrix products  7.43 us (6%)
  other arithmetic  4.73 us (4%)
    pallas_call x7, Pallas kernels, call(): pl.pallas_call(body, out_shape=shapes, in_specs=specs, out_specs=[VMEM] *...  24.9 us
    ppermute x6, waiting for transfers between devices, reduce_rows(): total = total + lax.ppermute(sent, ('seq', 'head'), moves).astype(F32)  15.6 us
    ppermute x9, starting transfers between devices, shift(): return lax.ppermute(value, 'seq', pairs)  15.5 us
    ppermute x6, starting transfers between devices, reduce_rows(): total = total + lax.ppermute(sent, ('seq', 'head'), moves).astype(F32)  14.8 us
    unnamed x45, local copies, waits for them, and re-layouts  9.51 us
    ppermute x6, waiting for transfers between devices, gather_pieces(): lax.ppermute(a, 'head', [(i, i ^ k) for i in range(count)])  8.6 us
    dot_general x8, matrix products, mm(): return lax.dot_general(left, right, dims, preferred_element_type=F32)  7.43 us
    ppermute x6, starting transfers between devices, gather_pieces(): lax.ppermute(a, 'head', [(i, i ^ k) for i in range(count)])  5.3 us
  transfers between devices with their start and end apart: 28, of which 8 were waited for; matrix products, arithmetic and copies ran while one was open for 11% of the time, Pallas kernels for 21%

profile of v1, /device:TPU:16, one launch (start us, length us, event | category | flops | bytes accessed | tf_op | source)
XLA Modules:
  0.0 117.6 jit_solution(8633562005956045553)
XLA Ops:
  0.7 2.4 %fusion.23 = (bf16[1024,256]{1,0:T(8,128)(2,1)}, bf16[1024,256]{1,0:T(8,128)(2,1)}) fusion(bf16[1024,512]{1,0:T(8,128)(2,1)} %param.11), kind=kLoop, calls=%fused_computation.86 | loop fusion | bytes 2097152 | tf_op jit(solution)/shard_map/slice | solution.py:279
  3.1 1.5 %collective-permute-start.10 = (bf16[1024,256]{1,0:T(8,128)(2,1)}, bf16[1024,256]{1,0:T(8,128)(2,1)}, u32[]{:S(2)}, u32[]{:S(2)}) collective-permute-start(bf16[1024,256]{1,0:T(8,128)(2,1)} %get-tuple-element.44.refs_2_), channel_id=1, source_target_pairs={{0,1},{1,0},{2,3},{3,2},{4,5},{5,4},{6,7},{7,6},{8,9},{9,8},{10,11... | collective-permute-start | bytes 1572872 | tf_op jit(solution)/shard_map/ppermute | solution.py:278
  4.6 1.5 %collective-permute-start.9 = (bf16[1024,256]{1,0:T(8,128)(2,1)}, bf16[1024,256]{1,0:T(8,128)(2,1)}, u32[]{:S(2)}, u32[]{:S(2)}) collective-permute-start(bf16[1024,256]{1,0:T(8,128)(2,1)} %get-tuple-element.44.refs_2_), channel_id=1, source_target_pairs={{0,2},{1,3},{2,0},{3,1},{4,6},{5,7},{6,4},{7,5},{8,10},{9,11},{10,... | collective-permute-start | bytes 1572872 | tf_op jit(solution)/shard_map/ppermute | solution.py:278
  6.3 2.3 %shard_map.101 = (f32[4,4,256]{2,1,0:T(4,128)S(1)}, f32[4,256,4]{2,1,0:T(8,128)S(1)}, f32[4,4,128,128]{3,2,1,0:T(8,128)S(1)}, f32[4,128,128]{2,1,0:T(8,128)S(1)}) custom-call(bf16[1024,512]{1,0:T(8,128)(2,1)S(1)} %copy-done, bf16[1024,512]{1,0:T(8,128)(2,1)S(1)} %copy-done.1, f32[4,1024]{1,0:T(4,128)S(1)} %copy-done.15), custom_call_target="tpu_custom_call" | custom-call | flops 134217728 | bytes 3457024 | tf_op jit(solution)/shard_map/pallas_call | solution.py:27
  12.6 1.2 %copy-done.8 = f32[4,4,128,128]{3,2,1,0:T(8,128)S(1)} copy-done((f32[4,4,128,128]{3,2,1,0:T(8,128)S(1)}, f32[4,4,128,128]{3,2,1,0:T(8,128)}, u32[]{:S(2)}) %copy-start.8) | copy-done | bytes 1048600
  13.9 2.1 %shard_map.102 = (bf16[4,4,256,256]{3,2,1,0:T(8,128)(2,1)S(1)}, f32[1024,512]{1,0:T(8,128)S(1)}) custom-call(bf16[1024,512]{1,0:T(8,128)(2,1)S(1)} %copy-done.2, bf16[1024,512]{1,0:T(8,128)(2,1)S(1)} %copy-done, bf16[1024,512]{1,0:T(8,128)(2,1)S(1)} %copy-done.1, f32[4,4,256]{2,1,0:T(4,128)S(1)} %get-tuple-element.22.run_row, f32[4,256,4]{2,1,0:T(8,128)S(1)} %copy-done.4, ...), custom_call_target="tpu_custom_call" | custom-call | flops 671088640 | bytes 8421376 | tf_op jit(solution)/shard_map/pallas_call | solution.py:27
  15.9 1.4 %copy-done.10 = f32[1024,512]{1,0:T(8,128)} copy-done((f32[1024,512]{1,0:T(8,128)}, f32[1024,512]{1,0:T(8,128)S(1)}, u32[]{:S(2)}) %copy-start.10) | copy-done | bytes 2097176
  17.3 1.3 %copy-done.12 = bf16[4,4,256,256]{3,2,1,0:T(8,128)(2,1)} copy-done((bf16[4,4,256,256]{3,2,1,0:T(8,128)(2,1)}, bf16[4,4,256,256]{3,2,1,0:T(8,128)(2,1)S(1)}, u32[]{:S(2)}) %copy-start.12) | copy-done | bytes 2097176
  19.2 3.5 %collective-permute-start.5 = (f32[4]{0:T(128)S(1)}, f32[4]{0:T(128)S(1)}, u32[]{:S(2)}, u32[]{:S(2)}) collective-permute-start(f32[4]{0:T(128)S(1)} %get-tuple-element.60), channel_id=1, source_target_pairs={{0,16},{4,20},{8,24},{12,28},{16,0},{20,4},{24,8},{28,12},{1,17},{... | collective-permute-start | bytes 56 | tf_op jit(solution)/shard_map/ppermute | solution.py:249
  22.7 3.0 %collective-permute-start.3 = (f32[4]{0:T(128)S(1)}, f32[4]{0:T(128)S(1)}, u32[]{:S(2)}, u32[]{:S(2)}) collective-permute-start(f32[4]{0:T(128)S(1)} %get-tuple-element.60), channel_id=1, source_target_pairs={{0,8},{4,12},{8,16},{12,20},{16,24},{20,28},{24,0},{28,4},{1,9},{5... | collective-permute-start | bytes 56 | tf_op jit(solution)/shard_map/ppermute | solution.py:249
  25.7 1.3 %collective-permute-done.3 = f32[4]{0:T(128)S(1)} collective-permute-done((f32[4]{0:T(128)S(1)}, f32[4]{0:T(128)S(1)}, u32[]{:S(2)}, u32[]{:S(2)}) %collective-permute-start.3) | collective-permute-done | bytes 48 | tf_op jit(solution)/shard_map/ppermute | solution.py:249
  28.8 4.6 %collective-permute-start.4 = (bf16[256,128]{1,0:T(8,128)(2,1)S(1)}, bf16[256,128]{1,0:T(8,128)(2,1)S(1)}, u32[]{:S(2)}, u32[]{:S(2)}) collective-permute-start(bf16[256,128]{1,0:T(8,128)(2,1)S(1)} %dynamic-slice_bitcast_fusion.1), channel_id=1, source_target_pairs={{0,16},{4,20},{8,24},{12,28},{16,0},{20,4},{24,8},{28,12},{1,17},{... | collective-permute-start | bytes 196616 | tf_op jit(solution)/shard_map/ppermute | solution.py:249
  34.2 2.2 %collective-permute-done.4 = bf16[256,128]{1,0:T(8,128)(2,1)S(1)} collective-permute-done((bf16[256,128]{1,0:T(8,128)(2,1)S(1)}, bf16[256,128]{1,0:T(8,128)(2,1)S(1)}, u32[]{:S(2)}, u32[]{:S(2)}) %collective-permute-start.4) | collective-permute-done | bytes 65568 | tf_op jit(solution)/shard_map/ppermute | solution.py:249
  37.9 1.2 %collective-permute-done.7 = bf16[256,128]{1,0:T(8,128)(2,1)S(1)} collective-permute-done((bf16[256,128]{1,0:T(8,128)(2,1)S(1)}, bf16[256,128]{1,0:T(8,128)(2,1)S(1)}, u32[]{:S(2)}, u32[]{:S(2)}) %collective-permute-start.7) | collective-permute-done | bytes 65568 | tf_op jit(solution)/shard_map/ppermute | solution.py:243
  40.2 1.6 %copy-done.11 = f32[1024,512]{1,0:T(8,128)S(1)} copy-done((f32[1024,512]{1,0:T(8,128)S(1)}, f32[1024,512]{1,0:T(8,128)}, u32[]{:S(2)}) %copy-start.11) | copy-done | bytes 2097176
  41.8 4.3 %shard_map.103 = (f32[1024,512]{1,0:T(8,128)S(1)}, bf16[1024,512]{1,0:T(8,128)(2,1)}, f32[4,256,4]{2,1,0:T(8,128)S(1)}) custom-call(f32[1024,512]{1,0:T(8,128)S(1)} %copy-done.11, bf16[1024,512]{1,0:T(8,128)(2,1)S(1)} %copy-done.2, f32[4,256,4]{2,1,0:T(8,128)S(1)} %copy-done.5, f32[4,128,128]{2,1,0:T(8,128)S(1)} %convert_select_fusion.1.incoming), custom_call_target="tpu_custom_call" | custom-call | flops 134217728 | bytes 6586368 | tf_op jit(solution)/shard_map/pallas_call | solution.py:27
  46.1 1.8 %fusion.2 = bf16[1,256,512]{1,2,0:T(8,128)(2,1)S(1)} fusion(bf16[1024,512]{1,0:T(8,128)(2,1)} %get-tuple-element.39, bf16[1024,512]{1,0:T(8,128)(2,1)S(1)} %copy-done.16), kind=kOutput, calls=%fused_computation.10 | convolution fusion | flops 268566528 | bytes 1835008 | tf_op jit(solution)/shard_map/dot_general | solution.py:21
  50.2 1.5 %fusion.1 = bf16[1,256,512]{1,2,0:T(8,128)(2,1)S(1)} fusion(bf16[1024,512]{1,0:T(8,128)(2,1)S(1)} %copy-done.17, bf16[1024,256]{1,0:T(8,128)(2,1)} %collective-permute-done.10.refs_4_), kind=kOutput, calls=%fused_computation.9 | convolution fusion | flops 268566528 | bytes 1835008 | tf_op jit(solution)/shard_map/dot_general | solution.py:21
  51.9 1.7 %fusion.5 = bf16[1,256,512]{1,2,0:T(8,128)(2,1)S(1)} fusion(bf16[1024,512]{1,0:T(8,128)(2,1)S(1)} %copy-done.17, bf16[1024,256]{1,0:T(8,128)(2,1)} %collective-permute-done.9.refs_3_), kind=kOutput, calls=%fused_computation.13 | convolution fusion | flops 268566528 | bytes 1835008 | tf_op jit(solution)/shard_map/dot_general | solution.py:21
  54.1 8.6 %collective-permute-done.12.refs_6_ = bf16[1024,256]{1,0:T(8,128)(2,1)S(1)} collective-permute-done((bf16[1024,256]{1,0:T(8,128)(2,1)}, bf16[1024,256]{1,0:T(8,128)(2,1)S(1)}, u32[]{:S(2)}, u32[]{:S(2)}) %collective-permute-start.12) | collective-permute-done | bytes 524320 | tf_op jit(solution)/shard_map/ppermute | solution.py:278
  62.7 3.0 %shard_map.104.refs_4_ = f32[1024,512]{1,0:T(8,128)S(1)} custom-call(s32[6]{0:T(128)S(1)} %stack.75.refs_0_, bf16[2048,512]{1,0:T(8,128)(2,1)S(1)} %copy-done.6, bf16[1024,256]{1,0:T(8,128)(2,1)} %get-tuple-element.44.refs_2_, bf16[1024,256]{1,0:T(8,128)(2,1)S(1)} %copy-done.14, bf16[1024,256]{1,0:T(8,128)(2,1)} %collective-permute-done.10.refs_4_, ...), custom_call_target="tpu_custom_call" | custom-call | flops 1610612736 | bytes 7340056 | tf_op jit(solution)/shard_map/pallas_call | solution.py:27
  65.7 5.1 %shard_map.105 = (bf16[1024,512]{1,0:T(8,128)(2,1)S(1)}, f32[4,4,128,128]{3,2,1,0:T(8,128)S(1)}, f32[4,128,128]{2,1,0:T(8,128)S(1)}) custom-call(s32[2]{0:T(128)S(1)} %pad_add_fusion.refs_0_, bf16[2048,512]{1,0:T(8,128)(2,1)S(1)} %copy-done.6, bf16[1024,256]{1,0:T(8,128)(2,1)S(1)} %collective-permute-done.8.refs_2_, ...), custom_call_target="tpu_custom_call" | custom-call | flops 671088640 | bytes 10780680 | tf_op jit(solution)/shard_map/pallas_call | solution.py:27
  73.0 3.9 %collective-permute-start.17 = (bf16[256,128]{1,0:T(8,128)(2,1)S(1)}, bf16[256,128]{1,0:T(8,128)(2,1)S(1)}, u32[]{:S(2)}, u32[]{:S(2)}) collective-permute-start(bf16[256,128]{1,0:T(8,128)(2,1)S(1)} %dynamic-slice_bitcast_fusion), channel_id=1, source_target_pairs={{0,16},{4,20},{8,24},{12,28},{16,0},{20,4},{24,8},{28,12},{1,17},{... | collective-permute-start | bytes 196616 | tf_op jit(solution)/shard_map/ppermute | solution.py:249
  77.6 6.9 %collective-permute-start.22 = (bf16[256,512]{0,1:T(8,128)(2,1)S(1)}, bf16[256,512]{0,1:T(8,128)(2,1)S(1)}, u32[]{:S(2)}, u32[]{:S(2)}) collective-permute-start(bf16[256,512]{0,1:T(8,128)(2,1)S(1)} %get-tuple-element.47), channel_id=1, source_target_pairs={{2,18},{3,19},{4,20},{6,22},{10,26},{11,27},{13,29},{15,31},{16,0}... | collective-permute-start | bytes 786440 | tf_op jit(solution)/shard_map/ppermute | solution.py:328
  84.5 1.3 %collective-permute-start.23 = (bf16[256,512]{0,1:T(8,128)(2,1)S(1)}, bf16[256,512]{0,1:T(8,128)(2,1)S(1)}, u32[]{:S(2)}, u32[]{:S(2)}) collective-permute-start(bf16[256,512]{0,1:T(8,128)(2,1)S(1)} %get-tuple-element.48), channel_id=1, source_target_pairs={{2,26},{3,27},{5,29},{7,31},{10,18},{11,19},{12,20},{14,22},{16,8}... | collective-permute-start | bytes 786440 | tf_op jit(solution)/shard_map/ppermute | solution.py:328
  86.1 5.9 %shard_map.106 = (bf16[1024,512]{1,0:T(8,128)(2,1)}, f32[1024,512]{1,0:T(8,128)S(1)}, f32[1024,512]{1,0:T(8,128)S(1)}) custom-call(bf16[1024,512]{1,0:T(8,128)(2,1)S(1)} %copy-done.2, bf16[1024,512]{1,0:T(8,128)(2,1)S(1)} %copy-done, bf16[1024,512]{1,0:T(8,128)(2,1)S(1)} %copy-done.1, bf16[1024,512]{1,0:T(8,128)(2,1)S(1)} %get-tuple-element.30.mixed_grad, ...), custom_call_target="tpu_custom_call" | custom-call | flops 1476395008 | bytes 13926400 | tf_op jit(solution)/shard_map/pallas_call | solution.py:27
  92.3 3.4 %collective-permute-start.25 = (bf16[256,512]{0,1:T(8,128)(2,1)S(1)}, bf16[256,512]{0,1:T(8,128)(2,1)S(1)}, u32[]{:S(2)}, u32[]{:S(2)}) collective-permute-start(bf16[256,512]{0,1:T(8,128)(2,1)S(1)} %get-tuple-element.49), channel_id=1, source_target_pairs={{2,10},{3,11},{4,12},{6,14},{10,2},{11,3},{13,5},{15,7},{16,24},{1... | collective-permute-start | bytes 786440 | tf_op jit(solution)/shard_map/ppermute | solution.py:328
  95.7 1.3 %collective-permute-start.26 = (bf16[256,512]{0,1:T(8,128)(2,1)S(1)}, bf16[256,512]{0,1:T(8,128)(2,1)S(1)}, u32[]{:S(2)}, u32[]{:S(2)}) collective-permute-start(bf16[256,512]{0,1:T(8,128)(2,1)S(1)} %get-tuple-element.50), channel_id=1, source_target_pairs={{0,16},{1,17},{5,21},{7,23},{8,24},{9,25},{12,28},{14,30},{18,2},{... | collective-permute-start | bytes 786440 | tf_op jit(solution)/shard_map/ppermute | solution.py:328
  97.0 1.3 %collective-permute-start.27 = (bf16[256,512]{0,1:T(8,128)(2,1)S(1)}, bf16[256,512]{0,1:T(8,128)(2,1)S(1)}, u32[]{:S(2)}, u32[]{:S(2)}) collective-permute-start(bf16[256,512]{0,1:T(8,128)(2,1)S(1)} %get-tuple-element.51), channel_id=1, source_target_pairs={{0,24},{1,25},{4,28},{6,30},{8,16},{9,17},{13,21},{15,23},{18,10},... | collective-permute-start | bytes 786440 | tf_op jit(solution)/shard_map/ppermute | solution.py:328
  98.4 2.3 %shard_map.107 = (bf16[1024,512]{1,0:T(8,128)(2,1)}, bf16[1024,512]{1,0:T(8,128)(2,1)}) custom-call(bf16[1024,512]{1,0:T(8,128)(2,1)S(1)} %copy-done, bf16[1024,512]{1,0:T(8,128)(2,1)S(1)} %copy-done.1, f32[4,256,4]{2,1,0:T(8,128)S(1)} %copy-done.5, f32[4,128,128]{2,1,0:T(8,128)S(1)} %convert_select_fusion.outgoing, ...), custom_call_target="tpu_custom_call" | custom-call | flops 268435456 | bytes 8667136 | tf_op jit(solution)/shard_map/pallas_call | solution.py:27
  100.8 12.4 %collective-permute-done.25 = bf16[256,512]{0,1:T(8,128)(2,1)S(1)} collective-permute-done((bf16[256,512]{0,1:T(8,128)(2,1)S(1)}, bf16[256,512]{0,1:T(8,128)(2,1)S(1)}, u32[]{:S(2)}, u32[]{:S(2)}) %collective-permute-start.25) | collective-permute-done | bytes 262176 | tf_op jit(solution)/shard_map/ppermute | solution.py:328
  113.1 3.2 %collective-permute-done.27 = bf16[256,512]{0,1:T(8,128)(2,1)S(1)} collective-permute-done((bf16[256,512]{0,1:T(8,128)(2,1)S(1)}, bf16[256,512]{0,1:T(8,128)(2,1)S(1)}, u32[]{:S(2)}, u32[]{:S(2)}) %collective-permute-start.27) | collective-permute-done | bytes 262176 | tf_op jit(solution)/shard_map/ppermute | solution.py:328
  (117 shorter events, 17.7 us)
Async XLA Ops:
  0.7 10.9 %copy-start.2 = (bf16[1024,512]{1,0:T(8,128)(2,1)S(1)}, bf16[1024,512]{1,0:T(8,128)(2,1)}, u32[]{:S(2)}) copy-start(bf16[1024,512]{1,0:T(8,128)(2,1)} %queries.5) | copy-start | bytes 3145732
  3.1 45.4 %collective-permute-start.10 = (bf16[1024,256]{1,0:T(8,128)(2,1)}, bf16[1024,256]{1,0:T(8,128)(2,1)}, u32[]{:S(2)}, u32[]{:S(2)}) collective-permute-start(bf16[1024,256]{1,0:T(8,128)(2,1)} %get-tuple-element.44.refs_2_), channel_id=1, source_target_pairs={{0,1},{1,0},{2,3},{3,2},{4,5},{5,4},{6,7},{7,6},{8,9},{9,8},{10,11... | collective-permute-start | bytes 1572872 | tf_op jit(solution)/shard_map/ppermute | solution.py:278
  4.6 47.4 %collective-permute-start.9 = (bf16[1024,256]{1,0:T(8,128)(2,1)}, bf16[1024,256]{1,0:T(8,128)(2,1)}, u32[]{:S(2)}, u32[]{:S(2)}) collective-permute-start(bf16[1024,256]{1,0:T(8,128)(2,1)} %get-tuple-element.44.refs_2_), channel_id=1, source_target_pairs={{0,2},{1,3},{2,0},{3,1},{4,6},{5,7},{6,4},{7,5},{8,10},{9,11},{10,... | collective-permute-start | bytes 1572872 | tf_op jit(solution)/shard_map/ppermute | solution.py:278
  6.2 12.5 %collective-permute-start.1 = (f32[4]{0:T(128)S(1)}, f32[4]{0:T(128)S(1)}, u32[]{:S(2)}, u32[]{:S(2)}) collective-permute-start(f32[4]{0:T(128)S(1)} %reduce_sum.9), channel_id=1, source_target_pairs={{0,4},{4,0},{8,12},{12,8},{16,20},{20,16},{24,28},{28,24},{1,5},{5... | collective-permute-start | bytes 56 | tf_op jit(solution)/shard_map/ppermute | solution.py:243
  11.0 16.6 %collective-permute-start = (bf16[4,128,128]{2,1,0:T(8,128)(2,1)}, bf16[4,128,128]{2,1,0:T(8,128)(2,1)}, u32[]{:S(2)}, u32[]{:S(2)}) collective-permute-start(bf16[4,128,128]{2,1,0:T(8,128)(2,1)} %convert_element_type.157), channel_id=1, source_target_pairs={{0,4},{4,0},{8,12},{12,8},{16,20},{20,16},{24,28},{28,24},{1,5},{5... | collective-permute-start | bytes 393224 | tf_op jit(solution)/shard_map/ppermute | solution.py:243
  18.7 4.0 %collective-permute-start.15 = (f32[4]{0:T(128)S(1)}, f32[4]{0:T(128)S(1)}, u32[]{:S(2)}, u32[]{:S(2)}) collective-permute-start(f32[4]{0:T(128)S(1)} %get-tuple-element.60), channel_id=1, source_target_pairs={{0,24},{4,28},{8,0},{12,4},{16,8},{20,12},{24,16},{28,20},{1,25},{... | collective-permute-start | bytes 56 | tf_op jit(solution)/shard_map/ppermute | solution.py:249
  19.2 6.5 %collective-permute-start.5 = (f32[4]{0:T(128)S(1)}, f32[4]{0:T(128)S(1)}, u32[]{:S(2)}, u32[]{:S(2)}) collective-permute-start(f32[4]{0:T(128)S(1)} %get-tuple-element.60), channel_id=1, source_target_pairs={{0,16},{4,20},{8,24},{12,28},{16,0},{20,4},{24,8},{28,12},{1,17},{... | collective-permute-start | bytes 56 | tf_op jit(solution)/shard_map/ppermute | solution.py:249
  22.7 4.3 %collective-permute-start.3 = (f32[4]{0:T(128)S(1)}, f32[4]{0:T(128)S(1)}, u32[]{:S(2)}, u32[]{:S(2)}) collective-permute-start(f32[4]{0:T(128)S(1)} %get-tuple-element.60), channel_id=1, source_target_pairs={{0,8},{4,12},{8,16},{12,20},{16,24},{20,28},{24,0},{28,4},{1,9},{5... | collective-permute-start | bytes 56 | tf_op jit(solution)/shard_map/ppermute | solution.py:249
  27.6 12.7 %copy-start.5 = (f32[4,256,4]{2,1,0:T(8,128)S(1)}, f32[4,256,4]{2,1,0:T(8,128)}, u32[]{:S(2)}) copy-start(f32[4,256,4]{2,1,0:T(8,128)} %copy-done.3) | copy-start | bytes 49156
  28.8 4.9 %collective-permute-start.6 = (bf16[256,128]{1,0:T(8,128)(2,1)S(1)}, bf16[256,128]{1,0:T(8,128)(2,1)S(1)}, u32[]{:S(2)}, u32[]{:S(2)}) collective-permute-start(bf16[256,128]{1,0:T(8,128)(2,1)S(1)} %dynamic-slice_bitcast_fusion.1), channel_id=1, source_target_pairs={{0,24},{4,28},{8,0},{12,4},{16,8},{20,12},{24,16},{28,20},{1,25},{... | collective-permute-start | bytes 196616 | tf_op jit(solution)/shard_map/ppermute | solution.py:249
  28.8 7.5 %collective-permute-start.4 = (bf16[256,128]{1,0:T(8,128)(2,1)S(1)}, bf16[256,128]{1,0:T(8,128)(2,1)S(1)}, u32[]{:S(2)}, u32[]{:S(2)}) collective-permute-start(bf16[256,128]{1,0:T(8,128)(2,1)S(1)} %dynamic-slice_bitcast_fusion.1), channel_id=1, source_target_pairs={{0,16},{4,20},{8,24},{12,28},{16,0},{20,4},{24,8},{28,12},{1,17},{... | collective-permute-start | bytes 196616 | tf_op jit(solution)/shard_map/ppermute | solution.py:249
  33.4 4.3 %collective-permute-start.2 = (bf16[256,128]{1,0:T(8,128)(2,1)S(1)}, bf16[256,128]{1,0:T(8,128)(2,1)S(1)}, u32[]{:S(2)}, u32[]{:S(2)}) collective-permute-start(bf16[256,128]{1,0:T(8,128)(2,1)S(1)} %dynamic-slice_bitcast_fusion.1), channel_id=1, source_target_pairs={{0,8},{4,12},{8,16},{12,20},{16,24},{20,28},{24,0},{28,4},{1,9},{5... | collective-permute-start | bytes 196616 | tf_op jit(solution)/shard_map/ppermute | solution.py:249
  33.7 15.3 %collective-permute-start.11 = (bf16[1024,256]{1,0:T(8,128)(2,1)}, bf16[1024,256]{1,0:T(8,128)(2,1)S(1)}, u32[]{:S(2)}, u32[]{:S(2)}) collective-permute-start(bf16[1024,256]{1,0:T(8,128)(2,1)} %get-tuple-element.45.refs_3_), channel_id=1, source_target_pairs={{0,2},{1,3},{2,0},{3,1},{4,6},{5,7},{6,4},{7,5},{8,10},{9,11},{10,... | collective-permute-start | bytes 1572872 | tf_op jit(solution)/shard_map/ppermute | solution.py:278
  36.4 17.3 %collective-permute-start.8 = (bf16[1024,256]{1,0:T(8,128)(2,1)}, bf16[1024,256]{1,0:T(8,128)(2,1)S(1)}, u32[]{:S(2)}, u32[]{:S(2)}) collective-permute-start(bf16[1024,256]{1,0:T(8,128)(2,1)} %get-tuple-element.45.refs_3_), channel_id=1, source_target_pairs={{0,1},{1,0},{2,3},{3,2},{4,5},{5,4},{6,7},{7,6},{8,9},{9,8},{10,11... | collective-permute-start | bytes 1572872 | tf_op jit(solution)/shard_map/ppermute | solution.py:278
  37.8 1.3 %collective-permute-start.7 = (bf16[256,128]{1,0:T(8,128)(2,1)S(1)}, bf16[256,128]{1,0:T(8,128)(2,1)S(1)}, u32[]{:S(2)}, u32[]{:S(2)}) collective-permute-start(bf16[256,128]{1,0:T(8,128)(2,1)S(1)} %add_convert_fusion.3), channel_id=1, source_target_pairs={{0,4},{4,0},{8,12},{12,8},{16,20},{20,16},{24,28},{28,24},{1,5},{5... | collective-permute-start | bytes 196616 | tf_op jit(solution)/shard_map/ppermute | solution.py:243
  48.4 14.3 %collective-permute-start.12 = (bf16[1024,256]{1,0:T(8,128)(2,1)}, bf16[1024,256]{1,0:T(8,128)(2,1)S(1)}, u32[]{:S(2)}, u32[]{:S(2)}) collective-permute-start(bf16[1024,256]{1,0:T(8,128)(2,1)} %collective-permute-done.10.refs_4_), channel_id=1, source_target_pairs={{0,2},{1,3},{2,0},{3,1},{4,6},{5,7},{6,4},{7,5},{8,10},{9,11},{10,... | collective-permute-start | bytes 1572872 | tf_op jit(solution)/shard_map/ppermute | solution.py:278
  49.0 13.7 %collective-permute-start.13 = (bf16[1024,256]{1,0:T(8,128)(2,1)S(1)}, bf16[1024,256]{1,0:T(8,128)(2,1)S(1)}, u32[]{:S(2)}, u32[]{:S(2)}) collective-permute-start(bf16[1024,256]{1,0:T(8,128)(2,1)S(1)} %collective-permute-done.11.refs_5_), channel_id=1, source_target_pairs={{0,1},{1,0},{2,3},{3,2},{4,5},{5,4},{6,7},{7,6},{8,9},{9,8},{10,11... | collective-permute-start | bytes 1572872 | tf_op jit(solution)/shard_map/ppermute | solution.py:278
  51.9 20.7 %collective-permute-start.20 = (bf16[2,256,512]{1,2,0:T(8,128)(2,1)S(1)}, bf16[2,256,512]{1,2,0:T(8,128)(2,1)S(1)}, u32[]{:S(2)}, u32[]{:S(2)}) collective-permute-start(bf16[2,256,512]{1,2,0:T(8,128)(2,1)S(1)} %broadcast_select_fusion.1), channel_id=1, source_target_pairs={{0,4},{4,0},{8,12},{12,8},{16,20},{20,16},{24,28},{28,24},{1,5},{5... | collective-permute-start | bytes 1572872 | tf_op jit(solution)/shard_map/ppermute | solution.py:297
  70.8 2.0 %collective-permute-start.14 = (bf16[4,128,128]{2,1,0:T(8,128)(2,1)S(1)}, bf16[4,128,128]{2,1,0:T(8,128)(2,1)S(1)}, u32[]{:S(2)}, u32[]{:S(2)}) collective-permute-start(bf16[4,128,128]{2,1,0:T(8,128)(2,1)S(1)} %convert_element_type.166), channel_id=1, source_target_pairs={{0,4},{4,0},{8,12},{12,8},{16,20},{20,16},{24,28},{28,24},{1,5},{5... | collective-permute-start | bytes 393224 | tf_op jit(solution)/shard_map/ppermute | solution.py:243
  72.0 14.1 %copy-start.9 = (f32[4,4,128,128]{3,2,1,0:T(8,128)S(1)}, f32[4,4,128,128]{3,2,1,0:T(8,128)}, u32[]{:S(2)}) copy-start(f32[4,4,128,128]{3,2,1,0:T(8,128)} %copy-done.7) | copy-start | bytes 3145732
  72.0 14.1 %copy-start.13 = (bf16[4,4,256,256]{3,2,1,0:T(8,128)(2,1)S(1)}, bf16[4,4,256,256]{3,2,1,0:T(8,128)(2,1)}, u32[]{:S(2)}) copy-start(bf16[4,4,256,256]{3,2,1,0:T(8,128)(2,1)} %copy-done.12) | copy-start | bytes 6291460
  72.0 20.0 %collective-permute-start.24 = (bf16[2,256,512]{1,2,0:T(8,128)(2,1)S(1)}, bf16[2,256,512]{1,2,0:T(8,128)(2,1)S(1)}, u32[]{:S(2)}, u32[]{:S(2)}) collective-permute-start(bf16[2,256,512]{1,2,0:T(8,128)(2,1)S(1)} %broadcast_select_fusion), channel_id=1, source_target_pairs={{0,4},{4,0},{8,12},{12,8},{16,20},{20,16},{24,28},{28,24},{1,5},{5... | collective-permute-start | bytes 1572872 | tf_op jit(solution)/shard_map/ppermute | solution.py:297
  72.9 4.7 %collective-permute-start.18 = (bf16[256,128]{1,0:T(8,128)(2,1)S(1)}, bf16[256,128]{1,0:T(8,128)(2,1)S(1)}, u32[]{:S(2)}, u32[]{:S(2)}) collective-permute-start(bf16[256,128]{1,0:T(8,128)(2,1)S(1)} %dynamic-slice_bitcast_fusion), channel_id=1, source_target_pairs={{0,24},{4,28},{8,0},{12,4},{16,8},{20,12},{24,16},{28,20},{1,25},{... | collective-permute-start | bytes 196616 | tf_op jit(solution)/shard_map/ppermute | solution.py:249
  73.0 11.5 %collective-permute-start.17 = (bf16[256,128]{1,0:T(8,128)(2,1)S(1)}, bf16[256,128]{1,0:T(8,128)(2,1)S(1)}, u32[]{:S(2)}, u32[]{:S(2)}) collective-permute-start(bf16[256,128]{1,0:T(8,128)(2,1)S(1)} %dynamic-slice_bitcast_fusion), channel_id=1, source_target_pairs={{0,16},{4,20},{8,24},{12,28},{16,0},{20,4},{24,8},{28,12},{1,17},{... | collective-permute-start | bytes 196616 | tf_op jit(solution)/shard_map/ppermute | solution.py:249
  76.9 8.9 %collective-permute-start.16 = (bf16[256,128]{1,0:T(8,128)(2,1)S(1)}, bf16[256,128]{1,0:T(8,128)(2,1)S(1)}, u32[]{:S(2)}, u32[]{:S(2)}) collective-permute-start(bf16[256,128]{1,0:T(8,128)(2,1)S(1)} %dynamic-slice_bitcast_fusion), channel_id=1, source_target_pairs={{0,8},{4,12},{8,16},{12,20},{16,24},{20,28},{24,0},{28,4},{1,9},{5... | collective-permute-start | bytes 196616 | tf_op jit(solution)/shard_map/ppermute | solution.py:249
  76.9 20.0 %collective-permute-start.21 = (bf16[256,512]{0,1:T(8,128)(2,1)S(1)}, bf16[256,512]{0,1:T(8,128)(2,1)S(1)}, u32[]{:S(2)}, u32[]{:S(2)}) collective-permute-start(bf16[256,512]{0,1:T(8,128)(2,1)S(1)} %get-tuple-element.46), channel_id=1, source_target_pairs={{0,8},{1,9},{5,13},{7,15},{8,0},{9,1},{12,4},{14,6},{18,26},{19,27... | collective-permute-start | bytes 786440 | tf_op jit(solution)/shard_map/ppermute | solution.py:328
  77.6 23.1 %collective-permute-start.22 = (bf16[256,512]{0,1:T(8,128)(2,1)S(1)}, bf16[256,512]{0,1:T(8,128)(2,1)S(1)}, u32[]{:S(2)}, u32[]{:S(2)}) collective-permute-start(bf16[256,512]{0,1:T(8,128)(2,1)S(1)} %get-tuple-element.47), channel_id=1, source_target_pairs={{2,18},{3,19},{4,20},{6,22},{10,26},{11,27},{13,29},{15,31},{16,0}... | collective-permute-start | bytes 786440 | tf_op jit(solution)/shard_map/ppermute | solution.py:328
  84.5 16.3 %collective-permute-start.23 = (bf16[256,512]{0,1:T(8,128)(2,1)S(1)}, bf16[256,512]{0,1:T(8,128)(2,1)S(1)}, u32[]{:S(2)}, u32[]{:S(2)}) collective-permute-start(bf16[256,512]{0,1:T(8,128)(2,1)S(1)} %get-tuple-element.48), channel_id=1, source_target_pairs={{2,26},{3,27},{5,29},{7,31},{10,18},{11,19},{12,20},{14,22},{16,8}... | collective-permute-start | bytes 786440 | tf_op jit(solution)/shard_map/ppermute | solution.py:328
  86.0 6.0 %collective-permute-start.19 = (bf16[256,128]{1,0:T(8,128)(2,1)S(1)}, bf16[256,128]{1,0:T(8,128)(2,1)S(1)}, u32[]{:S(2)}, u32[]{:S(2)}) collective-permute-start(bf16[256,128]{1,0:T(8,128)(2,1)S(1)} %add_convert_fusion.2), channel_id=1, source_target_pairs={{0,4},{4,0},{8,12},{12,8},{16,20},{20,16},{24,28},{28,24},{1,5},{5... | collective-permute-start | bytes 196616 | tf_op jit(solution)/shard_map/ppermute | solution.py:243
  92.3 20.9 %collective-permute-start.25 = (bf16[256,512]{0,1:T(8,128)(2,1)S(1)}, bf16[256,512]{0,1:T(8,128)(2,1)S(1)}, u32[]{:S(2)}, u32[]{:S(2)}) collective-permute-start(bf16[256,512]{0,1:T(8,128)(2,1)S(1)} %get-tuple-element.49), channel_id=1, source_target_pairs={{2,10},{3,11},{4,12},{6,14},{10,2},{11,3},{13,5},{15,7},{16,24},{1... | collective-permute-start | bytes 786440 | tf_op jit(solution)/shard_map/ppermute | solution.py:328
  95.7 17.5 %collective-permute-start.26 = (bf16[256,512]{0,1:T(8,128)(2,1)S(1)}, bf16[256,512]{0,1:T(8,128)(2,1)S(1)}, u32[]{:S(2)}, u32[]{:S(2)}) collective-permute-start(bf16[256,512]{0,1:T(8,128)(2,1)S(1)} %get-tuple-element.50), channel_id=1, source_target_pairs={{0,16},{1,17},{5,21},{7,23},{8,24},{9,25},{12,28},{14,30},{18,2},{... | collective-permute-start | bytes 786440 | tf_op jit(solution)/shard_map/ppermute | solution.py:328
  97.0 19.4 %collective-permute-start.27 = (bf16[256,512]{0,1:T(8,128)(2,1)S(1)}, bf16[256,512]{0,1:T(8,128)(2,1)S(1)}, u32[]{:S(2)}, u32[]{:S(2)}) collective-permute-start(bf16[256,512]{0,1:T(8,128)(2,1)S(1)} %get-tuple-element.51), channel_id=1, source_target_pairs={{0,24},{1,25},{4,28},{6,30},{8,16},{9,17},{13,21},{15,23},{18,10},... | collective-permute-start | bytes 786440 | tf_op jit(solution)/shard_map/ppermute | solution.py:328
  (14 other events, 52.9 us)

commit v2 on v0

v2 whole, which is shorter than its diff:
```python
import functools

import jax
import jax.numpy as jnp
from jax import lax
from jax.experimental import pallas as pl
from jax.experimental.pallas import tpu as pltpu
from jax.sharding import PartitionSpec as P

HIGH = lax.Precision.HIGHEST
F32 = jnp.float32
BF16 = jnp.bfloat16
VMEM = pl.BlockSpec(memory_space=pltpu.VMEM)
ANY = pl.BlockSpec(memory_space=pl.ANY)
SMEM = pl.BlockSpec(memory_space=pltpu.SMEM)
NN = (((1,), (0,)), ((), ()))
NT = (((1,), (1,)), ((), ()))
TN = (((0,), (0,)), ((), ()))


def mm(left, right, dims):
    return lax.dot_general(left, right, dims, preferred_element_type=F32)


class Fetch:
    def __init__(self, source, buffer, semaphores, axis=1):
        self.buffer, self.axis = buffer, axis
        self.count = semaphores.shape[0]
        self.step = buffer.shape[axis] // self.count
        at = [
            (slice(None),) * axis + (slice(i * self.step, (i + 1) * self.step),)
            for i in range(self.count)
        ]
        self.copies = [
            pltpu.make_async_copy(source.at[p], buffer.at[p], semaphores.at[i])
            for i, p in enumerate(at)
        ]
        self.waiting = set(range(self.count))

    def __getitem__(self, index):
        span = index[self.axis] if isinstance(index, tuple) else slice(None)
        first, last = span.start or 0, span.stop or self.buffer.shape[self.axis]
        for i in sorted(self.waiting):
            if first < (i + 1) * self.step and i * self.step < last:
                self.copies[i].wait()
                self.waiting.discard(i)
        return self.buffer[index]


def start_all(*fetches):
    for i in range(max(f.count for f in fetches)):
        for f in fetches:
            if i < f.count:
                f.copies[i].start()


class Store(Fetch):
    def __init__(self, target, buffer, semaphores, axis=1):
        self.buffer, self.axis = buffer, axis
        self.count = semaphores.shape[0]
        self.step = buffer.shape[axis] // self.count
        at = [
            (slice(None),) * axis + (slice(i * self.step, (i + 1) * self.step),)
            for i in range(self.count)
        ]
        self.copies = [
            pltpu.make_async_copy(buffer.at[p], target.at[p], semaphores.at[i])
            for i, p in enumerate(at)
        ]

    def __setitem__(self, index, value):
        self.buffer[index] = value

    def send(self, i):
        self.copies[i].start()

    def finish(self):
        for copy in self.copies:
            copy.wait()


class Line:
    def __init__(self):
        self.last = None
        self.held = {}

    def call(self, body, outs, *args, scratch=(), scalars=0, fetch={}, store={}, raw=(), raw_out=()):
        fetch = {i: f if isinstance(f, tuple) else (f, 1) for i, f in fetch.items()}
        store = {i: f if isinstance(f, tuple) else (f, 1) for i, f in store.items()}
        shapes = [
            (pltpu.HBM if i in store or i in raw_out else jax.ShapeDtypeStruct)(shape, dtype)
            for i, (shape, dtype) in enumerate(outs)
        ]
        seen = {id(a) for a in args}
        extra = [] if self.last is None else [self.last]
        extra += [a for a in self.held.values() if a is not self.last]
        extra = [a for a in extra if id(a) not in seen]
        count, more, results = len(args), len(extra), len(outs)
        hbm = pl.BlockSpec(memory_space=pltpu.HBM)
        specs = [SMEM if i < scalars else hbm if i in fetch or i in raw else VMEM for i in range(count)]
        buffers = []
        for i, (blocks, _) in fetch.items():
            buffers += [pltpu.VMEM(args[i].shape, args[i].dtype), pltpu.SemaphoreType.DMA((blocks,))]
        for i, (blocks, _) in store.items():
            buffers += [pltpu.VMEM(*outs[i]), pltpu.SemaphoreType.DMA((blocks,))]

        def kernel(*refs):
            ins, out = list(refs[:count]), list(refs[count + more : count + more + results])
            rest = list(refs[count + more + results :])
            for i, (_, axis) in fetch.items():
                ins[i] = Fetch(ins[i], rest.pop(0), rest.pop(0), axis)
            for i, (_, axis) in store.items():
                out[i] = Store(out[i], rest.pop(0), rest.pop(0), axis)
            if fetch:
                start_all(*[ins[i] for i in fetch])
            body(*ins, *out, *rest)
            for i in store:
                out[i].finish()

        args = [
            pltpu.with_memory_space_constraint(a, pltpu.HBM) if i in fetch or i in raw else a
            for i, a in enumerate(args)
        ]
        values = pl.pallas_call(
            kernel,
            out_shape=shapes,
            in_specs=specs + [ANY] * more,
            out_specs=[hbm if i in store or i in raw_out else VMEM for i in range(results)],
            scratch_shapes=buffers + list(scratch),
            compiler_params=pltpu.CompilerParams(vmem_limit_bytes=24 * 1024 * 1024),
        )(*args, *extra)
        self.last = values[0]
        return values


def foot_rows(heads):
    return -(-3 * heads // 16) * 16


def put_foot(out, base, totals):
    rows = []
    for total in totals:
        for _ in range(3):
            part = total.astype(BF16)
            rows.append(part.astype(F32))
            total = total - part.astype(F32)
    width = rows[0].shape[1]
    fill = foot_rows(len(totals)) - len(rows)
    if fill:
        rows.append(jnp.zeros((fill, width), F32))
    out[base:, :] = jnp.concatenate(rows, axis=0).astype(BF16)


def get_foot(message, base, heads):
    foot = message[base:, :].astype(F32)
    return [
        foot[3 * h : 3 * h + 1, :] + foot[3 * h + 1 : 3 * h + 2, :] + foot[3 * h + 2 : 3 * h + 3, :]
        for h in range(heads)
    ]


RUN, GROW, TAIL, GROW_BLOCK, TAIL_BLOCK = range(5)


def state_body(keys, values, log_decay, tables, update, packed):
    heads, size = log_decay.buffer.shape[0], tables.shape[2]
    chunks = tables.shape[1] // heads
    width = update.shape[1]
    upper = (
        lax.broadcasted_iota(jnp.int32, (size, size), 0)
        <= lax.broadcasted_iota(jnp.int32, (size, size), 1)
    ).astype(F32)
    pieces = jnp.concatenate(
        [log_decay[:, j * size : (j + 1) * size] for j in range(chunks)], axis=0
    )
    run = lax.dot_general(pieces, upper, NN, precision=HIGH, preferred_element_type=F32)
    ends = [run[j * heads : (j + 1) * heads, size - 1 : size] for j in range(chunks)]
    before, after = [jnp.zeros((heads, 1), F32)], [jnp.zeros((heads, 1), F32)]
    for j in range(chunks - 1):
        before.append(before[-1] + ends[j])
        after.append(after[-1] + ends[chunks - 1 - j])
    before = jnp.concatenate(before, axis=0)
    after = jnp.concatenate(after[::-1], axis=0)
    left = run[:, size - 1 : size] - run
    tables[RUN] = run
    tables[GROW] = jnp.exp(run)
    tables[TAIL] = jnp.exp(left)
    tables[GROW_BLOCK] = jnp.exp(run + before)
    tables[TAIL_BLOCK] = jnp.exp(left + after)
    tail_columns = jnp.exp(left).T
    for h in range(heads):
        cols = slice(h * width, (h + 1) * width)
        state = None
        for j in range(chunks):
            rows = slice(j * size, (j + 1) * size)
            r = j * heads + h
            tail = (keys[rows, cols] * tail_columns[:, r : r + 1]).astype(BF16)
            term = mm(tail, values[rows, cols], TN)
            end = jnp.exp(run[r : r + 1, size - 1 : size])
            state = term if state is None else state * end + term
        update[cols, :] = state
        packed[cols, :] = state.astype(BF16)
    put_foot(packed, heads * width, block_totals(run, heads, width))


def block_totals(run, heads, width):
    chunks, size = run.shape[0] // heads, run.shape[1]
    ends = run[:, size - 1 : size]
    return [
        sum(
            jnp.broadcast_to(ends[j * heads + h : j * heads + h + 1, :], (1, width))
            for j in range(chunks)
        )
        for h in range(heads)
    ]


def combine_body(forward, heads, place, own, packed, other, out, whole):
    core = place[1]
    width = own.shape[1]
    rows = heads * width
    mine, theirs = get_foot(packed, rows, heads), get_foot(other, rows, heads)
    late = core == (1 if forward else 0)
    for h in range(heads):
        at = slice(h * width, (h + 1) * width)
        a, b = own[at, :], other[at, :].astype(F32)
        joined = jnp.where(late, a + jnp.exp(mine[h]) * b, b + jnp.exp(theirs[h]) * a)
        whole[at, :] = joined
    half = rows // 2
    out[:half, :] = whole[pl.ds(pl.multiple_of(core * half, half), half), :].astype(BF16)
    put_foot(out, half, [a + b for a, b in zip(mine, theirs)])


def join_body(forward, heads, chips, place, *refs):
    messages, out = refs[: chips - 1], refs[chips - 1]
    chip, core = place[0], place[1]
    half, width = out.shape
    feet = [get_foot(m, half, heads) for m in messages]
    spans = [jnp.zeros((1, width), F32)] * heads
    head_rows = half * 2 // heads
    groups = max(1, half // head_rows)
    total = [None] * groups
    for k in range(1, chips) if forward else range(chips - 1, 0, -1):
        used = (k <= chip) if forward else (k > chip)
        for g in range(groups):
            span = spans[0] if heads == 1 else jnp.where(core == 0, spans[g], spans[groups + g])
            factor = jnp.where(used, jnp.exp(span), 0.0)
            at = slice(g * half // groups, (g + 1) * half // groups)
            term = factor * messages[k - 1][at, :].astype(F32)
            total[g] = term if total[g] is None else total[g] + term
        spans = [span + foot for span, foot in zip(spans, feet[k - 1])]
    for g in range(groups):
        out[g * half // groups : (g + 1) * half // groups, :] = total[g].astype(BF16)


def enter(forward, heads, place, mine, theirs, other, out):
    core = place[1]
    half, width = mine.shape
    rows = 2 * half
    out[pl.ds(pl.multiple_of(core * half, half), half), :] = mine[...].astype(F32)
    out[pl.ds(pl.multiple_of((1 - core) * half, half), half), :] = theirs[...].astype(F32)
    totals = get_foot(other, rows, heads)
    late = core == (1 if forward else 0)
    for h in range(heads):
        at = slice(h * width, (h + 1) * width)
        now = out[at, :]
        moved = other[at, :].astype(F32) + jnp.exp(totals[h]) * now
        out[at, :] = jnp.where(late, moved, now)


def causal_mask(size):
    return lax.broadcasted_iota(jnp.int32, (size, size), 0) >= lax.broadcasted_iota(
        jnp.int32, (size, size), 1
    )


def decay_of(run, columns, r, causal):
    return jnp.exp(jnp.where(causal, columns[:, r : r + 1] - run[r : r + 1, :], -jnp.inf))


def local_body(queries, keys, values, tables, mixed, grown_rows):
    size = tables.shape[2]
    length, columns = mixed.shape
    chunks = length // size
    heads = tables.shape[1] // chunks
    width = columns // heads
    causal = causal_mask(size)
    run = tables[RUN]
    sums, grow, tails = run.T, tables[GROW].T, tables[TAIL].T
    for h in range(heads):
        cols = slice(h * width, (h + 1) * width)
        state = None
        for j in range(chunks):
            rows = slice(j * size, (j + 1) * size)
            r = j * heads + h
            query, key, value = queries[rows, cols], keys[rows, cols], values[rows, cols]
            weight = (mm(query, key, NT) * decay_of(run, sums, r, causal)).astype(BF16)
            grown = query * grow[:, r : r + 1]
            grown_rows[cols, rows] = grown.T.astype(BF16)
            out = mm(weight, value, NN)
            if state is not None:
                out = out + mm(grown.astype(BF16), state.astype(BF16), NN)
            mixed[rows, cols] = out
            if j < chunks - 1:
                term = mm((key * tails[:, r : r + 1]).astype(BF16), value, TN)
                end = grow[size - 1 : size, r : r + 1]
                state = term if state is None else state * end + term
        grown_rows.send(h)


def norm_body(
    heads, place, mixed, queries, tables, mine, theirs, other, attended, inverse, incoming
):
    width = mine.shape[1]
    size = tables.shape[2]
    chunks = tables.shape[1] // heads
    enter(True, heads, place, mine, theirs, other, incoming)
    grow = tables[GROW_BLOCK].T
    ones = jnp.full((width, width), 1.0 / width, BF16)
    lane = lax.broadcasted_iota(jnp.int32, (size, width), 1)
    low = [incoming[h * width : (h + 1) * width, :].astype(BF16) for h in range(heads)]
    for j in range(chunks):
        rows = slice(j * size, (j + 1) * size)
        scales = jnp.zeros((size, width), F32)
        for h in range(heads):
            cols = slice(h * width, (h + 1) * width)
            r = j * heads + h
            grown = (queries[rows, cols] * grow[:, r : r + 1]).astype(BF16)
            total = mixed[rows, cols] + mm(grown, low[h], NN)
            scale = lax.rsqrt(mm((total * total).astype(BF16), ones, NN) + 1e-05)
            scales = jnp.where(lane == h, scale, scales)
            attended[rows, cols] = (total * scale).astype(BF16)
        inverse[j * heads : (j + 1) * heads, :] = scales.T[:heads, :]
        attended.send(j)


def head_grad_body(size, starts, weight, whole, out):
    for t in range(out.shape[0] // size):
        rows = slice(t * size, (t + 1) * size)
        out[rows, :] = mm(whole[rows, :], weight[...], NN)


def early_body(size, place, starts, weight, attended, *refs):
    pieces, mine, theirs, out, rows_of_weight, semaphores = (
        refs[:3], refs[3], refs[4:7], refs[7], refs[8], refs[9]
    )
    core = place[1]
    part = mine.shape[1]
    copies = []
    for i in range(3):
        start = pl.multiple_of(starts[i] * 64, 64)
        copies.append(
            pltpu.make_async_copy(
                weight.at[pl.ds(start, 2 * part), :], rows_of_weight.at[i], semaphores.at[i]
            )
        )
        copies[i].start()
    for i, piece in enumerate(pieces):
        product = mm(piece[...], attended[...], TN)
        low, high = product[:part, :].astype(BF16), product[part:, :].astype(BF16)
        mine[i] = jnp.where(core == 0, low, high)
        theirs[i][...] = jnp.where(core == 0, high, low)
    for copy in copies:
        copy.wait()
    for t in range(out.shape[0] // size):
        rows = slice(t * size, (t + 1) * size)
        out[rows, :] = sum(mm(piece[rows, :], rows_of_weight[i], NN) for i, piece in enumerate(pieces))


def late_body(heads, number, place, starts, weight, attended, *refs):
    pieces = refs[:number]
    refs = refs[number:]
    partial, inverse, grown_rows, tables, mixed_grad, update, packed = refs[:7]
    width = update.shape[1]
    size = tables.shape[2]
    chunks = tables.shape[1] // heads
    if number:
        mine, theirs, rows_of_weight, semaphores = refs[7:]
        core = place[1]
        part = mine.shape[0]
        start = pl.multiple_of(starts[0] * 64, 64)
        copy = pltpu.make_async_copy(
            weight.at[pl.ds(start, 2 * part), :], rows_of_weight, semaphores.at[0]
        )
        copy.start()
        low, high = [mm(p[...], attended[...], TN).astype(BF16) for p in pieces]
        mine[...] = jnp.where(core == 0, low, high)
        theirs[...] = jnp.where(core == 0, high, low)
        copy.wait()
    ones = jnp.full((width, width), 1.0 / width, BF16)
    states = [None] * heads
    run = tables[RUN]
    scales = inverse[...].T
    for j in reversed(range(chunks)):
        rows = slice(j * size, (j + 1) * size)
        total = partial[rows, :]
        for i, piece in enumerate(pieces):
            total = total + mm(
                piece[rows, :], rows_of_weight[i * part : (i + 1) * part, :], NN
            )
        for h in range(heads):
            cols = slice(h * width, (h + 1) * width)
            r = j * heads + h
            grad = total[:, cols]
            unit = attended[rows, cols].astype(F32)
            mean = mm((grad * unit).astype(BF16), ones, NN)
            grad = ((grad - unit * mean) * scales[:, r : r + 1]).astype(BF16)
            mixed_grad[rows, cols] = grad
            term = mm(grown_rows[cols, rows], grad, NN)
            end = jnp.exp(run[r : r + 1, size - 1 : size])
            states[h] = term if states[h] is None else term + states[h] * end
    for h in range(heads):
        at = slice(h * width, (h + 1) * width)
        update[at, :] = states[h]
        packed[at, :] = states[h].astype(BF16)
    put_foot(packed, heads * width, block_totals(run, heads, width))


def back_body(
    heads, queries, keys, values, mixed_grad, tables, incoming, grown_rows,
    query_grad, key_grad, value_grad, states,
):
    width = incoming.shape[1]
    size = tables.shape[2]
    chunks = tables.shape[1] // heads
    causal = causal_mask(size)
    run = tables[RUN]
    sums, grow, tails = run.T, tables[GROW].T, tables[TAIL].T
    for h in range(heads):
        cols = slice(h * width, (h + 1) * width)
        state = incoming[cols, :]
        for j in range(chunks):
            rows = slice(j * size, (j + 1) * size)
            r = j * heads + h
            states[j] = state.astype(BF16)
            if j < chunks - 1:
                tail = (keys[rows, cols] * tails[:, r : r + 1]).astype(BF16)
                state = state * grow[size - 1 : size, r : r + 1] + mm(tail, values[rows, cols], TN)
        back = None
        for j in reversed(range(chunks)):
            rows = slice(j * size, (j + 1) * size)
            r = j * heads + h
            grad, query = mixed_grad[rows, cols], queries[rows, cols]
            key, value = keys[rows, cols], values[rows, cols]
            decay = decay_of(run, sums, r, causal)
            weight = (mm(query, key, NT) * decay).astype(BF16)
            masked = (mm(grad, value, NT) * decay).astype(BF16)
            grown = (grad * grow[:, r : r + 1]).astype(BF16)
            query_grad[rows, cols] = (mm(masked, key, NN) + mm(grown, states[j], NT)).astype(BF16)
            key_part = mm(masked, query, TN)
            value_part = mm(weight, grad, TN)
            term = mm(grown_rows[cols, rows], grad, NN)
            if back is not None:
                tail = tails[:, r : r + 1]
                low = back.astype(BF16)
                key_part = key_part + mm((value * tail).astype(BF16), low, NT)
                value_part = value_part + mm((key * tail).astype(BF16), low, NN)
                term = term + back * grow[size - 1 : size, r : r + 1]
            back = term
            key_grad[rows, cols] = key_part.astype(BF16)
            value_grad[rows, cols] = value_part.astype(BF16)
        query_grad.send(h)
        key_grad.send(h)
        value_grad.send(h)


def final_body(
    heads, place, keys, values, tables, mine, theirs, other, key_part, value_part,
    key_grad, value_grad, outgoing,
):
    width = mine.shape[1]
    size = tables.shape[2]
    chunks = tables.shape[1] // heads
    enter(False, heads, place, mine, theirs, other, outgoing)
    tails = tables[TAIL_BLOCK].T
    for h in range(heads):
        cols = slice(h * width, (h + 1) * width)
        state = outgoing[cols, :].astype(BF16)
        for j in range(chunks):
            rows = slice(j * size, (j + 1) * size)
            r = j * heads + h
            tail = tails[:, r : r + 1]
            key_grad[rows, cols] = (
                key_part[rows, cols] + mm((values[rows, cols] * tail).astype(BF16), state, NT)
            ).astype(BF16)
            value_grad[rows, cols] = (
                value_part[rows, cols] + mm((keys[rows, cols] * tail).astype(BF16), state, NN)
            ).astype(BF16)
        key_grad.send(h)
        value_grad.send(h)


def fold_body(place, mine, low, middle, high, kept, sent):
    odd = place[2] % 2 == 1
    sums = [mine[i].astype(F32) + part[...].astype(F32) for i, part in enumerate((low, middle, high))]
    kept[0] = jnp.where(odd, sums[1], sums[0]).astype(BF16)
    kept[1] = sums[2].astype(BF16)
    sent[0] = jnp.where(odd, sums[0], sums[1]).astype(BF16)
    sent[1] = sums[2].astype(BF16)


def fold_again_body(place, kept, arrived, total, sent):
    turn = place[2]
    first = kept[0].astype(F32) + arrived[0].astype(F32)
    second = kept[1].astype(F32) + arrived[1].astype(F32)
    total[...] = jnp.where(turn == 2, second, first)
    sent[...] = jnp.where(turn == 0, second, first).astype(BF16)


def fold_last_body(mine, arrived, kept, sent):
    value = mine[...].astype(F32) + arrived[...].astype(F32)
    kept[...] = value
    sent[...] = value.astype(BF16)


def add_body(kept, arrived, total, sent):
    value = kept[...] + arrived[...].astype(F32)
    total[...] = value
    sent[...] = value.astype(BF16)


def cut_body(part, x, y, low, high, *rest):
    buffers, semaphores = rest[:2], rest[2]
    loads = [
        pltpu.make_async_copy(source, buffer, semaphores.at[i])
        for i, (source, buffer) in enumerate(
            ((x.at[:, :part], buffers[0]), (y.at[:, part:], buffers[1]))
        )
    ]
    stores = [
        pltpu.make_async_copy(buffer, target, semaphores.at[2 + i])
        for i, (buffer, target) in enumerate(((buffers[0], low), (buffers[1], high)))
    ]
    for load in loads:
        load.start()
    for load, store in zip(loads, stores):
        load.wait()
        store.start()
    for store in stores:
        store.wait()


def hop(value, step, senders, chips, count):
    moves = [
        (s * count + y, ((s // 2 ^ step) * 2 + s % 2) * count + y)
        for s in range(2 * chips)
        for y in range(count)
        if s // 2 ^ y in senders
    ]
    return lax.ppermute(value, ("seq", "head"), moves)


class Chain:
    def __init__(self, line, forward, heads, chips, place, update, packed):
        self.line, self.forward, self.heads, self.chips = line, forward, heads, chips
        self.place, self.update, self.packed = place, update, packed
        self.other = self.swap(packed)

    def swap(self, value):
        return lax.ppermute(value, "seq", [(i, i ^ 1) for i in range(2 * self.chips)])

    def send(self):
        rows, width = self.update.shape
        self.half = (rows // 2, width)
        message, = self.line.call(
            functools.partial(combine_body, self.forward, self.heads),
            [((rows // 2 + foot_rows(self.heads), width), BF16)],
            self.place, self.update, self.packed, self.other,
            scratch=[pltpu.VMEM((rows, width), F32)], scalars=1,
        )
        self.line.held[self] = self.other
        self.arrived = [
            lax.ppermute(
                message, "seq",
                [(i, (i // 2 + k) % self.chips * 2 + i % 2) for i in range(2 * self.chips)],
            )
            for k in range(1, self.chips)
        ]

    def join(self):
        self.mine, = self.line.call(
            functools.partial(join_body, self.forward, self.heads, self.chips),
            [(self.half, BF16)], self.place, *self.arrived, scalars=1,
        )
        self.theirs = self.swap(self.mine)

    def done(self):
        self.line.held.pop(self)
        return self.mine, self.theirs, self.other


def on_device(seq_size, head_size, queries, keys, values, log_decay, out_weight, out_grad):
    length, columns = queries.shape
    heads = log_decay.shape[0]
    width = columns // heads
    size = 256 if length % 256 == 0 else length
    chunks = length // size
    chips = seq_size // 2
    near = head_size == 4 and chips == 4
    seq, head = lax.axis_index("seq"), lax.axis_index("head")
    place = jnp.stack([seq // 2, seq % 2, (seq // 2) ^ head]).astype(jnp.int32)
    block = out_grad.shape[1]
    part = block // 2
    move = lambda a, k: lax.ppermute(a, "head", [(i, i ^ k) for i in range(head_size)])
    if near:
        x, y = move(out_grad, 1), move(out_grad, 2)
    else:
        whole = lax.all_gather(out_grad, "head", axis=1, tiled=True)
    state = ((heads * width, width), F32)
    message = ((heads * width + foot_rows(heads), width), BF16)
    rows = (length, columns)
    line = Line()
    held = line.held

    def starts_of(group):
        return jnp.stack(
            [((head ^ k) * block + side * part) // 64 for k, side in group]
        ).astype(jnp.int32)

    tables, update, packed = line.call(
        state_body, [((5, chunks * heads, size), F32), state, message], keys, values, log_decay,
        fetch={2: 1, 0: heads, 1: heads},
    )
    forward = Chain(line, True, heads, chips, place, update, packed)
    pass
    forward.send()
    mixed, grown_rows = line.call(
        local_body, [(rows, F32), ((columns, length), BF16)], queries, keys, values, tables,
        fetch={i: heads for i in range(3)}, store={1: (heads, 0)},
    )
    held.update(mixed=mixed)
    forward.join()
    entering = forward.done()
    held.pop("mixed")
    attended, inverse, incoming = line.call(
        functools.partial(norm_body, heads),
        [(rows, BF16), ((chunks * heads, size), F32), state],
        place, mixed, queries, tables, *entering, scalars=1,
        fetch={2: (chunks, 0)}, store={0: (chunks, 0)},
    )
    held.update(inverse=inverse, incoming=incoming)
    swap = lambda a: lax.ppermute(a, "seq", [(i, i ^ 1) for i in range(2 * chips)])
    shape = (part, columns)
    if near:
        low, high = line.call(
            functools.partial(cut_body, part), [((length, part), BF16)] * 2, x, y,
            scratch=[pltpu.VMEM((length, part), BF16)] * 2 + [pltpu.SemaphoreType.DMA((4,))],
            raw=(0, 1), raw_out=(0, 1),
        )
        diagonal = [move(low, 2), move(high, 1)]
        products, *theirs, partial = line.call(
            functools.partial(early_body, size),
            [((3,) + shape, BF16)] + [(shape, BF16)] * 3 + [(rows, F32)],
            place, starts_of([(0, 0), (1, 0), (2, 0)]), out_weight, attended, out_grad, x, y,
            scratch=[pltpu.VMEM((3, block, columns), BF16), pltpu.SemaphoreType.DMA((3,))],
            scalars=2, raw=(2,), fetch={3: 1, 4: 1, 5: 1, 6: 1},
        )
        arrived = [swap(a) for a in theirs]
        held["partial"] = partial
        kept, sent = line.call(
            fold_body, [((2,) + shape, BF16), ((2,) + shape, BF16)],
            place, products, *arrived, scalars=1,
        )
        arrived = hop(sent, 1, (0, 1, 2, 3), chips, head_size)
        held["kept"] = kept
        held.pop("partial")
        mixed_grad, back_update, back_packed, last, theirs = line.call(
            functools.partial(late_body, heads, 2),
            [(rows, BF16), state, message, (shape, BF16), (shape, BF16)],
            place, starts_of([(3, 0)]), out_weight, attended, *diagonal, partial, inverse,
            grown_rows, tables,
            scratch=[pltpu.VMEM((block, columns), BF16), pltpu.SemaphoreType.DMA((1,))],
            scalars=2, raw=(2,), fetch={3: 1, 4: 1, 5: 1, 8: (1, 0)},
        )
        held["last"] = last
        last_arrived = swap(theirs)
    else:
        partial, = line.call(
            functools.partial(head_grad_body, size), [(rows, F32)],
            jnp.zeros((1,), jnp.int32), out_weight, whole, scalars=1,
        )
        mixed_grad, back_update, back_packed = line.call(
            functools.partial(late_body, heads, 0), [(rows, BF16), state, message],
            place, jnp.zeros((1,), jnp.int32), out_weight, attended, partial, inverse,
            grown_rows, tables, scalars=2,
        )
    back = Chain(line, False, heads, chips, place, back_update, back_packed)
    held.pop("inverse")
    held["mixed_grad"] = mixed_grad
    held["update"] = back_update
    if near:
        held.pop("last")
        last, sent = line.call(
            fold_last_body, [(shape, F32), (shape, BF16)], last, last_arrived
        )
        held["last"] = last
        last_arrived = hop(sent, 1, (0, 2), chips, head_size)
    held.pop("update")
    back.send()
    if near:
        held.pop("kept")
        kept, sent = line.call(
            fold_again_body, [(shape, F32), (shape, BF16)], place, kept, arrived, scalars=1
        )
        arrived = hop(sent, 2, (0, 2, 3), chips, head_size)
    query_grad, key_part, value_part = line.call(
        functools.partial(back_body, heads), [(rows, BF16), (rows, BF16), (rows, BF16)],
        queries, keys, values, mixed_grad, tables, incoming, grown_rows,
        fetch={0: heads, 1: heads, 2: heads, 6: (heads, 0)}, store={i: heads for i in range(3)},
        scratch=[pltpu.VMEM((chunks, width, width), BF16)],
    )
    for name in ("mixed_grad", "incoming"):
        held.pop(name)
    back.join()
    if near:
        held.pop("last")
        last, sent = line.call(add_body, [(shape, F32), (shape, BF16)], last, last_arrived)
        last_arrived = hop(sent, 2, (1,), chips, head_size)
    key_grad, value_grad = line.call(
        functools.partial(final_body, heads), [(rows, BF16)] * 2,
        place, keys, values, tables, *back.done(), key_part, value_part,
        scratch=[pltpu.VMEM((heads * width, width), F32)], scalars=1,
        fetch={1: heads, 2: heads, 7: heads, 8: heads}, store={0: heads, 1: heads},
    )
    if near:
        weight_grad = jnp.where(
            place[2] == 3, last + last_arrived.astype(F32), kept + arrived.astype(F32)
        )
    else:
        weight_grad = lax.psum_scatter(
            mm(whole, attended, TN), "seq", scatter_dimension=0, tiled=True
        )
    return attended, query_grad, key_grad, value_grad, weight_grad.astype(BF16)


def solution(mesh):
    block = P("seq", "head")
    return jax.shard_map(
        functools.partial(on_device, mesh.shape["seq"], mesh.shape["head"]),
        mesh=mesh,
        in_specs=(block, block, block, P("head", "seq"), P(None, "head"), block),
        out_specs=(block,) * 5,
        check_vma=False,
    )
```

time: 199 us -> 89.7 us (0.45)
  waiting for transfers between devices: 77.3 us -> 8.71 us
  matrix products: 60.2 us -> 0 us
  Pallas kernels: 0 us -> 48.1 us
  starting transfers between devices: 0.34 us -> 25.3 us
  blocking collectives: 18.4 us -> 0 us
  local copies, waits for them, and re-layouts: 18.9 us -> 4.44 us
  between operations: 14.6 us -> 0.97 us
  other arithmetic: 8.4 us -> 1.03 us
    dot_general x16 -> x0, matrix products: 60.2 us -> none  [the longest x1 7.6 us: on_device(): jnp.einsum('thd,shd->hts', query_rows, key_rows, preferred_element_type=j...]
    pallas_call x0 -> x16, Pallas kernels: none -> 48.1 us  [call(): pl.pallas_call(kernel, out_shape=shapes, in_specs=specs + [ANY] * more, o...]
    all_gather x3 -> x0, waiting for transfers between devices: 44 us -> none  [the longest x1 44 us: on_device(): full_grad = lax.all_gather(out_grad, 'head', axis=1, tiled=True)]
    reduce_scatter x1 -> x0, waiting for transfers between devices: 32.6 us -> none  [on_device(): lax.psum_scatter(lax.dot_general(full_grad, attended_flat, (((0,), (0,)),...]
    ppermute x0 -> x22, starting transfers between devices: none -> 25.3 us  [the longest x6 10.8 us: send(): lax.ppermute(message, 'seq', [(i, (i // 2 + k) % self.chips * 2 + i % 2)...]
    unnamed x1 -> x0, blocking collectives: 18.4 us -> none
    unnamed x36 -> x8, local copies, waits for them, and re-layouts: 18.4 us -> 4.44 us
    ppermute x0 -> x22, waiting for transfers between devices: none -> 8.71 us  [the longest x4 5.06 us: swap(): lax.ppermute(value, 'seq', [(i, i ^ 1) for i in range(2 * self.chips)])]
  transfers between devices with their start and end apart: 4 -> 22, of which waited for: 2 -> 9; matrix products, arithmetic and copies ran while one was open for 33% -> 0% of each run, Pallas kernels for 0% -> 52%
where the time goes in v2:
time: 89.7 us; the launch traced here: 88.6 us
  Pallas kernels  48.1 us (54%)
  starting transfers between devices  25.3 us (28%)
  waiting for transfers between devices  8.71 us (10%)
  local copies, waits for them, and re-layouts  4.44 us (5%)
  other arithmetic  1.03 us (1%)
  between operations  0.97 us (1%)
    pallas_call x16, Pallas kernels, call(): pl.pallas_call(kernel, out_shape=shapes, in_specs=specs + [ANY] * more, o...  48.1 us
    ppermute x6, starting transfers between devices, send(): lax.ppermute(message, 'seq', [(i, (i // 2 + k) % self.chips * 2 + i % 2)...  10.8 us
    ppermute x4, starting transfers between devices, hop(): return lax.ppermute(value, ('seq', 'head'), moves)  7.67 us
    ppermute x4, starting transfers between devices, on_device(): lax.ppermute(a, 'head', [(i, i ^ k) for i in range(head_size)])  5.77 us
    ppermute x4, waiting for transfers between devices, swap(): lax.ppermute(value, 'seq', [(i, i ^ 1) for i in range(2 * self.chips)])  5.06 us
    unnamed x8, local copies, waits for them, and re-layouts  4.44 us
    ppermute x4, waiting for transfers between devices, on_device(): lax.ppermute(a, 'seq', [(i, i ^ 1) for i in range(2 * chips)])  3.56 us
  transfers between devices with their start and end apart: 22, of which 9 were waited for; matrix products, arithmetic and copies ran while one was open for 0% of the time, Pallas kernels for 52%

profile of v2, /device:TPU:0, one launch (start us, length us, event | category | flops | bytes accessed | tf_op | source)
XLA Modules:
  0.0 88.6 jit_solution(14776278044838422206)
XLA Ops:
  0.6 3.0 %collective-permute-start.5 = (bf16[1024,512]{1,0:T(8,128)(2,1)}, bf16[1024,512]{1,0:T(8,128)(2,1)S(1)}, u32[]{:S(2)}, u32[]{:S(2)}) collective-permute-start(bf16[1024,512]{1,0:T(8,128)(2,1)} %refs_4_.1), channel_id=1, source_target_pairs={{0,1},{1,0},{2,3},{3,2},{4,5},{5,4},{6,7},{7,6},{8,9},{9,8},{10,11... | collective-permute-start | bytes 3145736 | tf_op jit(solution)/shard_map/ppermute | solution.py:604
  3.6 1.5 %collective-permute-start.6 = (bf16[1024,512]{1,0:T(8,128)(2,1)}, bf16[1024,512]{1,0:T(8,128)(2,1)}, u32[]{:S(2)}, u32[]{:S(2)}) collective-permute-start(bf16[1024,512]{1,0:T(8,128)(2,1)} %refs_4_.1), channel_id=1, source_target_pairs={{0,2},{1,3},{2,0},{3,1},{4,6},{5,7},{6,4},{7,5},{8,10},{9,11},{10,... | collective-permute-start | bytes 3145736 | tf_op jit(solution)/shard_map/ppermute | solution.py:604
  5.2 4.0 %shard_map.101 = (f32[5,16,256]{2,1,0:T(8,128)S(1)}, f32[512,128]{1,0:T(8,128)S(1)}, bf16[528,128]{1,0:T(8,128)(2,1)S(1)}) custom-call(bf16[1024,512]{1,0:T(8,128)(2,1)} %refs_1_.7, bf16[1024,512]{1,0:T(8,128)(2,1)} %refs_2_.13, f32[4,1024]{1,0:T(4,128)} %refs_2_.7), custom_call_target="tpu_custom_call" | custom-call | tf_op jit(solution)/shard_map/pallas_call | solution.py:124
  9.3 1.2 %collective-permute-done.refs_3_.refs_5_.refs_6_ = bf16[528,128]{1,0:T(8,128)(2,1)S(1)} collective-permute-done((bf16[528,128]{1,0:T(8,128)(2,1)S(1)}, bf16[528,128]{1,0:T(8,128)(2,1)S(1)}, u32[]{:S(2)}, u32[]{:S(2)}) %collective-permute-start) | collective-permute-done | bytes 135200 | tf_op jit(solution)/shard_map/ppermute | solution.py:560
  11.2 1.6 %collective-permute-start.1 = (bf16[272,128]{1,0:T(8,128)(2,1)S(1)}, bf16[272,128]{1,0:T(8,128)(2,1)S(1)}, u32[]{:S(2)}, u32[]{:S(2)}) collective-permute-start(bf16[272,128]{1,0:T(8,128)(2,1)S(1)} %shard_map.102.refs_4_), channel_id=1, source_target_pairs={{0,8},{4,12},{8,16},{12,20},{16,24},{20,28},{24,0},{28,4},{1,9},{5... | collective-permute-start | bytes 208904 | tf_op jit(solution)/shard_map/ppermute | solution.py:573
  12.8 2.6 %collective-permute-start.2 = (bf16[272,128]{1,0:T(8,128)(2,1)S(1)}, bf16[272,128]{1,0:T(8,128)(2,1)S(1)}, u32[]{:S(2)}, u32[]{:S(2)}) collective-permute-start(bf16[272,128]{1,0:T(8,128)(2,1)S(1)} %shard_map.102.refs_4_), channel_id=1, source_target_pairs={{0,16},{4,20},{8,24},{12,28},{16,0},{20,4},{24,8},{28,12},{1,17},{... | collective-permute-start | bytes 208904 | tf_op jit(solution)/shard_map/ppermute | solution.py:573
  15.4 1.3 %collective-permute-start.3 = (bf16[272,128]{1,0:T(8,128)(2,1)S(1)}, bf16[272,128]{1,0:T(8,128)(2,1)S(1)}, u32[]{:S(2)}, u32[]{:S(2)}) collective-permute-start(bf16[272,128]{1,0:T(8,128)(2,1)S(1)} %shard_map.102.refs_4_), channel_id=1, source_target_pairs={{0,24},{4,28},{8,0},{12,4},{16,8},{20,12},{24,16},{28,20},{1,25},{... | collective-permute-start | bytes 208904 | tf_op jit(solution)/shard_map/ppermute | solution.py:573
  16.8 6.1 %shard_map.103 = (f32[1024,512]{1,0:T(8,128)S(1)}, bf16[512,1024]{1,0:T(8,128)(2,1)}) custom-call(bf16[1024,512]{1,0:T(8,128)(2,1)} %refs_0_.5, bf16[1024,512]{1,0:T(8,128)(2,1)} %refs_1_.7, bf16[1024,512]{1,0:T(8,128)(2,1)} %refs_2_.13, f32[5,16,256]{2,1,0:T(8,128)S(1)} %get-tuple-element.38.refs_4_.refs_3_.refs_9_, ...), custom_call_target="tpu_custom_call" | custom-call | tf_op jit(solution)/shard_map/pallas_call | solution.py:124
  23.6 1.2 %collective-permute-done.4.refs_5_ = bf16[256,128]{1,0:T(8,128)(2,1)S(1)} collective-permute-done((bf16[256,128]{1,0:T(8,128)(2,1)S(1)}, bf16[256,128]{1,0:T(8,128)(2,1)S(1)}, u32[]{:S(2)}, u32[]{:S(2)}) %collective-permute-start.4) | collective-permute-done | bytes 65568 | tf_op jit(solution)/shard_map/ppermute | solution.py:560
  24.8 4.3 %shard_map.105 = (bf16[1024,512]{1,0:T(8,128)(2,1)}, f32[16,256]{1,0:T(8,128)S(1)}, f32[512,128]{1,0:T(8,128)S(1)}) custom-call(s32[3]{0:T(128)S(1)} %pad_add_fusion.refs_0_, f32[1024,512]{1,0:T(8,128)S(1)} %get-tuple-element.41.refs_4_.refs_1_, bf16[1024,512]{1,0:T(8,128)(2,1)} %refs_0_.5, f32[5,16,256]{2,1,0:T(8,128)S(1)} %get-tuple-element.38.refs_4_.refs_3_.refs_9_, ...), custom_call_target="tpu_custom_call" | custom-call | tf_op jit(solution)/shard_map/pallas_call | solution.py:124
  29.1 0.9 %copy-done.3 = bf16[1024,512]{1,0:T(8,128)(2,1)} copy-done((bf16[1024,512]{1,0:T(8,128)(2,1)}, bf16[1024,512]{1,0:T(8,128)(2,1)S(1)}, u32[]{:S(2)}) %copy-start.3) | copy-done | bytes 1048600
  30.1 1.2 %copy-done = bf16[1024,512]{1,0:T(8,128)(2,1)S(1)} copy-done((bf16[1024,512]{1,0:T(8,128)(2,1)S(1)}, bf16[1024,512]{1,0:T(8,128)(2,1)}, u32[]{:S(2)}) %copy-start) | copy-done | bytes 1048600
  31.3 2.0 %shard_map.106 = (bf16[1024,256]{1,0:T(8,128)(2,1)}, bf16[1024,256]{1,0:T(8,128)(2,1)}) custom-call(bf16[1024,512]{1,0:T(8,128)(2,1)} %copy-done.3, bf16[1024,512]{1,0:T(8,128)(2,1)} %collective-permute-done.6.refs_1_.refs_6_, bf16[1024,512]{1,0:T(8,128)(2,1)S(1)} %copy-done, f32[16,256]{1,0:T(8,128)S(1)} %get-tuple-element.43.refs_3_.refs_8_.refs_5_.refs_7_, ...), custom_call_target="tpu_custom_call" | custom-call | tf_op jit(solution)/shard_map/pallas_call | solution.py:124
  34.6 1.0 %copy-done.2 = bf16[1024,256]{1,0:T(8,128)(2,1)S(1)} copy-done((bf16[1024,256]{1,0:T(8,128)(2,1)S(1)}, bf16[1024,256]{1,0:T(8,128)(2,1)}, u32[]{:S(2)}) %copy-start.2) | copy-done | bytes 524312
  35.7 6.6 %shard_map.107 = (bf16[3,256,512]{2,1,0:T(8,128)(2,1)S(1)}, bf16[256,512]{1,0:T(8,128)(2,1)}, bf16[256,512]{1,0:T(8,128)(2,1)}, bf16[256,512]{1,0:T(8,128)(2,1)}, f32[1024,512]{1,0:T(8,128)S(1)}) custom-call(s32[3]{0:T(128)S(1)} %pad_add_fusion.refs_0_, s32[3]{0:T(128)S(1)} %pad_add_fusion.1.refs_1_, bf16[2048,512]{1,0:T(8,128)(2,1)} %refs_2_.11, ...), custom_call_target="tpu_custom_call" | custom-call | tf_op jit(solution)/shard_map/pallas_call | solution.py:124
  42.9 1.2 %collective-permute-done.10.refs_3_ = bf16[256,512]{1,0:T(8,128)(2,1)S(1)} collective-permute-done((bf16[256,512]{1,0:T(8,128)(2,1)}, bf16[256,512]{1,0:T(8,128)(2,1)S(1)}, u32[]{:S(2)}, u32[]{:S(2)}) %collective-permute-start.10) | collective-permute-done | bytes 262176 | tf_op jit(solution)/shard_map/ppermute | solution.py:642
  44.9 1.3 %shard_map.108 = (bf16[2,256,512]{2,1,0:T(8,128)(2,1)S(1)}, bf16[2,256,512]{2,1,0:T(8,128)(2,1)S(1)}) custom-call(s32[3]{0:T(128)S(1)} %pad_add_fusion.refs_0_, bf16[3,256,512]{2,1,0:T(8,128)(2,1)S(1)} %get-tuple-element.49.refs_1_, bf16[256,512]{1,0:T(8,128)(2,1)} %collective-permute-done.9.refs_2_, bf16[256,512]{1,0:T(8,128)(2,1)S(1)} %collective-permute-done.10.refs_3_, ...), custom_call_target="tpu_custom_call" | custom-call | tf_op jit(solution)/shard_map/pallas_call | solution.py:124
  46.2 1.6 %collective-permute-start.12 = (bf16[2,256,512]{2,1,0:T(8,128)(2,1)S(1)}, bf16[2,256,512]{2,1,0:T(8,128)(2,1)S(1)}, u32[]{:S(2)}, u32[]{:S(2)}) collective-permute-start(bf16[2,256,512]{2,1,0:T(8,128)(2,1)S(1)} %get-tuple-element.55), channel_id=1, source_target_pairs={{0,8},{1,9},{2,10},{3,11},{4,12},{5,13},{6,14},{7,15},{8,0},{9,1},... | collective-permute-start | bytes 1572872 | tf_op jit(solution)/shard_map/ppermute | solution.py:550
  47.9 5.2 %shard_map.109 = (bf16[1024,512]{1,0:T(8,128)(2,1)S(1)}, f32[512,128]{1,0:T(8,128)S(1)}, bf16[528,128]{1,0:T(8,128)(2,1)S(1)}, bf16[256,512]{1,0:T(8,128)(2,1)S(1)}, bf16[256,512]{1,0:T(8,128)(2,1)S(1)}) custom-call(s32[3]{0:T(128)S(1)} %pad_add_fusion.refs_0_, s32[1]{0:T(128)} %bitcast.3.refs_1_, bf16[2048,512]{1,0:T(8,128)(2,1)} %refs_2_.11, ...), custom_call_target="tpu_custom_call" | custom-call | tf_op jit(solution)/shard_map/pallas_call | solution.py:124
  53.2 1.5 %collective-permute-done.14.refs_1_ = bf16[256,512]{1,0:T(8,128)(2,1)S(1)} collective-permute-done((bf16[256,512]{1,0:T(8,128)(2,1)S(1)}, bf16[256,512]{1,0:T(8,128)(2,1)S(1)}, u32[]{:S(2)}, u32[]{:S(2)}) %collective-permute-start.14) | collective-permute-done | bytes 262176 | tf_op jit(solution)/shard_map/ppermute | solution.py:642
  54.8 2.8 %collective-permute-start.19 = (bf16[256,512]{1,0:T(8,128)(2,1)S(1)}, bf16[256,512]{1,0:T(8,128)(2,1)S(1)}, u32[]{:S(2)}, u32[]{:S(2)}) collective-permute-start(bf16[256,512]{1,0:T(8,128)(2,1)S(1)} %get-tuple-element.65), channel_id=1, source_target_pairs={{0,8},{2,10},{4,12},{6,14},{9,1},{11,3},{13,5},{15,7},{16,24},{18,... | collective-permute-start | bytes 786440 | tf_op jit(solution)/shard_map/ppermute | solution.py:550
  57.7 1.3 %collective-permute-done.13.refs_3_.refs_7_.refs_9_.refs_6_ = bf16[528,128]{1,0:T(8,128)(2,1)S(1)} collective-permute-done((bf16[528,128]{1,0:T(8,128)(2,1)S(1)}, bf16[528,128]{1,0:T(8,128)(2,1)S(1)}, u32[]{:S(2)}, u32[]{:S(2)}) %collective-permute-start.13) | collective-permute-done | bytes 135200 | tf_op jit(solution)/shard_map/ppermute | solution.py:560
  59.7 2.4 %collective-permute-start.16 = (bf16[272,128]{1,0:T(8,128)(2,1)S(1)}, bf16[272,128]{1,0:T(8,128)(2,1)S(1)}, u32[]{:S(2)}, u32[]{:S(2)}) collective-permute-start(bf16[272,128]{1,0:T(8,128)(2,1)S(1)} %shard_map.111.refs_3_), channel_id=1, source_target_pairs={{0,16},{4,20},{8,24},{12,28},{16,0},{20,4},{24,8},{28,12},{1,17},{... | collective-permute-start | bytes 208904 | tf_op jit(solution)/shard_map/ppermute | solution.py:573
  62.1 2.8 %collective-permute-start.17 = (bf16[272,128]{1,0:T(8,128)(2,1)S(1)}, bf16[272,128]{1,0:T(8,128)(2,1)S(1)}, u32[]{:S(2)}, u32[]{:S(2)}) collective-permute-start(bf16[272,128]{1,0:T(8,128)(2,1)S(1)} %shard_map.111.refs_3_), channel_id=1, source_target_pairs={{0,24},{4,28},{8,0},{12,4},{16,8},{20,12},{24,16},{28,20},{1,25},{... | collective-permute-start | bytes 208904 | tf_op jit(solution)/shard_map/ppermute | solution.py:573
  64.9 0.7 shard_map.112
  65.6 2.5 %collective-permute-start.21 = (bf16[256,512]{1,0:T(8,128)(2,1)S(1)}, bf16[256,512]{1,0:T(8,128)(2,1)S(1)}, u32[]{:S(2)}, u32[]{:S(2)}) collective-permute-start(bf16[256,512]{1,0:T(8,128)(2,1)S(1)} %get-tuple-element.70), channel_id=1, source_target_pairs={{0,16},{2,18},{3,19},{4,20},{6,22},{7,23},{9,25},{10,26},{11,27},{... | collective-permute-start | bytes 786440 | tf_op jit(solution)/shard_map/ppermute | solution.py:550
  68.2 10.5 %shard_map.113 = (bf16[1024,512]{1,0:T(8,128)(2,1)}, bf16[1024,512]{1,0:T(8,128)(2,1)}, bf16[1024,512]{1,0:T(8,128)(2,1)}) custom-call(bf16[1024,512]{1,0:T(8,128)(2,1)} %refs_0_.5, bf16[1024,512]{1,0:T(8,128)(2,1)} %refs_1_.7, bf16[1024,512]{1,0:T(8,128)(2,1)} %refs_2_.13, bf16[1024,512]{1,0:T(8,128)(2,1)S(1)} %get-tuple-element.54.refs_2_.refs_7_.refs_5_.refs_3_, ...), custom_call_target="tpu_custom_call" | custom-call | tf_op jit(solution)/shard_map/pallas_call | solution.py:124
  78.7 1.2 %copy-done.1 = bf16[1024,512]{1,0:T(8,128)(2,1)S(1)} copy-done((bf16[1024,512]{1,0:T(8,128)(2,1)S(1)}, bf16[1024,512]{1,0:T(8,128)(2,1)}, u32[]{:S(2)}) %copy-start.1) | copy-done | bytes 1048600
  80.7 0.7 collective-permute-start.20
  81.4 1.2 %collective-permute-done.18.refs_5_ = bf16[256,128]{1,0:T(8,128)(2,1)S(1)} collective-permute-done((bf16[256,128]{1,0:T(8,128)(2,1)S(1)}, bf16[256,128]{1,0:T(8,128)(2,1)S(1)}, u32[]{:S(2)}, u32[]{:S(2)}) %collective-permute-start.18) | collective-permute-done | bytes 65568 | tf_op jit(solution)/shard_map/ppermute | solution.py:560
  82.7 5.0 %shard_map.116 = (bf16[1024,512]{1,0:T(8,128)(2,1)}, bf16[1024,512]{1,0:T(8,128)(2,1)}) custom-call(s32[3]{0:T(128)S(1)} %pad_add_fusion.refs_0_, bf16[1024,512]{1,0:T(8,128)(2,1)} %refs_1_.7, bf16[1024,512]{1,0:T(8,128)(2,1)} %refs_2_.13, f32[5,16,256]{2,1,0:T(8,128)S(1)} %get-tuple-element.38.refs_4_.refs_3_.refs_9_, ...), custom_call_target="tpu_custom_call" | custom-call | tf_op jit(solution)/shard_map/pallas_call | solution.py:124
  87.7 0.9 select_convert_fusion
  (39 shorter events, 6.0 us)
Async XLA Ops:
  0.6 28.4 %collective-permute-start.5 = (bf16[1024,512]{1,0:T(8,128)(2,1)}, bf16[1024,512]{1,0:T(8,128)(2,1)S(1)}, u32[]{:S(2)}, u32[]{:S(2)}) collective-permute-start(bf16[1024,512]{1,0:T(8,128)(2,1)} %refs_4_.1), channel_id=1, source_target_pairs={{0,1},{1,0},{2,3},{3,2},{4,5},{5,4},{6,7},{7,6},{8,9},{9,8},{10,11... | collective-permute-start | bytes 3145736 | tf_op jit(solution)/shard_map/ppermute | solution.py:604
  3.6 25.5 %collective-permute-start.6 = (bf16[1024,512]{1,0:T(8,128)(2,1)}, bf16[1024,512]{1,0:T(8,128)(2,1)}, u32[]{:S(2)}, u32[]{:S(2)}) collective-permute-start(bf16[1024,512]{1,0:T(8,128)(2,1)} %refs_4_.1), channel_id=1, source_target_pairs={{0,2},{1,3},{2,0},{3,1},{4,6},{5,7},{6,4},{7,5},{8,10},{9,11},{10,... | collective-permute-start | bytes 3145736 | tf_op jit(solution)/shard_map/ppermute | solution.py:604
  9.1 1.4 %collective-permute-start = (bf16[528,128]{1,0:T(8,128)(2,1)S(1)}, bf16[528,128]{1,0:T(8,128)(2,1)S(1)}, u32[]{:S(2)}, u32[]{:S(2)}) collective-permute-start(bf16[528,128]{1,0:T(8,128)(2,1)S(1)} %get-tuple-element.40.refs_2_), channel_id=1, source_target_pairs={{0,4},{4,0},{8,12},{12,8},{16,20},{20,16},{24,28},{28,24},{1,5},{5... | collective-permute-start | bytes 405512 | tf_op jit(solution)/shard_map/ppermute | solution.py:560
  11.2 11.7 %collective-permute-start.1 = (bf16[272,128]{1,0:T(8,128)(2,1)S(1)}, bf16[272,128]{1,0:T(8,128)(2,1)S(1)}, u32[]{:S(2)}, u32[]{:S(2)}) collective-permute-start(bf16[272,128]{1,0:T(8,128)(2,1)S(1)} %shard_map.102.refs_4_), channel_id=1, source_target_pairs={{0,8},{4,12},{8,16},{12,20},{16,24},{20,28},{24,0},{28,4},{1,9},{5... | collective-permute-start | bytes 208904 | tf_op jit(solution)/shard_map/ppermute | solution.py:573
  12.8 10.0 %collective-permute-start.2 = (bf16[272,128]{1,0:T(8,128)(2,1)S(1)}, bf16[272,128]{1,0:T(8,128)(2,1)S(1)}, u32[]{:S(2)}, u32[]{:S(2)}) collective-permute-start(bf16[272,128]{1,0:T(8,128)(2,1)S(1)} %shard_map.102.refs_4_), channel_id=1, source_target_pairs={{0,16},{4,20},{8,24},{12,28},{16,0},{20,4},{24,8},{28,12},{1,17},{... | collective-permute-start | bytes 208904 | tf_op jit(solution)/shard_map/ppermute | solution.py:573
  15.4 7.5 %collective-permute-start.3 = (bf16[272,128]{1,0:T(8,128)(2,1)S(1)}, bf16[272,128]{1,0:T(8,128)(2,1)S(1)}, u32[]{:S(2)}, u32[]{:S(2)}) collective-permute-start(bf16[272,128]{1,0:T(8,128)(2,1)S(1)} %shard_map.102.refs_4_), channel_id=1, source_target_pairs={{0,24},{4,28},{8,0},{12,4},{16,8},{20,12},{24,16},{28,20},{1,25},{... | collective-permute-start | bytes 208904 | tf_op jit(solution)/shard_map/ppermute | solution.py:573
  23.5 1.3 %collective-permute-start.4 = (bf16[256,128]{1,0:T(8,128)(2,1)S(1)}, bf16[256,128]{1,0:T(8,128)(2,1)S(1)}, u32[]{:S(2)}, u32[]{:S(2)}) collective-permute-start(bf16[256,128]{1,0:T(8,128)(2,1)S(1)} %shard_map.104.refs_4_), channel_id=1, source_target_pairs={{0,4},{4,0},{8,12},{12,8},{16,20},{20,16},{24,28},{28,24},{1,5},{5... | collective-permute-start | bytes 196616 | tf_op jit(solution)/shard_map/ppermute | solution.py:560
  29.1 1.0 %copy-start.3 = (bf16[1024,512]{1,0:T(8,128)(2,1)}, bf16[1024,512]{1,0:T(8,128)(2,1)S(1)}, u32[]{:S(2)}) copy-start(bf16[1024,512]{1,0:T(8,128)(2,1)S(1)} %collective-permute-done.5.refs_0_.refs_5_) | copy-start | bytes 3145732
  30.1 1.2 %copy-start = (bf16[1024,512]{1,0:T(8,128)(2,1)S(1)}, bf16[1024,512]{1,0:T(8,128)(2,1)}, u32[]{:S(2)}) copy-start(bf16[1024,512]{1,0:T(8,128)(2,1)} %get-tuple-element.33.refs_2_.refs_3_) | copy-start | bytes 3145732
  33.3 14.5 %collective-permute-start.7 = (bf16[1024,256]{1,0:T(8,128)(2,1)}, bf16[1024,256]{1,0:T(8,128)(2,1)}, u32[]{:S(2)}, u32[]{:S(2)}) collective-permute-start(bf16[1024,256]{1,0:T(8,128)(2,1)} %get-tuple-element.45.refs_7_), channel_id=1, source_target_pairs={{0,2},{1,3},{2,0},{3,1},{4,6},{5,7},{6,4},{7,5},{8,10},{9,11},{10,... | collective-permute-start | bytes 1572872 | tf_op jit(solution)/shard_map/ppermute | solution.py:604
  33.9 14.0 %collective-permute-start.8 = (bf16[1024,256]{1,0:T(8,128)(2,1)}, bf16[1024,256]{1,0:T(8,128)(2,1)}, u32[]{:S(2)}, u32[]{:S(2)}) collective-permute-start(bf16[1024,256]{1,0:T(8,128)(2,1)} %get-tuple-element.46), channel_id=1, source_target_pairs={{0,1},{1,0},{2,3},{3,2},{4,5},{5,4},{6,7},{7,6},{8,9},{9,8},{10,11... | collective-permute-start | bytes 1572872 | tf_op jit(solution)/shard_map/ppermute | solution.py:604
  34.6 1.0 %copy-start.2 = (bf16[1024,256]{1,0:T(8,128)(2,1)S(1)}, bf16[1024,256]{1,0:T(8,128)(2,1)}, u32[]{:S(2)}) copy-start(bf16[1024,256]{1,0:T(8,128)(2,1)} %get-tuple-element.45.refs_7_) | copy-start | bytes 1572868
  42.2 1.8 %collective-permute-start.10 = (bf16[256,512]{1,0:T(8,128)(2,1)}, bf16[256,512]{1,0:T(8,128)(2,1)S(1)}, u32[]{:S(2)}, u32[]{:S(2)}) collective-permute-start(bf16[256,512]{1,0:T(8,128)(2,1)} %get-tuple-element.51), channel_id=1, source_target_pairs={{0,4},{4,0},{8,12},{12,8},{16,20},{20,16},{24,28},{28,24},{1,5},{5... | collective-permute-start | bytes 786440 | tf_op jit(solution)/shard_map/ppermute | solution.py:642
  42.3 2.2 %collective-permute-start.11 = (bf16[256,512]{1,0:T(8,128)(2,1)}, bf16[256,512]{1,0:T(8,128)(2,1)}, u32[]{:S(2)}, u32[]{:S(2)}) collective-permute-start(bf16[256,512]{1,0:T(8,128)(2,1)} %get-tuple-element.52), channel_id=1, source_target_pairs={{0,4},{4,0},{8,12},{12,8},{16,20},{20,16},{24,28},{28,24},{1,5},{5... | collective-permute-start | bytes 786440 | tf_op jit(solution)/shard_map/ppermute | solution.py:642
  42.8 2.1 %collective-permute-start.9 = (bf16[256,512]{1,0:T(8,128)(2,1)}, bf16[256,512]{1,0:T(8,128)(2,1)}, u32[]{:S(2)}, u32[]{:S(2)}) collective-permute-start(bf16[256,512]{1,0:T(8,128)(2,1)} %get-tuple-element.50), channel_id=1, source_target_pairs={{0,4},{4,0},{8,12},{12,8},{16,20},{20,16},{24,28},{28,24},{1,5},{5... | collective-permute-start | bytes 786440 | tf_op jit(solution)/shard_map/ppermute | solution.py:642
  46.2 18.7 %collective-permute-start.12 = (bf16[2,256,512]{2,1,0:T(8,128)(2,1)S(1)}, bf16[2,256,512]{2,1,0:T(8,128)(2,1)S(1)}, u32[]{:S(2)}, u32[]{:S(2)}) collective-permute-start(bf16[2,256,512]{2,1,0:T(8,128)(2,1)S(1)} %get-tuple-element.55), channel_id=1, source_target_pairs={{0,8},{1,9},{2,10},{3,11},{4,12},{5,13},{6,14},{7,15},{8,0},{9,1},... | collective-permute-start | bytes 1572872 | tf_op jit(solution)/shard_map/ppermute | solution.py:550
  53.1 1.6 %collective-permute-start.14 = (bf16[256,512]{1,0:T(8,128)(2,1)S(1)}, bf16[256,512]{1,0:T(8,128)(2,1)S(1)}, u32[]{:S(2)}, u32[]{:S(2)}) collective-permute-start(bf16[256,512]{1,0:T(8,128)(2,1)S(1)} %get-tuple-element.59), channel_id=1, source_target_pairs={{0,4},{4,0},{8,12},{12,8},{16,20},{20,16},{24,28},{28,24},{1,5},{5... | collective-permute-start | bytes 786440 | tf_op jit(solution)/shard_map/ppermute | solution.py:642
  54.8 25.8 %collective-permute-start.19 = (bf16[256,512]{1,0:T(8,128)(2,1)S(1)}, bf16[256,512]{1,0:T(8,128)(2,1)S(1)}, u32[]{:S(2)}, u32[]{:S(2)}) collective-permute-start(bf16[256,512]{1,0:T(8,128)(2,1)S(1)} %get-tuple-element.65), channel_id=1, source_target_pairs={{0,8},{2,10},{4,12},{6,14},{9,1},{11,3},{13,5},{15,7},{16,24},{18,... | collective-permute-start | bytes 786440 | tf_op jit(solution)/shard_map/ppermute | solution.py:550
  57.6 1.4 %collective-permute-start.13 = (bf16[528,128]{1,0:T(8,128)(2,1)S(1)}, bf16[528,128]{1,0:T(8,128)(2,1)S(1)}, u32[]{:S(2)}, u32[]{:S(2)}) collective-permute-start(bf16[528,128]{1,0:T(8,128)(2,1)S(1)} %get-tuple-element.57.refs_2_), channel_id=1, source_target_pairs={{0,4},{4,0},{8,12},{12,8},{16,20},{20,16},{24,28},{28,24},{1,5},{5... | collective-permute-start | bytes 405512 | tf_op jit(solution)/shard_map/ppermute | solution.py:560
  59.7 19.0 %collective-permute-start.15 = (bf16[272,128]{1,0:T(8,128)(2,1)S(1)}, bf16[272,128]{1,0:T(8,128)(2,1)S(1)}, u32[]{:S(2)}, u32[]{:S(2)}) collective-permute-start(bf16[272,128]{1,0:T(8,128)(2,1)S(1)} %shard_map.111.refs_3_), channel_id=1, source_target_pairs={{0,8},{4,12},{8,16},{12,20},{16,24},{20,28},{24,0},{28,4},{1,9},{5... | collective-permute-start | bytes 208904 | tf_op jit(solution)/shard_map/ppermute | solution.py:573
  59.7 19.0 %collective-permute-start.16 = (bf16[272,128]{1,0:T(8,128)(2,1)S(1)}, bf16[272,128]{1,0:T(8,128)(2,1)S(1)}, u32[]{:S(2)}, u32[]{:S(2)}) collective-permute-start(bf16[272,128]{1,0:T(8,128)(2,1)S(1)} %shard_map.111.refs_3_), channel_id=1, source_target_pairs={{0,16},{4,20},{8,24},{12,28},{16,0},{20,4},{24,8},{28,12},{1,17},{... | collective-permute-start | bytes 208904 | tf_op jit(solution)/shard_map/ppermute | solution.py:573
  62.1 16.6 %collective-permute-start.17 = (bf16[272,128]{1,0:T(8,128)(2,1)S(1)}, bf16[272,128]{1,0:T(8,128)(2,1)S(1)}, u32[]{:S(2)}, u32[]{:S(2)}) collective-permute-start(bf16[272,128]{1,0:T(8,128)(2,1)S(1)} %shard_map.111.refs_3_), channel_id=1, source_target_pairs={{0,24},{4,28},{8,0},{12,4},{16,8},{20,12},{24,16},{28,20},{1,25},{... | collective-permute-start | bytes 208904 | tf_op jit(solution)/shard_map/ppermute | solution.py:573
  65.6 22.0 %collective-permute-start.21 = (bf16[256,512]{1,0:T(8,128)(2,1)S(1)}, bf16[256,512]{1,0:T(8,128)(2,1)S(1)}, u32[]{:S(2)}, u32[]{:S(2)}) collective-permute-start(bf16[256,512]{1,0:T(8,128)(2,1)S(1)} %get-tuple-element.70), channel_id=1, source_target_pairs={{0,16},{2,18},{3,19},{4,20},{6,22},{7,23},{9,25},{10,26},{11,27},{... | collective-permute-start | bytes 786440 | tf_op jit(solution)/shard_map/ppermute | solution.py:550
  78.7 1.2 %copy-start.1 = (bf16[1024,512]{1,0:T(8,128)(2,1)S(1)}, bf16[1024,512]{1,0:T(8,128)(2,1)}, u32[]{:S(2)}) copy-start(bf16[1024,512]{1,0:T(8,128)(2,1)} %get-tuple-element.34.refs_4_) | copy-start | bytes 3145732
  80.7 7.0 %collective-permute-start.20 = (bf16[256,512]{1,0:T(8,128)(2,1)S(1)}, bf16[256,512]{1,0:T(8,128)(2,1)S(1)}, u32[]{:S(2)}, u32[]{:S(2)}) collective-permute-start(bf16[256,512]{1,0:T(8,128)(2,1)S(1)} %get-tuple-element.69), channel_id=1, source_target_pairs={{1,17},{5,21},{8,24},{12,28},{19,3},{23,7},{26,10},{30,14}} | collective-permute-start | bytes 786440 | tf_op jit(solution)/shard_map/ppermute | solution.py:550
  81.4 1.3 %collective-permute-start.18 = (bf16[256,128]{1,0:T(8,128)(2,1)S(1)}, bf16[256,128]{1,0:T(8,128)(2,1)S(1)}, u32[]{:S(2)}, u32[]{:S(2)}) collective-permute-start(bf16[256,128]{1,0:T(8,128)(2,1)S(1)} %shard_map.114.refs_2_.refs_4_), channel_id=1, source_target_pairs={{0,4},{4,0},{8,12},{12,8},{16,20},{20,16},{24,28},{28,24},{1,5},{5... | collective-permute-start | bytes 196616 | tf_op jit(solution)/shard_map/ppermute | solution.py:560

commit v3 on v2

v3 whole, which is shorter than its diff:
```python
import functools

import jax
import jax.numpy as jnp
from jax import lax
from jax.experimental import pallas as pl
from jax.experimental.pallas import tpu as pltpu
from jax.sharding import PartitionSpec as P

HIGH = lax.Precision.HIGHEST
F32 = jnp.float32
BF16 = jnp.bfloat16
VMEM = pl.BlockSpec(memory_space=pltpu.VMEM)
ANY = pl.BlockSpec(memory_space=pl.ANY)
NN = (((1,), (0,)), ((), ()))
NT = (((1,), (1,)), ((), ()))
TN = (((0,), (0,)), ((), ()))


def mm(left, right, dims):
    return lax.dot_general(left, right, dims, preferred_element_type=F32)


class Fetch:
    def __init__(self, source, buffer, semaphores, axis=1):
        self.buffer, self.axis = buffer, axis
        self.count = semaphores.shape[0]
        self.step = buffer.shape[axis] // self.count
        at = [
            (slice(None),) * axis + (slice(i * self.step, (i + 1) * self.step),)
            for i in range(self.count)
        ]
        self.copies = [
            pltpu.make_async_copy(source.at[p], buffer.at[p], semaphores.at[i])
            for i, p in enumerate(at)
        ]
        self.waiting = set(range(self.count))

        self.shape = buffer.shape

    def __getitem__(self, index):
        span = index[self.axis] if isinstance(index, tuple) else slice(None)
        first, last = span.start or 0, span.stop or self.buffer.shape[self.axis]
        wanted = {i for i in self.waiting if first < (i + 1) * self.step and i * self.step < last}
        if wanted and 0 not in self.waiting or len(wanted) > 1:
            wanted = set(self.waiting)
        for i in sorted(wanted):
            self.copies[i].wait()
        self.waiting -= wanted
        return self.buffer[index]


def start_all(*fetches):
    for i in range(max(f.count for f in fetches)):
        for f in fetches:
            if i < f.count:
                f.copies[i].start()


class Store(Fetch):
    def __init__(self, target, buffer, semaphores, axis=1):
        self.buffer, self.axis = buffer, axis
        self.count = semaphores.shape[0]
        self.step = buffer.shape[axis] // self.count
        at = [
            (slice(None),) * axis + (slice(i * self.step, (i + 1) * self.step),)
            for i in range(self.count)
        ]
        self.copies = [
            pltpu.make_async_copy(buffer.at[p], target.at[p], semaphores.at[i])
            for i, p in enumerate(at)
        ]

        self.shape, self.ready, self.left = buffer.shape, [], set(range(self.count))

    def __setitem__(self, index, value):
        self.buffer[index] = value

    def send(self, i):
        self.ready.append(i)
        if len(self.ready) * 2 >= self.count:
            self.start(self.ready)
            self.ready = []

    def start(self, blocks):
        for i in blocks:
            self.copies[i].start()
            self.left.remove(i)

    def finish(self):
        self.start(sorted(self.left))
        for copy in self.copies:
            copy.wait()


GROUP = 4


def together(steps):
    steps = list(steps)
    for i in range(0, len(steps), GROUP):
        running = steps[i : i + GROUP]
        while running:
            running = [step for step in running if next(step, None) is not None]


def here():
    seq, head = lax.axis_index("seq"), lax.axis_index("head")
    return seq >> 1, seq & 1, (seq >> 1) ^ head, head


class Line:
    def __init__(self):
        self.last = None
        self.held = {}

    def call(self, body, outs, *args, scratch=(), place=False, fetch={}, store={}, raw=(), raw_out=(), loose=()):
        fetch = {i: f if isinstance(f, tuple) else (f, 1) for i, f in fetch.items()}
        store = {i: f if isinstance(f, tuple) else (f, 1) for i, f in store.items()}
        shapes = [
            (pltpu.HBM if i in store or i in raw_out else jax.ShapeDtypeStruct)(shape, dtype)
            for i, (shape, dtype) in enumerate(outs)
        ]
        seen = {id(a) for a in args}
        extra = [] if self.last is None else [self.last]
        extra += [a for a in self.held.values()]
        extra = [a for a in extra if id(a) not in seen]
        count, more, results = len(args), len(extra), len(outs)
        hbm = pl.BlockSpec(memory_space=pltpu.HBM)
        specs = [ANY if i in loose else hbm if i in fetch else hbm if i in raw else VMEM for i in range(count)]
        buffers = []
        for i, (blocks, _) in fetch.items():
            buffers += [pltpu.VMEM(args[i].shape, args[i].dtype), pltpu.SemaphoreType.DMA((blocks,))]
        for i, (blocks, _) in store.items():
            buffers += [pltpu.VMEM(*outs[i]), pltpu.SemaphoreType.DMA((blocks,))]

        def kernel(*refs):
            ins, out = list(refs[:count]), list(refs[count + more : count + more + results])
            rest = list(refs[count + more + results :])
            for i, (_, axis) in fetch.items():
                ins[i] = Fetch(ins[i], rest.pop(0), rest.pop(0), axis)
            for i, (_, axis) in store.items():
                out[i] = Store(out[i], rest.pop(0), rest.pop(0), axis)
            if fetch:
                start_all(*[ins[i] for i in fetch])
            if place:
                ins = [here()] + ins
            body(*ins, *out, *rest)
            for i in store:
                out[i].finish()

        args = [
            pltpu.with_memory_space_constraint(a, pltpu.HBM) if (i in fetch or i in raw) and i not in loose else a
            for i, a in enumerate(args)
        ]
        values = pl.pallas_call(
            kernel,
            out_shape=shapes,
            in_specs=specs + [ANY] * more,
            out_specs=[hbm if i in store or i in raw_out else VMEM for i in range(results)],
            scratch_shapes=buffers + list(scratch),
            compiler_params=pltpu.CompilerParams(vmem_limit_bytes=24 * 1024 * 1024),
        )(*args, *extra)
        least = min(range(results), key=lambda i: values[i].size * values[i].dtype.itemsize)
        self.last = values[least]
        if least in store or least in raw_out:
            self.last = pltpu.with_memory_space_constraint(self.last, pltpu.HBM)
        return values


def foot_rows(heads):
    return -(-3 * heads // 16) * 16


def put_foot(out, base, totals):
    rows = []
    for total in totals:
        for _ in range(3):
            part = total.astype(BF16)
            rows.append(part.astype(F32))
            total = total - part.astype(F32)
    width = rows[0].shape[1]
    fill = foot_rows(len(totals)) - len(rows)
    if fill:
        rows.append(jnp.zeros((fill, width), F32))
    out[base:, :] = jnp.concatenate(rows, axis=0).astype(BF16)


def get_foot(message, base, heads):
    foot = message[base:, :].astype(F32)
    return [
        foot[3 * h : 3 * h + 1, :] + foot[3 * h + 1 : 3 * h + 2, :] + foot[3 * h + 2 : 3 * h + 3, :]
        for h in range(heads)
    ]


RUN, GROW, TAIL, GROW_BLOCK, TAIL_BLOCK = range(5)


def state_body(keys, values, log_decay, tables, update, packed, states):
    heads, size = log_decay.buffer.shape[0], tables.shape[2]
    chunks = tables.shape[1] // heads
    width = update.shape[1]
    upper = (
        lax.broadcasted_iota(jnp.int32, (size, size), 0)
        <= lax.broadcasted_iota(jnp.int32, (size, size), 1)
    ).astype(F32)
    pieces = jnp.concatenate(
        [log_decay[:, j * size : (j + 1) * size] for j in range(chunks)], axis=0
    )
    run = lax.dot_general(pieces, upper, NN, precision=HIGH, preferred_element_type=F32)
    ends = [run[j * heads : (j + 1) * heads, size - 1 : size] for j in range(chunks)]
    before, after = [jnp.zeros((heads, 1), F32)], [jnp.zeros((heads, 1), F32)]
    for j in range(chunks - 1):
        before.append(before[-1] + ends[j])
        after.append(after[-1] + ends[chunks - 1 - j])
    before = jnp.concatenate(before, axis=0)
    after = jnp.concatenate(after[::-1], axis=0)
    left = run[:, size - 1 : size] - run
    tables[RUN] = run
    tables[GROW] = jnp.exp(run)
    tables[TAIL] = jnp.exp(left)
    tables[GROW_BLOCK] = jnp.exp(run + before)
    tables[TAIL_BLOCK] = jnp.exp(left + after)
    tail_columns = jnp.exp(left).T
    def product(h, j, terms):
        cols, rows = slice(h * width, (h + 1) * width), slice(j * size, (j + 1) * size)
        r = j * heads + h
        tail = (keys[rows, cols] * tail_columns[:, r : r + 1]).astype(BF16)
        value = values[rows, cols]
        yield True
        terms.append(mm(tail, value, TN))
        yield True

    for h in range(heads):
        cols = slice(h * width, (h + 1) * width)
        terms = []
        together(product(h, j, terms) for j in range(chunks))
        state = None
        for j in range(chunks):
            r = j * heads + h
            at = slice((h * chunks + j) * width, (h * chunks + j + 1) * width)
            states[at, :] = jnp.zeros((width, width), BF16) if j == 0 else state.astype(BF16)
            end = jnp.exp(run[r : r + 1, size - 1 : size])
            state = terms[j] if state is None else state * end + terms[j]
        states.send(h)
        update[cols, :] = state
        packed[cols, :] = state.astype(BF16)
    put_foot(packed, heads * width, block_totals(run, heads, width))


def block_totals(run, heads, width):
    chunks, size = run.shape[0] // heads, run.shape[1]
    ends = run[:, size - 1 : size]
    return [
        sum(
            jnp.broadcast_to(ends[j * heads + h : j * heads + h + 1, :], (1, width))
            for j in range(chunks)
        )
        for h in range(heads)
    ]


def combine_body(forward, heads, place, own, packed, other, out, whole):
    core = place[1]
    width = own.shape[1]
    rows = heads * width
    mine, theirs = get_foot(packed, rows, heads), get_foot(other, rows, heads)
    late = core == (1 if forward else 0)
    for h in range(heads):
        at = slice(h * width, (h + 1) * width)
        a, b = own[at, :], other[at, :].astype(F32)
        joined = jnp.where(late, a + jnp.exp(mine[h]) * b, b + jnp.exp(theirs[h]) * a)
        whole[at, :] = joined
    half = rows // 2
    out[:half, :] = whole[pl.ds(pl.multiple_of(core * half, half), half), :].astype(BF16)
    put_foot(out, half, [a + b for a, b in zip(mine, theirs)])


def join_body(forward, heads, chips, place, *refs):
    messages, out = refs[: chips - 1], refs[chips - 1]
    chip, core = place[0], place[1]
    half, width = out.shape
    feet = [get_foot(m, half, heads) for m in messages]
    spans = [jnp.zeros((1, width), F32)] * heads
    head_rows = half * 2 // heads
    groups = max(1, half // head_rows)
    total = [None] * groups
    for k in range(1, chips) if forward else range(chips - 1, 0, -1):
        used = (k <= chip) if forward else (k > chip)
        for g in range(groups):
            span = spans[0] if heads == 1 else jnp.where(core == 0, spans[g], spans[groups + g])
            factor = jnp.where(used, jnp.exp(span), 0.0)
            at = slice(g * half // groups, (g + 1) * half // groups)
            term = factor * messages[k - 1][at, :].astype(F32)
            total[g] = term if total[g] is None else total[g] + term
        spans = [span + foot for span, foot in zip(spans, feet[k - 1])]
    for g in range(groups):
        out[g * half // groups : (g + 1) * half // groups, :] = total[g].astype(BF16)


def enter(forward, heads, place, mine, theirs, other, out):
    core = place[1]
    half, width = mine.shape
    rows = 2 * half
    out[pl.ds(pl.multiple_of(core * half, half), half), :] = mine[...].astype(F32)
    out[pl.ds(pl.multiple_of((1 - core) * half, half), half), :] = theirs[...].astype(F32)
    totals = get_foot(other, rows, heads)
    late = core == (1 if forward else 0)
    for h in range(heads):
        at = slice(h * width, (h + 1) * width)
        now = out[at, :]
        moved = other[at, :].astype(F32) + jnp.exp(totals[h]) * now
        out[at, :] = jnp.where(late, moved, now)


def causal_mask(size):
    return lax.broadcasted_iota(jnp.int32, (size, size), 0) >= lax.broadcasted_iota(
        jnp.int32, (size, size), 1
    )


def decay_of(run, columns, r, causal):
    return jnp.exp(jnp.where(causal, columns[:, r : r + 1] - run[r : r + 1, :], -jnp.inf))


def local_body(queries, keys, values, tables, states, mixed, grown_rows):
    size = tables.shape[2]
    length, columns = mixed.shape
    chunks = length // size
    heads = tables.shape[1] // chunks
    width = columns // heads
    causal = causal_mask(size)
    run = tables[RUN]
    sums, grow = run.T, tables[GROW].T
    def step(h, j):
        cols, rows = slice(h * width, (h + 1) * width), slice(j * size, (j + 1) * size)
        r = j * heads + h
        query, key, value = queries[rows, cols], keys[rows, cols], values[rows, cols]
        scores = mm(query, key, NT)
        grown = (query * grow[:, r : r + 1]).astype(BF16)
        yield True
        weight = (scores * decay_of(run, sums, r, causal)).astype(BF16)
        turned = grown.T
        yield True
        out = mm(weight, value, NN)
        if j:
            at = slice((h * chunks + j) * width, (h * chunks + j + 1) * width)
            out = out + mm(grown, states[at, :], NN)
        yield True
        grown_rows[cols, rows] = turned
        mixed[rows, cols] = out
        yield True

    for h in range(heads):
        together(step(h, j) for j in range(chunks))
        grown_rows.send(h)


def norm_body(
    heads, place, mixed, queries, tables, mine, theirs, other, attended, inverse, incoming
):
    width = mine.shape[1]
    size = tables.shape[2]
    chunks = tables.shape[1] // heads
    enter(True, heads, place, mine, theirs, other, incoming)
    grow = tables[GROW_BLOCK].T
    ones = jnp.full((width, width), 1.0 / width, BF16)
    lane = lax.broadcasted_iota(jnp.int32, (size, width), 1)
    low = [incoming[h * width : (h + 1) * width, :].astype(BF16) for h in range(heads)]
    def step(j, h, scales):
        cols, rows = slice(h * width, (h + 1) * width), slice(j * size, (j + 1) * size)
        r = j * heads + h
        grown = (queries[rows, cols] * grow[:, r : r + 1]).astype(BF16)
        yield True
        total = mixed[rows, cols] + mm(grown, low[h], NN)
        square = (total * total).astype(BF16)
        yield True
        scale = lax.rsqrt(mm(square, ones, NN) + 1e-05)
        yield True
        scales[0] = jnp.where(lane == h, scale, scales[0])
        attended[rows, cols] = (total * scale).astype(BF16)
        yield True

    for j in range(chunks):
        scales = [jnp.zeros((size, width), F32)]
        together(step(j, h, scales) for h in range(heads))
        inverse[j * heads : (j + 1) * heads, :] = scales[0].T[:heads, :]
        attended.send(j)


def head_grad_body(size, weight, whole, out):
    for t in range(out.shape[0] // size):
        rows = slice(t * size, (t + 1) * size)
        out[rows, :] = mm(whole[rows, :], weight[...], NN)


def weight_copies(head, blocks, weight, rows_of_weight, semaphores):
    depth = rows_of_weight.shape[0] // len(blocks)
    return [
        pltpu.make_async_copy(
            weight.at[pl.ds(pl.multiple_of((head ^ k) * depth, depth), depth), :],
            rows_of_weight.at[i * depth : (i + 1) * depth, :],
            semaphores.at[i],
        )
        for i, k in enumerate(blocks)
    ]


def early_body(size, place, weight, attended, *refs):
    pieces, mine, theirs, out, rows_of_weight, semaphores = (
        refs[:3], refs[3], refs[4:7], refs[7], refs[8], refs[9]
    )
    _, core, _, head = place
    part = mine.shape[1]
    copies = weight_copies(head, (0, 1, 2), weight, rows_of_weight, semaphores)
    for copy in copies:
        copy.start()
    for i, piece in enumerate(pieces):
        product = mm(piece[...], attended[...], TN)
        low, high = product[:part, :].astype(BF16), product[part:, :].astype(BF16)
        mine[i] = jnp.where(core == 0, low, high)
        theirs[i][...] = jnp.where(core == 0, high, low)
    for copy in copies:
        copy.wait()
    for t in range(out.shape[0] // size):
        rows = slice(t * size, (t + 1) * size)
        out[rows, :] = sum(
            mm(piece[rows, :], rows_of_weight[2 * part * i : 2 * part * (i + 1), :], NN)
            for i, piece in enumerate(pieces)
        )


def late_body(heads, number, place, weight, attended, *refs):
    pieces = refs[:number]
    refs = refs[number:]
    partial, inverse, grown_rows, tables, mixed_grad, update, packed, exits = refs[:8]
    width = update.shape[1]
    size = tables.shape[2]
    chunks = tables.shape[1] // heads
    if number:
        mine, theirs, rows_of_weight, semaphores = refs[8:]
        _, core, _, head = place
        part = mine.shape[0]
        copy, = weight_copies(head, (3,), weight, rows_of_weight, semaphores)
        copy.start()
        low, high = [mm(p[...], attended[...], TN).astype(BF16) for p in pieces]
        mine[...] = jnp.where(core == 0, low, high)
        theirs[...] = jnp.where(core == 0, high, low)
        copy.wait()
    ones = jnp.full((width, width), 1.0 / width, BF16)
    states = [None] * heads
    run = tables[RUN]
    scales = inverse[...].T

    def step(j, h, total):
        cols, rows = slice(h * width, (h + 1) * width), slice(j * size, (j + 1) * size)
        r = j * heads + h
        grad = total[:, cols]
        unit = attended[rows, cols].astype(F32)
        both = (grad * unit).astype(BF16)
        yield True
        mean = mm(both, ones, NN)
        yield True
        grad = ((grad - unit * mean) * scales[:, r : r + 1]).astype(BF16)
        yield True
        term = mm(grown_rows[cols, rows], grad, NN)
        yield True
        mixed_grad[rows, cols] = grad
        at = slice((h * chunks + j) * width, (h * chunks + j + 1) * width)
        later = states[h]
        exits[at, :] = jnp.zeros((width, width), BF16) if later is None else later.astype(BF16)
        end = jnp.exp(run[r : r + 1, size - 1 : size])
        states[h] = term if later is None else term + later * end
        yield True

    for j in reversed(range(chunks)):
        rows = slice(j * size, (j + 1) * size)
        total = partial[rows, :]
        for i, piece in enumerate(pieces):
            total = total + mm(
                piece[rows, :], rows_of_weight[i * part : (i + 1) * part, :], NN
            )
        together(step(j, h, total) for h in range(heads))
    for h in range(heads):
        at = slice(h * width, (h + 1) * width)
        update[at, :] = states[h]
        packed[at, :] = states[h].astype(BF16)
    put_foot(packed, heads * width, block_totals(run, heads, width))


def back_body(
    heads, queries, keys, values, mixed_grad, tables, incoming, states, exits,
    query_grad, key_grad, value_grad,
):
    width = incoming.shape[1]
    size = tables.shape[2]
    chunks = tables.shape[1] // heads
    causal = lax.broadcasted_iota(jnp.int32, (size, size), 0) <= lax.broadcasted_iota(
        jnp.int32, (size, size), 1
    )
    below = causal_mask(size)
    run = tables[RUN]
    sums, grow, tails = run.T, tables[GROW].T, tables[TAIL].T

    def step(h, j, start):
        cols, rows = slice(h * width, (h + 1) * width), slice(j * size, (j + 1) * size)
        r = j * heads + h
        at = slice((h * chunks + j) * width, (h * chunks + j + 1) * width)
        grad, query = mixed_grad[rows, cols], queries[rows, cols]
        key, value = keys[rows, cols], values[rows, cols]
        weight, masked, turned = mm(key, query, NT), mm(value, grad, NT), mm(grad, value, NT)
        yield True
        decay = jnp.exp(
            jnp.where(causal, run[r : r + 1, :] - sums[:, r : r + 1], -jnp.inf)
        )
        weight, masked = (weight * decay).astype(BF16), (masked * decay).astype(BF16)
        yield True
        decay = jnp.exp(jnp.where(below, sums[:, r : r + 1] - run[r : r + 1, :], -jnp.inf))
        turned = (turned * decay).astype(BF16)
        grown = (grad * grow[:, r : r + 1]).astype(BF16)
        state = ((states[at, :].astype(F32) + start) if j else start).astype(BF16)
        if j < chunks - 1:
            tail = tails[:, r : r + 1]
            value_tail, key_tail = (value * tail).astype(BF16), (key * tail).astype(BF16)
        yield True
        query_part = mm(turned, key, NN) + mm(grown, state, NT)
        key_part = mm(masked, query, NN)
        value_part = mm(weight, grad, NN)
        if j < chunks - 1:
            key_part = key_part + mm(value_tail, exits[at, :], NT)
            value_part = value_part + mm(key_tail, exits[at, :], NN)
        yield True
        query_grad[rows, cols] = query_part.astype(BF16)
        key_grad[rows, cols] = key_part.astype(BF16)
        value_grad[rows, cols] = value_part.astype(BF16)
        yield True

    for h in range(heads):
        starts = [incoming[h * width : (h + 1) * width, :]]
        for j in range(1, chunks):
            r = (j - 1) * heads + h
            starts.append(starts[-1] * grow[size - 1 : size, r : r + 1])
        together(step(h, j, starts[j]) for j in range(chunks))
        query_grad.send(h)
        key_grad.send(h)
        value_grad.send(h)


def final_body(
    heads, place, keys, values, tables, mine, theirs, other, key_part, value_part,
    key_grad, value_grad, outgoing,
):
    width = mine.shape[1]
    size = tables.shape[2]
    chunks = tables.shape[1] // heads
    enter(False, heads, place, mine, theirs, other, outgoing)
    tails = tables[TAIL_BLOCK].T
    def step(h, j, state):
        cols, rows = slice(h * width, (h + 1) * width), slice(j * size, (j + 1) * size)
        r = j * heads + h
        tail = tails[:, r : r + 1]
        value_tail = (values[rows, cols] * tail).astype(BF16)
        key_tail = (keys[rows, cols] * tail).astype(BF16)
        yield True
        key_sum, value_sum = mm(value_tail, state, NT), mm(key_tail, state, NN)
        yield True
        key_grad[rows, cols] = (key_part[rows, cols] + key_sum).astype(BF16)
        value_grad[rows, cols] = (value_part[rows, cols] + value_sum).astype(BF16)
        yield True

    for h in range(heads):
        state = outgoing[h * width : (h + 1) * width, :].astype(BF16)
        together(step(h, j, state) for j in range(chunks))
        key_grad.send(h)
        value_grad.send(h)


def fold_body(place, mine, low, middle, high, kept, sent):
    odd = place[2] % 2 == 1
    parts = [
        (mine[i].astype(F32) + part[...].astype(F32)).astype(BF16)
        for i, part in enumerate((low, middle, high))
    ]
    kept[0] = jnp.where(odd, parts[1], parts[0])
    kept[1] = parts[2]
    sent[0] = jnp.where(odd, parts[0], parts[1])
    sent[1] = parts[2]


def fold_again_body(place, kept, arrived, total, sent):
    turn = place[2]
    first = kept[0].astype(F32) + arrived[0].astype(F32)
    second = kept[1].astype(F32) + arrived[1].astype(F32)
    total[...] = jnp.where(turn == 2, second, first)
    sent[...] = jnp.where(turn == 0, second, first).astype(BF16)


def add_body(mine, arrived, out):
    out[...] = (mine[...].astype(F32) + arrived[...].astype(F32)).astype(BF16)


def cut_body(part, x, y, low, high, token, *rest):
    buffers, semaphores = rest[:2], rest[2]
    loads = [
        pltpu.make_async_copy(source, buffer, semaphores.at[i])
        for i, (source, buffer) in enumerate(
            ((x.at[:, :part], buffers[0]), (y.at[:, part:], buffers[1]))
        )
    ]
    stores = [
        pltpu.make_async_copy(buffer, target, semaphores.at[2 + i])
        for i, (buffer, target) in enumerate(((buffers[0], low), (buffers[1], high)))
    ]
    for load in loads:
        load.start()
    for load, store in zip(loads, stores):
        load.wait()
        store.start()
    token[...] = jnp.zeros(token.shape, F32)
    for store in stores:
        store.wait()


def hop(value, step, turns, chips, count):
    moves = [
        (s * count + y, ((s // 2 ^ step) * 2 + s % 2) * count + y)
        for s in range(2 * chips)
        for y in range(count)
        if s // 2 ^ y in turns
    ]
    return lax.ppermute(value, ("seq", "head"), moves)


class Chain:
    def __init__(self, line, forward, heads, chips, update, packed):
        self.line, self.forward, self.heads, self.chips = line, forward, heads, chips
        self.update, self.packed = update, packed
        self.other = self.swap(packed)

    def swap(self, value):
        return lax.ppermute(value, "seq", [(i, i ^ 1) for i in range(2 * self.chips)])

    def send(self):
        rows, width = self.update.shape
        self.half = (rows // 2, width)
        message, = self.line.call(
            functools.partial(combine_body, self.forward, self.heads),
            [((rows // 2 + foot_rows(self.heads), width), BF16)],
            self.update, self.packed, self.other,
            scratch=[pltpu.VMEM((rows, width), F32)], place=True,
        )
        self.line.held[self] = self.other
        self.arrived = [
            lax.ppermute(
                message, "seq",
                [(i, (i // 2 + k) % self.chips * 2 + i % 2) for i in range(2 * self.chips)],
            )
            for k in range(1, self.chips)
        ]

    def join(self):
        self.mine, = self.line.call(
            functools.partial(join_body, self.forward, self.heads, self.chips),
            [(self.half, BF16)], *self.arrived, place=True,
        )
        self.theirs = self.swap(self.mine)

    def done(self):
        self.line.held.pop(self)
        return self.mine, self.theirs, self.other


def on_device(seq_size, head_size, queries, keys, values, log_decay, out_weight, out_grad):
    length, columns = queries.shape
    heads = log_decay.shape[0]
    width = columns // heads
    size = 256 if length % 256 == 0 else length
    chunks = length // size
    chips = seq_size // 2
    near = head_size == 4 and chips == 4
    seq, head = lax.axis_index("seq"), lax.axis_index("head")
    turn = (seq // 2) ^ head
    block = out_grad.shape[1]
    part = block // 2
    move = lambda a, k: lax.ppermute(a, "head", [(i, i ^ k) for i in range(head_size)])
    if near:
        x, y = move(out_grad, 1), move(out_grad, 2)
    else:
        whole = lax.all_gather(out_grad, "head", axis=1, tiled=True)
    state = ((heads * width, width), F32)
    message = ((heads * width + foot_rows(heads), width), BF16)
    rows = (length, columns)
    line = Line()
    held = line.held

    chunk_states = ((heads * chunks * width, width), BF16)
    tables, update, packed, states = line.call(
        state_body, [((5, chunks * heads, size), F32), state, message, chunk_states],
        keys, values, log_decay, fetch={2: 1, 0: heads, 1: heads}, store={3: (heads, 0)},
    )
    forward = Chain(line, True, heads, chips, update, packed)
    pass
    forward.send()
    mixed, grown_rows = line.call(
        local_body, [(rows, F32), ((columns, length), BF16)], queries, keys, values, tables, states,
        fetch={0: heads, 1: heads, 2: heads, 4: (heads, 0)}, store={1: (heads, 0)},
    )
    held.update(mixed=mixed)
    forward.join()
    entering = forward.done()
    held.pop("mixed")
    attended, inverse, incoming = line.call(
        functools.partial(norm_body, heads),
        [(rows, BF16), ((chunks * heads, size), F32), state],
        mixed, queries, tables, *entering, place=True,
        fetch={1: (chunks, 0)}, store={0: (chunks, 0)},
    )
    held.update(inverse=inverse, incoming=incoming)
    swap = lambda a: lax.ppermute(a, "seq", [(i, i ^ 1) for i in range(2 * chips)])
    shape = (part, columns)
    if near:
        low, high, _ = line.call(
            functools.partial(cut_body, part),
            [((length, part), BF16)] * 2 + [((8, 128), F32)], x, y,
            scratch=[pltpu.VMEM((length, part), BF16)] * 2 + [pltpu.SemaphoreType.DMA((4,))],
            raw=(0, 1), raw_out=(0, 1), loose=(0, 1),
        )
        diagonal = [move(low, 2), move(high, 1)]
        products, *theirs, partial = line.call(
            functools.partial(early_body, size),
            [((3,) + shape, BF16)] + [(shape, BF16)] * 3 + [(rows, F32)],
            out_weight, attended, out_grad, x, y,
            scratch=[pltpu.VMEM((3 * block, columns), BF16), pltpu.SemaphoreType.DMA((3,))],
            place=True, raw=(0,), fetch={1: 1, 2: 1, 3: 1, 4: 1}, loose=(3, 4),
            store={0: (1, 0)},
        )
        arrived = [swap(a) for a in theirs]
        held["partial"] = partial
        kept, sent = line.call(
            fold_body, [((2,) + shape, BF16), ((2,) + shape, BF16)],
            products, *arrived, place=True, fetch={0: (1, 0), 1: (1, 0), 2: (1, 0), 3: (1, 0)},
            loose=(1, 2, 3), store={0: (1, 0), 1: (1, 0)},
        )
        arrived = hop(sent, 1, (0, 1, 2, 3), chips, head_size)
        held.pop("partial")
        mixed_grad, back_update, back_packed, exits, last, theirs = line.call(
            functools.partial(late_body, heads, 2),
            [(rows, BF16), state, message, chunk_states, (shape, BF16), (shape, BF16)],
            out_weight, attended, *diagonal, partial, inverse, grown_rows, tables,
            scratch=[pltpu.VMEM((block, columns), BF16), pltpu.SemaphoreType.DMA((1,))],
            place=True, raw=(0,), fetch={1: 1, 2: 1, 3: 1, 6: (1, 0)}, loose=(2, 3),
            store={3: (heads, 0)},
        )
        held["last"] = last
        last_arrived = swap(theirs)
    else:
        partial, = line.call(
            functools.partial(head_grad_body, size), [(rows, F32)],
            out_weight, whole,
        )
        mixed_grad, back_update, back_packed, exits = line.call(
            functools.partial(late_body, heads, 0), [(rows, BF16), state, message, chunk_states],
            out_weight, attended, partial, inverse, grown_rows, tables, place=True,
        )
    back = Chain(line, False, heads, chips, back_update, back_packed)
    held.pop("inverse")
    held["mixed_grad"] = mixed_grad
    held["update"] = back_update
    back.send()
    held.pop("update")
    if near:
        held.pop("last")
        last, = line.call(add_body, [(shape, BF16)], last, last_arrived)
        held["last"] = last
        last_arrived = hop(last, 1, (0, 2), chips, head_size)
        total, sent = line.call(
            fold_again_body, [(shape, F32), (shape, BF16)], kept, arrived, place=True,
            fetch={0: (1, 0), 1: (1, 0)}, loose=(1,),
        )
        arrived = hop(sent, 2, (0, 2, 3), chips, head_size)
    query_grad, key_part, value_part = line.call(
        functools.partial(back_body, heads), [(rows, BF16), (rows, BF16), (rows, BF16)],
        queries, keys, values, mixed_grad, tables, incoming, states, exits,
        fetch={0: heads, 1: heads, 2: heads, 6: (heads, 0), 7: (heads, 0)},
        store={i: heads for i in range(3)},
    )
    for name in ("mixed_grad", "incoming"):
        held.pop(name)
    back.join()
    if near:
        held.pop("last")
        last, = line.call(add_body, [(shape, BF16)], last, last_arrived)
        last_arrived = hop(last, 2, (1,), chips, head_size)
    key_grad, value_grad = line.call(
        functools.partial(final_body, heads), [(rows, BF16)] * 2,
        keys, values, tables, *back.done(), key_part, value_part,
        scratch=[pltpu.VMEM((heads * width, width), F32)], place=True,
        fetch={0: heads, 1: heads, 6: heads, 7: heads}, store={0: heads, 1: heads},
    )
    if near:
        weight_grad = jnp.where(
            turn == 3, last.astype(F32) + last_arrived.astype(F32),
            total + arrived.astype(F32),
        )
    else:
        weight_grad = lax.psum_scatter(
            mm(whole, attended, TN), "seq", scatter_dimension=0, tiled=True
        )
    return attended, query_grad, key_grad, value_grad, weight_grad.astype(BF16)


def solution(mesh):
    block = P("seq", "head")
    return jax.shard_map(
        functools.partial(on_device, mesh.shape["seq"], mesh.shape["head"]),
        mesh=mesh,
        in_specs=(block, block, block, P("head", "seq"), P(None, "head"), block),
        out_specs=(block,) * 5,
        check_vma=False,
    )
```

time: 89.7 us -> 81.2 us (0.905)
  Pallas kernels: 48.1 us -> 41.5 us
  local copies, waits for them, and re-layouts: 4.44 us -> 0 us
  starting transfers between devices: 25.3 us -> 26.8 us
    pallas_call x16, Pallas kernels: 48.1 us -> 41.5 us  [call(): pl.pallas_call(kernel, out_shape=shapes, in_specs=specs + [ANY] * more, o...]
    unnamed x8 -> x0, local copies, waits for them, and re-layouts: 4.44 us -> none
    ppermute x4, waiting for transfers between devices: 0.07 us -> 2.8 us  [on_device(): lax.ppermute(a, 'head', [(i, i ^ k) for i in range(head_size)])]
    ppermute x4, waiting for transfers between devices: 3.56 us -> 1.7 us  [on_device(): lax.ppermute(a, 'seq', [(i, i ^ 1) for i in range(2 * chips)])]
  transfers between devices with their start and end apart: 22 -> 22, of which waited for: 9 -> 9; matrix products, arithmetic and copies ran while one was open for 0% -> 0% of each run, Pallas kernels for 52% -> 51%
where the time goes in v3:
time: 81.2 us; the launch traced here: 79.7 us
  Pallas kernels  41.5 us (51%)
  starting transfers between devices  26.8 us (33%)
  waiting for transfers between devices  9.55 us (12%)
  between operations  0.92 us (1%)
  other arithmetic  0.85 us (1%)
    pallas_call x16, Pallas kernels, call(): pl.pallas_call(kernel, out_shape=shapes, in_specs=specs + [ANY] * more, o...  41.5 us
    ppermute x6, starting transfers between devices, send(): lax.ppermute(message, 'seq', [(i, (i // 2 + k) % self.chips * 2 + i % 2)...  11.1 us
    ppermute x4, starting transfers between devices, hop(): return lax.ppermute(value, ('seq', 'head'), moves)  7.66 us
    ppermute x4, starting transfers between devices, on_device(): lax.ppermute(a, 'head', [(i, i ^ k) for i in range(head_size)])  6.64 us
    ppermute x4, waiting for transfers between devices, swap(): lax.ppermute(value, 'seq', [(i, i ^ 1) for i in range(2 * self.chips)])  5.02 us
    ppermute x4, waiting for transfers between devices, on_device(): lax.ppermute(a, 'head', [(i, i ^ k) for i in range(head_size)])  2.8 us
    ppermute x4, waiting for transfers between devices, on_device(): lax.ppermute(a, 'seq', [(i, i ^ 1) for i in range(2 * chips)])  1.7 us
  transfers between devices with their start and end apart: 22, of which 9 were waited for; matrix products, arithmetic and copies ran while one was open for 0% of the time, Pallas kernels for 51%

profile of v3, /device:TPU:0, one launch (start us, length us, event | category | flops | bytes accessed | tf_op | source)
XLA Modules:
  0.0 79.7 jit_solution(13872642751571200296)
XLA Ops:
  0.6 3.0 %collective-permute-start.5 = (bf16[1024,512]{1,0:T(8,128)(2,1)}, bf16[1024,512]{1,0:T(8,128)(2,1)S(1)}, u32[]{:S(2)}, u32[]{:S(2)}) collective-permute-start(bf16[1024,512]{1,0:T(8,128)(2,1)} %refs_2_.6), channel_id=1, source_target_pairs={{0,1},{1,0},{2,3},{3,2},{4,5},{5,4},{6,7},{7,6},{8,9},{9,8},{10,11... | collective-permute-start | bytes 3145736 | tf_op jit(solution)/shard_map/ppermute | solution.py:686
  3.6 1.5 %collective-permute-start.6 = (bf16[1024,512]{1,0:T(8,128)(2,1)}, bf16[1024,512]{1,0:T(8,128)(2,1)S(1)}, u32[]{:S(2)}, u32[]{:S(2)}) collective-permute-start(bf16[1024,512]{1,0:T(8,128)(2,1)} %refs_2_.6), channel_id=1, source_target_pairs={{0,2},{1,3},{2,0},{3,1},{4,6},{5,7},{6,4},{7,5},{8,10},{9,11},{10,... | collective-permute-start | bytes 3145736 | tf_op jit(solution)/shard_map/ppermute | solution.py:686
  5.2 4.2 %shard_map.101 = (f32[5,16,256]{2,1,0:T(8,128)S(1)}, f32[512,128]{1,0:T(8,128)S(1)}, bf16[528,128]{1,0:T(8,128)(2,1)S(1)}, bf16[2048,128]{1,0:T(8,128)(2,1)}) custom-call(bf16[1024,512]{1,0:T(8,128)(2,1)} %refs_0_.11, bf16[1024,512]{1,0:T(8,128)(2,1)} %refs_1_.9, f32[4,1024]{1,0:T(4,128)} %refs_2_.4), custom_call_target="tpu_custom_call" | custom-call | tf_op jit(solution)/shard_map/pallas_call | solution.py:156
  9.4 1.3 %collective-permute-done.refs_2_.refs_6_.refs_4_.refs_5_ = bf16[528,128]{1,0:T(8,128)(2,1)S(1)} collective-permute-done((bf16[528,128]{1,0:T(8,128)(2,1)S(1)}, bf16[528,128]{1,0:T(8,128)(2,1)S(1)}, u32[]{:S(2)}, u32[]{:S(2)}) %collective-permute-start) | collective-permute-done | bytes 135200 | tf_op jit(solution)/shard_map/ppermute | solution.py:642
  10.9 1.6 %collective-permute-start.1 = (bf16[272,128]{1,0:T(8,128)(2,1)S(1)}, bf16[272,128]{1,0:T(8,128)(2,1)S(1)}, u32[]{:S(2)}, u32[]{:S(2)}) collective-permute-start(bf16[272,128]{1,0:T(8,128)(2,1)S(1)} %shard_map.102.refs_5_), channel_id=1, source_target_pairs={{0,8},{4,12},{8,16},{12,20},{16,24},{20,28},{24,0},{28,4},{1,9},{5... | collective-permute-start | bytes 208904 | tf_op jit(solution)/shard_map/ppermute | solution.py:655
  12.5 2.6 %collective-permute-start.2 = (bf16[272,128]{1,0:T(8,128)(2,1)S(1)}, bf16[272,128]{1,0:T(8,128)(2,1)S(1)}, u32[]{:S(2)}, u32[]{:S(2)}) collective-permute-start(bf16[272,128]{1,0:T(8,128)(2,1)S(1)} %shard_map.102.refs_5_), channel_id=1, source_target_pairs={{0,16},{4,20},{8,24},{12,28},{16,0},{20,4},{24,8},{28,12},{1,17},{... | collective-permute-start | bytes 208904 | tf_op jit(solution)/shard_map/ppermute | solution.py:655
  15.1 1.3 %collective-permute-start.3 = (bf16[272,128]{1,0:T(8,128)(2,1)S(1)}, bf16[272,128]{1,0:T(8,128)(2,1)S(1)}, u32[]{:S(2)}, u32[]{:S(2)}) collective-permute-start(bf16[272,128]{1,0:T(8,128)(2,1)S(1)} %shard_map.102.refs_5_), channel_id=1, source_target_pairs={{0,24},{4,28},{8,0},{12,4},{16,8},{20,12},{24,16},{28,20},{1,25},{... | collective-permute-start | bytes 208904 | tf_op jit(solution)/shard_map/ppermute | solution.py:655
  16.4 4.6 %shard_map.103 = (f32[1024,512]{1,0:T(8,128)S(1)}, bf16[512,1024]{1,0:T(8,128)(2,1)}) custom-call(bf16[1024,512]{1,0:T(8,128)(2,1)} %refs_0_.10, bf16[1024,512]{1,0:T(8,128)(2,1)} %refs_0_.11, bf16[1024,512]{1,0:T(8,128)(2,1)} %refs_1_.9, f32[5,16,256]{2,1,0:T(8,128)S(1)} %get-tuple-element.37.refs_3_.refs_2_.refs_7_.refs_4_, ...), custom_call_target="tpu_custom_call" | custom-call | tf_op jit(solution)/shard_map/pallas_call | solution.py:156
  21.2 1.2 %collective-permute-done.4.refs_4_ = bf16[256,128]{1,0:T(8,128)(2,1)S(1)} collective-permute-done((bf16[256,128]{1,0:T(8,128)(2,1)S(1)}, bf16[256,128]{1,0:T(8,128)(2,1)S(1)}, u32[]{:S(2)}, u32[]{:S(2)}) %collective-permute-start.4) | collective-permute-done | bytes 65568 | tf_op jit(solution)/shard_map/ppermute | solution.py:642
  22.4 3.2 %shard_map.105 = (bf16[1024,512]{1,0:T(8,128)(2,1)}, f32[16,256]{1,0:T(8,128)S(1)}, f32[512,128]{1,0:T(8,128)S(1)}) custom-call(f32[1024,512]{1,0:T(8,128)S(1)} %get-tuple-element.41.refs_5_.refs_0_, bf16[1024,512]{1,0:T(8,128)(2,1)} %refs_0_.10, f32[5,16,256]{2,1,0:T(8,128)S(1)} %get-tuple-element.37.refs_3_.refs_2_.refs_7_.refs_4_, ...), custom_call_target="tpu_custom_call" | custom-call | tf_op jit(solution)/shard_map/pallas_call | solution.py:156
  25.7 1.3 %collective-permute-done.5.refs_0_.refs_3_ = bf16[1024,512]{1,0:T(8,128)(2,1)S(1)} collective-permute-done((bf16[1024,512]{1,0:T(8,128)(2,1)}, bf16[1024,512]{1,0:T(8,128)(2,1)S(1)}, u32[]{:S(2)}, u32[]{:S(2)}) %collective-permute-start.5) | collective-permute-done | bytes 1048608 | tf_op jit(solution)/shard_map/ppermute | solution.py:686
  27.0 1.5 %collective-permute-done.6.refs_1_.refs_4_ = bf16[1024,512]{1,0:T(8,128)(2,1)S(1)} collective-permute-done((bf16[1024,512]{1,0:T(8,128)(2,1)}, bf16[1024,512]{1,0:T(8,128)(2,1)S(1)}, u32[]{:S(2)}, u32[]{:S(2)}) %collective-permute-start.6) | collective-permute-done | bytes 1048608 | tf_op jit(solution)/shard_map/ppermute | solution.py:686
  28.5 1.1 %shard_map.106 = (bf16[1024,256]{1,0:T(8,128)(2,1)}, bf16[1024,256]{1,0:T(8,128)(2,1)}, f32[8,128]{1,0:T(8,128)S(1)}) custom-call(bf16[1024,512]{1,0:T(8,128)(2,1)S(1)} %collective-permute-done.5.refs_0_.refs_3_, bf16[1024,512]{1,0:T(8,128)(2,1)S(1)} %collective-permute-done.6.refs_1_.refs_4_, ...), custom_call_target="tpu_custom_call" | custom-call | tf_op jit(solution)/shard_map/pallas_call | solution.py:156
  29.6 1.6 %collective-permute-start.7 = (bf16[1024,256]{1,0:T(8,128)(2,1)}, bf16[1024,256]{1,0:T(8,128)(2,1)S(1)}, u32[]{:S(2)}, u32[]{:S(2)}) collective-permute-start(bf16[1024,256]{1,0:T(8,128)(2,1)} %get-tuple-element.46), channel_id=1, source_target_pairs={{0,2},{1,3},{2,0},{3,1},{4,6},{5,7},{6,4},{7,5},{8,10},{9,11},{10,... | collective-permute-start | bytes 1572872 | tf_op jit(solution)/shard_map/ppermute | solution.py:686
  31.1 0.5 collective-permute-start.8
  31.7 5.7 %shard_map.107 = (bf16[3,256,512]{2,1,0:T(8,128)(2,1)}, bf16[256,512]{1,0:T(8,128)(2,1)S(1)}, bf16[256,512]{1,0:T(8,128)(2,1)S(1)}, bf16[256,512]{1,0:T(8,128)(2,1)S(1)}, f32[1024,512]{1,0:T(8,128)S(1)}) custom-call(bf16[2048,512]{1,0:T(8,128)(2,1)} %refs_0_.9, bf16[1024,512]{1,0:T(8,128)(2,1)} %get-tuple-element.32.refs_1_, bf16[1024,512]{1,0:T(8,128)(2,1)} %refs_2_.6, ...), custom_call_target="tpu_custom_call" | custom-call | tf_op jit(solution)/shard_map/pallas_call | solution.py:156
  38.0 0.9 %collective-permute-done.9.refs_1_ = bf16[256,512]{1,0:T(8,128)(2,1)S(1)} collective-permute-done((bf16[256,512]{1,0:T(8,128)(2,1)S(1)}, bf16[256,512]{1,0:T(8,128)(2,1)S(1)}, u32[]{:S(2)}, u32[]{:S(2)}) %collective-permute-start.9) | collective-permute-done | bytes 262176 | tf_op jit(solution)/shard_map/ppermute | solution.py:720
  39.7 3.1 %shard_map.108 = (bf16[2,256,512]{2,1,0:T(8,128)(2,1)}, bf16[2,256,512]{2,1,0:T(8,128)(2,1)}) custom-call(bf16[3,256,512]{2,1,0:T(8,128)(2,1)} %get-tuple-element.50.refs_0_, bf16[256,512]{1,0:T(8,128)(2,1)S(1)} %collective-permute-done.9.refs_1_, bf16[256,512]{1,0:T(8,128)(2,1)S(1)} %collective-permute-done.10.refs_2_, ...), custom_call_target="tpu_custom_call" | custom-call | tf_op jit(solution)/shard_map/pallas_call | solution.py:156
  42.9 1.6 %collective-permute-start.12 = (bf16[2,256,512]{2,1,0:T(8,128)(2,1)}, bf16[2,256,512]{2,1,0:T(8,128)(2,1)S(1)}, u32[]{:S(2)}, u32[]{:S(2)}) collective-permute-start(bf16[2,256,512]{2,1,0:T(8,128)(2,1)} %get-tuple-element.57), channel_id=1, source_target_pairs={{0,8},{1,9},{2,10},{3,11},{4,12},{5,13},{6,14},{7,15},{8,0},{9,1},... | collective-permute-start | bytes 1572872 | tf_op jit(solution)/shard_map/ppermute | solution.py:632
  44.5 5.1 %shard_map.109 = (bf16[1024,512]{1,0:T(8,128)(2,1)S(1)}, f32[512,128]{1,0:T(8,128)S(1)}, bf16[528,128]{1,0:T(8,128)(2,1)S(1)}, bf16[2048,128]{1,0:T(8,128)(2,1)}...) custom-call(bf16[2048,512]{1,0:T(8,128)(2,1)} %refs_0_.9, bf16[1024,512]{1,0:T(8,128)(2,1)} %get-tuple-element.32.refs_1_, ...), custom_call_target="tpu_custom_call" | custom-call | tf_op jit(solution)/shard_map/pallas_call | solution.py:156
  49.7 0.5 collective-permute-start.14
  50.2 1.2 %collective-permute-done.14.refs_2_.refs_5_.refs_9_.refs_4_.refs_3_ = bf16[528,128]{1,0:T(8,128)(2,1)S(1)} collective-permute-done((bf16[528,128]{1,0:T(8,128)(2,1)S(1)}, bf16[528,128]{1,0:T(8,128)(2,1)S(1)}, u32[]{:S(2)}, u32[]{:S(2)}) %collective-permute-start.14) | collective-permute-done | bytes 135200 | tf_op jit(solution)/shard_map/ppermute | solution.py:642
  51.6 2.5 %collective-permute-start.19 = (bf16[256,512]{1,0:T(8,128)(2,1)S(1)}, bf16[256,512]{1,0:T(8,128)(2,1)S(1)}, u32[]{:S(2)}, u32[]{:S(2)}) collective-permute-start(bf16[256,512]{1,0:T(8,128)(2,1)S(1)} %shard_map.111.refs_2_.refs_6_.refs_10_.refs_5_.refs_0_), channel_id=1, source_target_pairs={{0,8},{2,10},{4,12},{6,14},{9,1},{11,3},{13,5},{15,7},{16,24},{18,... | collective-permute-start | bytes 786440 | tf_op jit(solution)/shard_map/ppermute | solution.py:632
  54.2 2.6 %collective-permute-start.16 = (bf16[272,128]{1,0:T(8,128)(2,1)S(1)}, bf16[272,128]{1,0:T(8,128)(2,1)S(1)}, u32[]{:S(2)}, u32[]{:S(2)}) collective-permute-start(bf16[272,128]{1,0:T(8,128)(2,1)S(1)} %shard_map.110.refs_2_), channel_id=1, source_target_pairs={{0,16},{4,20},{8,24},{12,28},{16,0},{20,4},{24,8},{28,12},{1,17},{... | collective-permute-start | bytes 208904 | tf_op jit(solution)/shard_map/ppermute | solution.py:655
  56.8 2.8 %collective-permute-start.17 = (bf16[272,128]{1,0:T(8,128)(2,1)S(1)}, bf16[272,128]{1,0:T(8,128)(2,1)S(1)}, u32[]{:S(2)}, u32[]{:S(2)}) collective-permute-start(bf16[272,128]{1,0:T(8,128)(2,1)S(1)} %shard_map.110.refs_2_), channel_id=1, source_target_pairs={{0,24},{4,28},{8,0},{12,4},{16,8},{20,12},{24,16},{28,20},{1,25},{... | collective-permute-start | bytes 208904 | tf_op jit(solution)/shard_map/ppermute | solution.py:655
  59.7 1.2 %shard_map.112 = (f32[256,512]{1,0:T(8,128)S(1)}, bf16[256,512]{1,0:T(8,128)(2,1)S(1)}) custom-call(bf16[2,256,512]{2,1,0:T(8,128)(2,1)} %get-tuple-element.54.refs_8_.refs_0_, bf16[2,256,512]{2,1,0:T(8,128)(2,1)S(1)} %collective-permute-done.12.refs_1_, bf16[256,512]{1,0:T(8,128)(2,1)S(1)} %shard_map.111.refs_2_.refs_6_.refs_10_.refs_5_.refs_0_, ...), custom_call_target="tpu_custom_call" | custom-call | tf_op jit(solution)/shard_map/pallas_call | solution.py:156
  60.9 2.8 %collective-permute-start.21 = (bf16[256,512]{1,0:T(8,128)(2,1)S(1)}, bf16[256,512]{1,0:T(8,128)(2,1)S(1)}, u32[]{:S(2)}, u32[]{:S(2)}) collective-permute-start(bf16[256,512]{1,0:T(8,128)(2,1)S(1)} %get-tuple-element.62.refs_8_), channel_id=1, source_target_pairs={{0,16},{2,18},{3,19},{4,20},{6,22},{7,23},{9,25},{10,26},{11,27},{... | collective-permute-start | bytes 786440 | tf_op jit(solution)/shard_map/ppermute | solution.py:632
  63.7 8.3 %shard_map.113 = (bf16[1024,512]{1,0:T(8,128)(2,1)}, bf16[1024,512]{1,0:T(8,128)(2,1)}, bf16[1024,512]{1,0:T(8,128)(2,1)}) custom-call(bf16[1024,512]{1,0:T(8,128)(2,1)} %refs_0_.10, bf16[1024,512]{1,0:T(8,128)(2,1)} %refs_0_.11, bf16[1024,512]{1,0:T(8,128)(2,1)} %refs_1_.9, bf16[1024,512]{1,0:T(8,128)(2,1)S(1)} %get-tuple-element.55.refs_5_.refs_4_.refs_3_, ...), custom_call_target="tpu_custom_call" | custom-call | tf_op jit(solution)/shard_map/pallas_call | solution.py:156
  72.2 0.7 collective-permute-start.20
  73.0 1.2 %collective-permute-done.18.refs_4_ = bf16[256,128]{1,0:T(8,128)(2,1)S(1)} collective-permute-done((bf16[256,128]{1,0:T(8,128)(2,1)S(1)}, bf16[256,128]{1,0:T(8,128)(2,1)S(1)}, u32[]{:S(2)}, u32[]{:S(2)}) %collective-permute-start.18) | collective-permute-done | bytes 65568 | tf_op jit(solution)/shard_map/ppermute | solution.py:642
  74.2 4.6 %shard_map.116 = (bf16[1024,512]{1,0:T(8,128)(2,1)}, bf16[1024,512]{1,0:T(8,128)(2,1)}) custom-call(bf16[1024,512]{1,0:T(8,128)(2,1)} %refs_0_.11, bf16[1024,512]{1,0:T(8,128)(2,1)} %refs_1_.9, f32[5,16,256]{2,1,0:T(8,128)S(1)} %get-tuple-element.37.refs_3_.refs_2_.refs_7_.refs_4_, bf16[256,128]{1,0:T(8,128)(2,1)S(1)} %shard_map.114.refs_2_.refs_3_, ...), custom_call_target="tpu_custom_call" | custom-call | tf_op jit(solution)/shard_map/pallas_call | solution.py:156
  78.8 0.8 %select_convert_fusion = bf16[256,512]{1,0:T(8,128)(2,1)} fusion(f32[256,512]{1,0:T(8,128)S(1)} %get-tuple-element.68, bf16[256,512]{1,0:T(8,128)(2,1)S(1)} %collective-permute-done.21, bf16[256,512]{1,0:T(8,128)(2,1)S(1)} %collective-permute-done.20, bf16[256,512]{1,0:T(8,128)(2,1)S(1)} %shard_map.115.refs_8_, pred[]{:T(512)S(6)} %eq.3), kind=kLoop, calls=%fused_computation | loop fusion | flops 917504 | bytes 1572865 | tf_op jit(solution)/shard_map/convert_element_type | solution.py:810
  (29 shorter events, 2.2 us)
Async XLA Ops:
  0.6 26.4 %collective-permute-start.5 = (bf16[1024,512]{1,0:T(8,128)(2,1)}, bf16[1024,512]{1,0:T(8,128)(2,1)S(1)}, u32[]{:S(2)}, u32[]{:S(2)}) collective-permute-start(bf16[1024,512]{1,0:T(8,128)(2,1)} %refs_2_.6), channel_id=1, source_target_pairs={{0,1},{1,0},{2,3},{3,2},{4,5},{5,4},{6,7},{7,6},{8,9},{9,8},{10,11... | collective-permute-start | bytes 3145736 | tf_op jit(solution)/shard_map/ppermute | solution.py:686
  3.6 24.8 %collective-permute-start.6 = (bf16[1024,512]{1,0:T(8,128)(2,1)}, bf16[1024,512]{1,0:T(8,128)(2,1)S(1)}, u32[]{:S(2)}, u32[]{:S(2)}) collective-permute-start(bf16[1024,512]{1,0:T(8,128)(2,1)} %refs_2_.6), channel_id=1, source_target_pairs={{0,2},{1,3},{2,0},{3,1},{4,6},{5,7},{6,4},{7,5},{8,10},{9,11},{10,... | collective-permute-start | bytes 3145736 | tf_op jit(solution)/shard_map/ppermute | solution.py:686
  9.3 1.4 %collective-permute-start = (bf16[528,128]{1,0:T(8,128)(2,1)S(1)}, bf16[528,128]{1,0:T(8,128)(2,1)S(1)}, u32[]{:S(2)}, u32[]{:S(2)}) collective-permute-start(bf16[528,128]{1,0:T(8,128)(2,1)S(1)} %get-tuple-element.40.refs_1_), channel_id=1, source_target_pairs={{0,4},{4,0},{8,12},{12,8},{16,20},{20,16},{24,28},{28,24},{1,5},{5... | collective-permute-start | bytes 405512 | tf_op jit(solution)/shard_map/ppermute | solution.py:642
  10.9 10.1 %collective-permute-start.1 = (bf16[272,128]{1,0:T(8,128)(2,1)S(1)}, bf16[272,128]{1,0:T(8,128)(2,1)S(1)}, u32[]{:S(2)}, u32[]{:S(2)}) collective-permute-start(bf16[272,128]{1,0:T(8,128)(2,1)S(1)} %shard_map.102.refs_5_), channel_id=1, source_target_pairs={{0,8},{4,12},{8,16},{12,20},{16,24},{20,28},{24,0},{28,4},{1,9},{5... | collective-permute-start | bytes 208904 | tf_op jit(solution)/shard_map/ppermute | solution.py:655
  12.5 8.5 %collective-permute-start.2 = (bf16[272,128]{1,0:T(8,128)(2,1)S(1)}, bf16[272,128]{1,0:T(8,128)(2,1)S(1)}, u32[]{:S(2)}, u32[]{:S(2)}) collective-permute-start(bf16[272,128]{1,0:T(8,128)(2,1)S(1)} %shard_map.102.refs_5_), channel_id=1, source_target_pairs={{0,16},{4,20},{8,24},{12,28},{16,0},{20,4},{24,8},{28,12},{1,17},{... | collective-permute-start | bytes 208904 | tf_op jit(solution)/shard_map/ppermute | solution.py:655
  15.1 5.9 %collective-permute-start.3 = (bf16[272,128]{1,0:T(8,128)(2,1)S(1)}, bf16[272,128]{1,0:T(8,128)(2,1)S(1)}, u32[]{:S(2)}, u32[]{:S(2)}) collective-permute-start(bf16[272,128]{1,0:T(8,128)(2,1)S(1)} %shard_map.102.refs_5_), channel_id=1, source_target_pairs={{0,24},{4,28},{8,0},{12,4},{16,8},{20,12},{24,16},{28,20},{1,25},{... | collective-permute-start | bytes 208904 | tf_op jit(solution)/shard_map/ppermute | solution.py:655
  21.1 1.3 %collective-permute-start.4 = (bf16[256,128]{1,0:T(8,128)(2,1)S(1)}, bf16[256,128]{1,0:T(8,128)(2,1)S(1)}, u32[]{:S(2)}, u32[]{:S(2)}) collective-permute-start(bf16[256,128]{1,0:T(8,128)(2,1)S(1)} %shard_map.104.refs_3_), channel_id=1, source_target_pairs={{0,4},{4,0},{8,12},{12,8},{16,20},{20,16},{24,28},{28,24},{1,5},{5... | collective-permute-start | bytes 196616 | tf_op jit(solution)/shard_map/ppermute | solution.py:642
  29.6 15.0 %collective-permute-start.7 = (bf16[1024,256]{1,0:T(8,128)(2,1)}, bf16[1024,256]{1,0:T(8,128)(2,1)S(1)}, u32[]{:S(2)}, u32[]{:S(2)}) collective-permute-start(bf16[1024,256]{1,0:T(8,128)(2,1)} %get-tuple-element.46), channel_id=1, source_target_pairs={{0,2},{1,3},{2,0},{3,1},{4,6},{5,7},{6,4},{7,5},{8,10},{9,11},{10,... | collective-permute-start | bytes 1572872 | tf_op jit(solution)/shard_map/ppermute | solution.py:686
  31.1 13.4 %collective-permute-start.8 = (bf16[1024,256]{1,0:T(8,128)(2,1)}, bf16[1024,256]{1,0:T(8,128)(2,1)S(1)}, u32[]{:S(2)}, u32[]{:S(2)}) collective-permute-start(bf16[1024,256]{1,0:T(8,128)(2,1)} %get-tuple-element.47), channel_id=1, source_target_pairs={{0,1},{1,0},{2,3},{3,2},{4,5},{5,4},{6,7},{7,6},{8,9},{9,8},{10,11... | collective-permute-start | bytes 1572872 | tf_op jit(solution)/shard_map/ppermute | solution.py:686
  37.4 1.6 %collective-permute-start.9 = (bf16[256,512]{1,0:T(8,128)(2,1)S(1)}, bf16[256,512]{1,0:T(8,128)(2,1)S(1)}, u32[]{:S(2)}, u32[]{:S(2)}) collective-permute-start(bf16[256,512]{1,0:T(8,128)(2,1)S(1)} %get-tuple-element.51.refs_4_), channel_id=1, source_target_pairs={{0,4},{4,0},{8,12},{12,8},{16,20},{20,16},{24,28},{28,24},{1,5},{5... | collective-permute-start | bytes 786440 | tf_op jit(solution)/shard_map/ppermute | solution.py:720
  37.5 1.9 %collective-permute-start.10 = (bf16[256,512]{1,0:T(8,128)(2,1)S(1)}, bf16[256,512]{1,0:T(8,128)(2,1)S(1)}, u32[]{:S(2)}, u32[]{:S(2)}) collective-permute-start(bf16[256,512]{1,0:T(8,128)(2,1)S(1)} %get-tuple-element.52), channel_id=1, source_target_pairs={{0,4},{4,0},{8,12},{12,8},{16,20},{20,16},{24,28},{28,24},{1,5},{5... | collective-permute-start | bytes 786440 | tf_op jit(solution)/shard_map/ppermute | solution.py:720
  38.0 1.8 %collective-permute-start.11 = (bf16[256,512]{1,0:T(8,128)(2,1)S(1)}, bf16[256,512]{1,0:T(8,128)(2,1)S(1)}, u32[]{:S(2)}, u32[]{:S(2)}) collective-permute-start(bf16[256,512]{1,0:T(8,128)(2,1)S(1)} %get-tuple-element.53), channel_id=1, source_target_pairs={{0,4},{4,0},{8,12},{12,8},{16,20},{20,16},{24,28},{28,24},{1,5},{5... | collective-permute-start | bytes 786440 | tf_op jit(solution)/shard_map/ppermute | solution.py:720
  42.9 16.8 %collective-permute-start.12 = (bf16[2,256,512]{2,1,0:T(8,128)(2,1)}, bf16[2,256,512]{2,1,0:T(8,128)(2,1)S(1)}, u32[]{:S(2)}, u32[]{:S(2)}) collective-permute-start(bf16[2,256,512]{2,1,0:T(8,128)(2,1)} %get-tuple-element.57), channel_id=1, source_target_pairs={{0,8},{1,9},{2,10},{3,11},{4,12},{5,13},{6,14},{7,15},{8,0},{9,1},... | collective-permute-start | bytes 1572872 | tf_op jit(solution)/shard_map/ppermute | solution.py:632
  49.6 1.9 %collective-permute-start.13 = (bf16[256,512]{1,0:T(8,128)(2,1)S(1)}, bf16[256,512]{1,0:T(8,128)(2,1)S(1)}, u32[]{:S(2)}, u32[]{:S(2)}) collective-permute-start(bf16[256,512]{1,0:T(8,128)(2,1)S(1)} %get-tuple-element.59), channel_id=1, source_target_pairs={{0,4},{4,0},{8,12},{12,8},{16,20},{20,16},{24,28},{28,24},{1,5},{5... | collective-permute-start | bytes 786440 | tf_op jit(solution)/shard_map/ppermute | solution.py:720
  49.7 1.7 %collective-permute-start.14 = (bf16[528,128]{1,0:T(8,128)(2,1)S(1)}, bf16[528,128]{1,0:T(8,128)(2,1)S(1)}, u32[]{:S(2)}, u32[]{:S(2)}) collective-permute-start(bf16[528,128]{1,0:T(8,128)(2,1)S(1)} %get-tuple-element.61.refs_1_), channel_id=1, source_target_pairs={{0,4},{4,0},{8,12},{12,8},{16,20},{20,16},{24,28},{28,24},{1,5},{5... | collective-permute-start | bytes 405512 | tf_op jit(solution)/shard_map/ppermute | solution.py:642
  51.6 20.5 %collective-permute-start.19 = (bf16[256,512]{1,0:T(8,128)(2,1)S(1)}, bf16[256,512]{1,0:T(8,128)(2,1)S(1)}, u32[]{:S(2)}, u32[]{:S(2)}) collective-permute-start(bf16[256,512]{1,0:T(8,128)(2,1)S(1)} %shard_map.111.refs_2_.refs_6_.refs_10_.refs_5_.refs_0_), channel_id=1, source_target_pairs={{0,8},{2,10},{4,12},{6,14},{9,1},{11,3},{13,5},{15,7},{16,24},{18,... | collective-permute-start | bytes 786440 | tf_op jit(solution)/shard_map/ppermute | solution.py:632
  54.1 17.9 %collective-permute-start.15 = (bf16[272,128]{1,0:T(8,128)(2,1)S(1)}, bf16[272,128]{1,0:T(8,128)(2,1)S(1)}, u32[]{:S(2)}, u32[]{:S(2)}) collective-permute-start(bf16[272,128]{1,0:T(8,128)(2,1)S(1)} %shard_map.110.refs_2_), channel_id=1, source_target_pairs={{0,8},{4,12},{8,16},{12,20},{16,24},{20,28},{24,0},{28,4},{1,9},{5... | collective-permute-start | bytes 208904 | tf_op jit(solution)/shard_map/ppermute | solution.py:655
  54.2 17.9 %collective-permute-start.16 = (bf16[272,128]{1,0:T(8,128)(2,1)S(1)}, bf16[272,128]{1,0:T(8,128)(2,1)S(1)}, u32[]{:S(2)}, u32[]{:S(2)}) collective-permute-start(bf16[272,128]{1,0:T(8,128)(2,1)S(1)} %shard_map.110.refs_2_), channel_id=1, source_target_pairs={{0,16},{4,20},{8,24},{12,28},{16,0},{20,4},{24,8},{28,12},{1,17},{... | collective-permute-start | bytes 208904 | tf_op jit(solution)/shard_map/ppermute | solution.py:655
  56.8 15.2 %collective-permute-start.17 = (bf16[272,128]{1,0:T(8,128)(2,1)S(1)}, bf16[272,128]{1,0:T(8,128)(2,1)S(1)}, u32[]{:S(2)}, u32[]{:S(2)}) collective-permute-start(bf16[272,128]{1,0:T(8,128)(2,1)S(1)} %shard_map.110.refs_2_), channel_id=1, source_target_pairs={{0,24},{4,28},{8,0},{12,4},{16,8},{20,12},{24,16},{28,20},{1,25},{... | collective-permute-start | bytes 208904 | tf_op jit(solution)/shard_map/ppermute | solution.py:655
  60.9 17.9 %collective-permute-start.21 = (bf16[256,512]{1,0:T(8,128)(2,1)S(1)}, bf16[256,512]{1,0:T(8,128)(2,1)S(1)}, u32[]{:S(2)}, u32[]{:S(2)}) collective-permute-start(bf16[256,512]{1,0:T(8,128)(2,1)S(1)} %get-tuple-element.62.refs_8_), channel_id=1, source_target_pairs={{0,16},{2,18},{3,19},{4,20},{6,22},{7,23},{9,25},{10,26},{11,27},{... | collective-permute-start | bytes 786440 | tf_op jit(solution)/shard_map/ppermute | solution.py:632
  72.2 6.6 %collective-permute-start.20 = (bf16[256,512]{1,0:T(8,128)(2,1)S(1)}, bf16[256,512]{1,0:T(8,128)(2,1)S(1)}, u32[]{:S(2)}, u32[]{:S(2)}) collective-permute-start(bf16[256,512]{1,0:T(8,128)(2,1)S(1)} %shard_map.115.refs_8_), channel_id=1, source_target_pairs={{1,17},{5,21},{8,24},{12,28},{19,3},{23,7},{26,10},{30,14}} | collective-permute-start | bytes 786440 | tf_op jit(solution)/shard_map/ppermute | solution.py:632
  72.9 1.3 %collective-permute-start.18 = (bf16[256,128]{1,0:T(8,128)(2,1)S(1)}, bf16[256,128]{1,0:T(8,128)(2,1)S(1)}, u32[]{:S(2)}, u32[]{:S(2)}) collective-permute-start(bf16[256,128]{1,0:T(8,128)(2,1)S(1)} %shard_map.114.refs_2_.refs_3_), channel_id=1, source_target_pairs={{0,4},{4,0},{8,12},{12,8},{16,20},{20,16},{24,28},{28,24},{1,5},{5... | collective-permute-start | bytes 196616 | tf_op jit(solution)/shard_map/ppermute | solution.py:642

commit v4 on v3

--- a/solution.py
+++ b/solution.py
@@ -600,26 +600,9 @@
     out[...] = (mine[...].astype(F32) + arrived[...].astype(F32)).astype(BF16)
 
 
-def cut_body(part, x, y, low, high, token, *rest):
-    buffers, semaphores = rest[:2], rest[2]
-    loads = [
-        pltpu.make_async_copy(source, buffer, semaphores.at[i])
-        for i, (source, buffer) in enumerate(
-            ((x.at[:, :part], buffers[0]), (y.at[:, part:], buffers[1]))
-        )
-    ]
-    stores = [
-        pltpu.make_async_copy(buffer, target, semaphores.at[2 + i])
-        for i, (buffer, target) in enumerate(((buffers[0], low), (buffers[1], high)))
-    ]
-    for load in loads:
-        load.start()
-    for load, store in zip(loads, stores):
-        load.wait()
-        store.start()
+def cut_body(span, block, out, token):
+    out[...] = block[:, span]
     token[...] = jnp.zeros(token.shape, F32)
-    for store in stores:
-        store.wait()
 
 
 def hop(value, step, turns, chips, count):
@@ -720,27 +703,23 @@
     swap = lambda a: lax.ppermute(a, "seq", [(i, i ^ 1) for i in range(2 * chips)])
     shape = (part, columns)
     if near:
-        low, high, _ = line.call(
-            functools.partial(cut_body, part),
-            [((length, part), BF16)] * 2 + [((8, 128), F32)], x, y,
-            scratch=[pltpu.VMEM((length, part), BF16)] * 2 + [pltpu.SemaphoreType.DMA((4,))],
-            raw=(0, 1), raw_out=(0, 1), loose=(0, 1),
-        )
-        diagonal = [move(low, 2), move(high, 1)]
+        cut = [((length, part), BF16), ((8, 128), F32)]
+        low, _ = line.call(functools.partial(cut_body, slice(0, part)), cut, x)
+        diagonal = [move(low, 2)]
+        high, _ = line.call(functools.partial(cut_body, slice(part, block)), cut, y)
+        diagonal.append(move(high, 1))
         products, *theirs, partial = line.call(
             functools.partial(early_body, size),
             [((3,) + shape, BF16)] + [(shape, BF16)] * 3 + [(rows, F32)],
             out_weight, attended, out_grad, x, y,
             scratch=[pltpu.VMEM((3 * block, columns), BF16), pltpu.SemaphoreType.DMA((3,))],
             place=True, raw=(0,), fetch={1: 1, 2: 1, 3: 1, 4: 1}, loose=(3, 4),
-            store={0: (1, 0)},
         )
         arrived = [swap(a) for a in theirs]
         held["partial"] = partial
         kept, sent = line.call(
             fold_body, [((2,) + shape, BF16), ((2,) + shape, BF16)],
-            products, *arrived, place=True, fetch={0: (1, 0), 1: (1, 0), 2: (1, 0), 3: (1, 0)},
-            loose=(1, 2, 3), store={0: (1, 0), 1: (1, 0)},
+            products, *arrived, place=True,
         )
         arrived = hop(sent, 1, (0, 1, 2, 3), chips, head_size)
         held.pop("partial")

time: 81.2 us -> 78.1 us (0.962)
  Pallas kernels: 41.5 us -> 37.5 us
  starting transfers between devices: 26.8 us -> 28.7 us
    pallas_call x16 -> x17, Pallas kernels: 41.5 us -> 37.5 us  [call(): pl.pallas_call(kernel, out_shape=shapes, in_specs=specs + [ANY] * more, o...]
    ppermute x4, starting transfers between devices: 6.64 us -> 7.91 us  [on_device(): lax.ppermute(a, 'head', [(i, i ^ k) for i in range(head_size)])]
  transfers between devices with their start and end apart: 22 -> 22, of which waited for: 9 -> 9; matrix products, arithmetic and copies ran while one was open for 0% -> 0% of each run, Pallas kernels for 51% -> 49%
where the time goes in v4:
time: 78.1 us; the launch traced here: 77.3 us
  Pallas kernels  37.5 us (48%)
  starting transfers between devices  28.7 us (37%)
  waiting for transfers between devices  9.22 us (12%)
  between operations  0.93 us (1%)
  other arithmetic  0.85 us (1%)
    pallas_call x17, Pallas kernels, call(): pl.pallas_call(kernel, out_shape=shapes, in_specs=specs + [ANY] * more, o...  37.5 us
    ppermute x6, starting transfers between devices, send(): lax.ppermute(message, 'seq', [(i, (i // 2 + k) % self.chips * 2 + i % 2)...  11.1 us
    ppermute x4, starting transfers between devices, hop(): return lax.ppermute(value, ('seq', 'head'), moves)  8.23 us
    ppermute x4, starting transfers between devices, on_device(): lax.ppermute(a, 'head', [(i, i ^ k) for i in range(head_size)])  7.91 us
    ppermute x4, waiting for transfers between devices, swap(): lax.ppermute(value, 'seq', [(i, i ^ 1) for i in range(2 * self.chips)])  5.02 us
    ppermute x4, waiting for transfers between devices, on_device(): lax.ppermute(a, 'head', [(i, i ^ k) for i in range(head_size)])  2.47 us
    ppermute x4, waiting for transfers between devices, on_device(): lax.ppermute(a, 'seq', [(i, i ^ 1) for i in range(2 * chips)])  1.7 us
  transfers between devices with their start and end apart: 22, of which 9 were waited for; matrix products, arithmetic and copies ran while one was open for 0% of the time, Pallas kernels for 49%

profile of v4, /device:TPU:0, one launch (start us, length us, event | category | flops | bytes accessed | tf_op | source)
XLA Modules:
  0.0 77.3 jit_solution(2303302030550440981)
XLA Ops:
  0.6 3.0 %collective-permute-start.5 = (bf16[1024,512]{1,0:T(8,128)(2,1)}, bf16[1024,512]{1,0:T(8,128)(2,1)S(1)}, u32[]{:S(2)}, u32[]{:S(2)}) collective-permute-start(bf16[1024,512]{1,0:T(8,128)(2,1)} %refs_2_.6), channel_id=1, source_target_pairs={{0,1},{1,0},{2,3},{3,2},{4,5},{5,4},{6,7},{7,6},{8,9},{9,8},{10,11... | collective-permute-start | bytes 3145736 | tf_op jit(solution)/shard_map/ppermute | solution.py:669
  3.6 1.5 %collective-permute-start.7 = (bf16[1024,512]{1,0:T(8,128)(2,1)}, bf16[1024,512]{1,0:T(8,128)(2,1)S(1)}, u32[]{:S(2)}, u32[]{:S(2)}) collective-permute-start(bf16[1024,512]{1,0:T(8,128)(2,1)} %refs_2_.6), channel_id=1, source_target_pairs={{0,2},{1,3},{2,0},{3,1},{4,6},{5,7},{6,4},{7,5},{8,10},{9,11},{10,... | collective-permute-start | bytes 3145736 | tf_op jit(solution)/shard_map/ppermute | solution.py:669
  5.2 4.2 %shard_map.101 = (f32[5,16,256]{2,1,0:T(8,128)S(1)}, f32[512,128]{1,0:T(8,128)S(1)}, bf16[528,128]{1,0:T(8,128)(2,1)S(1)}, bf16[2048,128]{1,0:T(8,128)(2,1)}) custom-call(bf16[1024,512]{1,0:T(8,128)(2,1)} %refs_0_.11, bf16[1024,512]{1,0:T(8,128)(2,1)} %refs_1_.9, f32[4,1024]{1,0:T(4,128)} %refs_2_.4), custom_call_target="tpu_custom_call" | custom-call | tf_op jit(solution)/shard_map/pallas_call | solution.py:156
  9.4 1.3 %collective-permute-done.refs_2_.refs_6_.refs_4_.refs_5_ = bf16[528,128]{1,0:T(8,128)(2,1)S(1)} collective-permute-done((bf16[528,128]{1,0:T(8,128)(2,1)S(1)}, bf16[528,128]{1,0:T(8,128)(2,1)S(1)}, u32[]{:S(2)}, u32[]{:S(2)}) %collective-permute-start) | collective-permute-done | bytes 135200 | tf_op jit(solution)/shard_map/ppermute | solution.py:625
  10.8 1.6 %collective-permute-start.1 = (bf16[272,128]{1,0:T(8,128)(2,1)S(1)}, bf16[272,128]{1,0:T(8,128)(2,1)S(1)}, u32[]{:S(2)}, u32[]{:S(2)}) collective-permute-start(bf16[272,128]{1,0:T(8,128)(2,1)S(1)} %shard_map.102.refs_5_), channel_id=1, source_target_pairs={{0,8},{4,12},{8,16},{12,20},{16,24},{20,28},{24,0},{28,4},{1,9},{5... | collective-permute-start | bytes 208904 | tf_op jit(solution)/shard_map/ppermute | solution.py:638
  12.5 2.6 %collective-permute-start.2 = (bf16[272,128]{1,0:T(8,128)(2,1)S(1)}, bf16[272,128]{1,0:T(8,128)(2,1)S(1)}, u32[]{:S(2)}, u32[]{:S(2)}) collective-permute-start(bf16[272,128]{1,0:T(8,128)(2,1)S(1)} %shard_map.102.refs_5_), channel_id=1, source_target_pairs={{0,16},{4,20},{8,24},{12,28},{16,0},{20,4},{24,8},{28,12},{1,17},{... | collective-permute-start | bytes 208904 | tf_op jit(solution)/shard_map/ppermute | solution.py:638
  15.1 1.3 %collective-permute-start.3 = (bf16[272,128]{1,0:T(8,128)(2,1)S(1)}, bf16[272,128]{1,0:T(8,128)(2,1)S(1)}, u32[]{:S(2)}, u32[]{:S(2)}) collective-permute-start(bf16[272,128]{1,0:T(8,128)(2,1)S(1)} %shard_map.102.refs_5_), channel_id=1, source_target_pairs={{0,24},{4,28},{8,0},{12,4},{16,8},{20,12},{24,16},{28,20},{1,25},{... | collective-permute-start | bytes 208904 | tf_op jit(solution)/shard_map/ppermute | solution.py:638
  16.4 4.6 %shard_map.103 = (f32[1024,512]{1,0:T(8,128)S(1)}, bf16[512,1024]{1,0:T(8,128)(2,1)}) custom-call(bf16[1024,512]{1,0:T(8,128)(2,1)} %refs_0_.10, bf16[1024,512]{1,0:T(8,128)(2,1)} %refs_0_.11, bf16[1024,512]{1,0:T(8,128)(2,1)} %refs_1_.9, f32[5,16,256]{2,1,0:T(8,128)S(1)} %get-tuple-element.38.refs_3_.refs_2_.refs_7_.refs_4_, ...), custom_call_target="tpu_custom_call" | custom-call | tf_op jit(solution)/shard_map/pallas_call | solution.py:156
  21.1 1.2 %collective-permute-done.4.refs_4_ = bf16[256,128]{1,0:T(8,128)(2,1)S(1)} collective-permute-done((bf16[256,128]{1,0:T(8,128)(2,1)S(1)}, bf16[256,128]{1,0:T(8,128)(2,1)S(1)}, u32[]{:S(2)}, u32[]{:S(2)}) %collective-permute-start.4) | collective-permute-done | bytes 65568 | tf_op jit(solution)/shard_map/ppermute | solution.py:625
  22.4 3.2 %shard_map.105 = (bf16[1024,512]{1,0:T(8,128)(2,1)}, f32[16,256]{1,0:T(8,128)S(1)}, f32[512,128]{1,0:T(8,128)S(1)}) custom-call(f32[1024,512]{1,0:T(8,128)S(1)} %get-tuple-element.42.refs_5_.refs_0_, bf16[1024,512]{1,0:T(8,128)(2,1)} %refs_0_.10, f32[5,16,256]{2,1,0:T(8,128)S(1)} %get-tuple-element.38.refs_3_.refs_2_.refs_7_.refs_4_, ...), custom_call_target="tpu_custom_call" | custom-call | tf_op jit(solution)/shard_map/pallas_call | solution.py:156
  25.6 1.4 %collective-permute-done.5.refs_0_.refs_3_ = bf16[1024,512]{1,0:T(8,128)(2,1)S(1)} collective-permute-done((bf16[1024,512]{1,0:T(8,128)(2,1)}, bf16[1024,512]{1,0:T(8,128)(2,1)S(1)}, u32[]{:S(2)}, u32[]{:S(2)}) %collective-permute-start.5) | collective-permute-done | bytes 1048608 | tf_op jit(solution)/shard_map/ppermute | solution.py:669
  27.0 1.8 %collective-permute-start.6 = (bf16[1024,256]{1,0:T(8,128)(2,1)S(1)}, bf16[1024,256]{1,0:T(8,128)(2,1)S(1)}, u32[]{:S(2)}, u32[]{:S(2)}) collective-permute-start(bf16[1024,256]{1,0:T(8,128)(2,1)S(1)} %get-tuple-element.47), channel_id=1, source_target_pairs={{0,2},{1,3},{2,0},{3,1},{4,6},{5,7},{6,4},{7,5},{8,10},{9,11},{10,... | collective-permute-start | bytes 1572872 | tf_op jit(solution)/shard_map/ppermute | solution.py:669
  28.9 1.6 %collective-permute-start.8 = (bf16[1024,256]{1,0:T(8,128)(2,1)S(1)}, bf16[1024,256]{1,0:T(8,128)(2,1)S(1)}, u32[]{:S(2)}, u32[]{:S(2)}) collective-permute-start(bf16[1024,256]{1,0:T(8,128)(2,1)S(1)} %get-tuple-element.49), channel_id=1, source_target_pairs={{0,1},{1,0},{2,3},{3,2},{4,5},{5,4},{6,7},{7,6},{8,9},{9,8},{10,11... | collective-permute-start | bytes 1572872 | tf_op jit(solution)/shard_map/ppermute | solution.py:669
  30.5 5.7 %shard_map.108 = (bf16[3,256,512]{2,1,0:T(8,128)(2,1)S(1)}, bf16[256,512]{1,0:T(8,128)(2,1)S(1)}, bf16[256,512]{1,0:T(8,128)(2,1)S(1)}, bf16[256,512]{1,0:T(8,128)(2,1)S(1)}, f32[1024,512]{1,0:T(8,128)S(1)}) custom-call(bf16[2048,512]{1,0:T(8,128)(2,1)} %refs_0_.9, bf16[1024,512]{1,0:T(8,128)(2,1)} %get-tuple-element.33.refs_1_, bf16[1024,512]{1,0:T(8,128)(2,1)} %refs_2_.6, ...), custom_call_target="tpu_custom_call" | custom-call | tf_op jit(solution)/shard_map/pallas_call | solution.py:156
  36.2 0.5 collective-permute-start.10
  36.8 0.9 %collective-permute-done.9.refs_1_ = bf16[256,512]{1,0:T(8,128)(2,1)S(1)} collective-permute-done((bf16[256,512]{1,0:T(8,128)(2,1)S(1)}, bf16[256,512]{1,0:T(8,128)(2,1)S(1)}, u32[]{:S(2)}, u32[]{:S(2)}) %collective-permute-start.9) | collective-permute-done | bytes 262176 | tf_op jit(solution)/shard_map/ppermute | solution.py:703
  38.1 0.4 collective-permute-done.11.refs_3_
  38.8 1.6 %collective-permute-start.12 = (bf16[2,256,512]{2,1,0:T(8,128)(2,1)S(1)}, bf16[2,256,512]{2,1,0:T(8,128)(2,1)S(1)}, u32[]{:S(2)}, u32[]{:S(2)}) collective-permute-start(bf16[2,256,512]{2,1,0:T(8,128)(2,1)S(1)} %get-tuple-element.59), channel_id=1, source_target_pairs={{0,8},{1,9},{2,10},{3,11},{4,12},{5,13},{6,14},{7,15},{8,0},{9,1},... | collective-permute-start | bytes 1572872 | tf_op jit(solution)/shard_map/ppermute | solution.py:615
  40.4 1.1 %collective-permute-done.8.refs_3_ = bf16[1024,256]{1,0:T(8,128)(2,1)S(1)} collective-permute-done((bf16[1024,256]{1,0:T(8,128)(2,1)S(1)}, bf16[1024,256]{1,0:T(8,128)(2,1)S(1)}, u32[]{:S(2)}, u32[]{:S(2)}) %collective-permute-start.8) | collective-permute-done | bytes 524320 | tf_op jit(solution)/shard_map/ppermute | solution.py:669
  41.5 5.1 %shard_map.110 = (bf16[1024,512]{1,0:T(8,128)(2,1)S(1)}, f32[512,128]{1,0:T(8,128)S(1)}, bf16[528,128]{1,0:T(8,128)(2,1)S(1)}, bf16[2048,128]{1,0:T(8,128)(2,1)}...) custom-call(bf16[2048,512]{1,0:T(8,128)(2,1)} %refs_0_.9, bf16[1024,512]{1,0:T(8,128)(2,1)} %get-tuple-element.33.refs_1_, ...), custom_call_target="tpu_custom_call" | custom-call | tf_op jit(solution)/shard_map/pallas_call | solution.py:156
  46.7 0.5 collective-permute-start.14
  47.2 1.2 %collective-permute-done.14.refs_2_.refs_5_.refs_9_.refs_4_.refs_3_ = bf16[528,128]{1,0:T(8,128)(2,1)S(1)} collective-permute-done((bf16[528,128]{1,0:T(8,128)(2,1)S(1)}, bf16[528,128]{1,0:T(8,128)(2,1)S(1)}, u32[]{:S(2)}, u32[]{:S(2)}) %collective-permute-start.14) | collective-permute-done | bytes 135200 | tf_op jit(solution)/shard_map/ppermute | solution.py:625
  48.6 3.5 %collective-permute-start.19 = (bf16[256,512]{1,0:T(8,128)(2,1)S(1)}, bf16[256,512]{1,0:T(8,128)(2,1)S(1)}, u32[]{:S(2)}, u32[]{:S(2)}) collective-permute-start(bf16[256,512]{1,0:T(8,128)(2,1)S(1)} %shard_map.112.refs_2_.refs_6_.refs_10_.refs_5_.refs_0_), channel_id=1, source_target_pairs={{0,8},{2,10},{4,12},{6,14},{9,1},{11,3},{13,5},{15,7},{16,24},{18,... | collective-permute-start | bytes 786440 | tf_op jit(solution)/shard_map/ppermute | solution.py:615
  52.1 2.7 %collective-permute-start.16 = (bf16[272,128]{1,0:T(8,128)(2,1)S(1)}, bf16[272,128]{1,0:T(8,128)(2,1)S(1)}, u32[]{:S(2)}, u32[]{:S(2)}) collective-permute-start(bf16[272,128]{1,0:T(8,128)(2,1)S(1)} %shard_map.111.refs_2_), channel_id=1, source_target_pairs={{0,16},{4,20},{8,24},{12,28},{16,0},{20,4},{24,8},{28,12},{1,17},{... | collective-permute-start | bytes 208904 | tf_op jit(solution)/shard_map/ppermute | solution.py:638
  54.8 2.8 %collective-permute-start.17 = (bf16[272,128]{1,0:T(8,128)(2,1)S(1)}, bf16[272,128]{1,0:T(8,128)(2,1)S(1)}, u32[]{:S(2)}, u32[]{:S(2)}) collective-permute-start(bf16[272,128]{1,0:T(8,128)(2,1)S(1)} %shard_map.111.refs_2_), channel_id=1, source_target_pairs={{0,24},{4,28},{8,0},{12,4},{16,8},{20,12},{24,16},{28,20},{1,25},{... | collective-permute-start | bytes 208904 | tf_op jit(solution)/shard_map/ppermute | solution.py:638
  57.7 1.2 %shard_map.113 = (f32[256,512]{1,0:T(8,128)S(1)}, bf16[256,512]{1,0:T(8,128)(2,1)S(1)}) custom-call(bf16[2,256,512]{2,1,0:T(8,128)(2,1)} %copy-done, bf16[2,256,512]{2,1,0:T(8,128)(2,1)S(1)} %collective-permute-done.12.refs_1_, bf16[256,512]{1,0:T(8,128)(2,1)S(1)} %shard_map.112.refs_2_.refs_6_.refs_10_.refs_5_.refs_0_, ...), custom_call_target="tpu_custom_call" | custom-call | tf_op jit(solution)/shard_map/pallas_call | solution.py:156
  58.9 2.4 %collective-permute-start.21 = (bf16[256,512]{1,0:T(8,128)(2,1)S(1)}, bf16[256,512]{1,0:T(8,128)(2,1)S(1)}, u32[]{:S(2)}, u32[]{:S(2)}) collective-permute-start(bf16[256,512]{1,0:T(8,128)(2,1)S(1)} %get-tuple-element.64.refs_8_), channel_id=1, source_target_pairs={{0,16},{2,18},{3,19},{4,20},{6,22},{7,23},{9,25},{10,26},{11,27},{... | collective-permute-start | bytes 786440 | tf_op jit(solution)/shard_map/ppermute | solution.py:615
  61.3 8.3 %shard_map.114 = (bf16[1024,512]{1,0:T(8,128)(2,1)}, bf16[1024,512]{1,0:T(8,128)(2,1)}, bf16[1024,512]{1,0:T(8,128)(2,1)}) custom-call(bf16[1024,512]{1,0:T(8,128)(2,1)} %refs_0_.10, bf16[1024,512]{1,0:T(8,128)(2,1)} %refs_0_.11, bf16[1024,512]{1,0:T(8,128)(2,1)} %refs_1_.9, bf16[1024,512]{1,0:T(8,128)(2,1)S(1)} %get-tuple-element.57.refs_5_.refs_4_.refs_3_, ...), custom_call_target="tpu_custom_call" | custom-call | tf_op jit(solution)/shard_map/pallas_call | solution.py:156
  69.8 0.7 collective-permute-start.20
  70.6 1.2 %collective-permute-done.18.refs_4_ = bf16[256,128]{1,0:T(8,128)(2,1)S(1)} collective-permute-done((bf16[256,128]{1,0:T(8,128)(2,1)S(1)}, bf16[256,128]{1,0:T(8,128)(2,1)S(1)}, u32[]{:S(2)}, u32[]{:S(2)}) %collective-permute-start.18) | collective-permute-done | bytes 65568 | tf_op jit(solution)/shard_map/ppermute | solution.py:625
  71.8 4.6 %shard_map.117 = (bf16[1024,512]{1,0:T(8,128)(2,1)}, bf16[1024,512]{1,0:T(8,128)(2,1)}) custom-call(bf16[1024,512]{1,0:T(8,128)(2,1)} %refs_0_.11, bf16[1024,512]{1,0:T(8,128)(2,1)} %refs_1_.9, f32[5,16,256]{2,1,0:T(8,128)S(1)} %get-tuple-element.38.refs_3_.refs_2_.refs_7_.refs_4_, bf16[256,128]{1,0:T(8,128)(2,1)S(1)} %shard_map.115.refs_2_.refs_3_, ...), custom_call_target="tpu_custom_call" | custom-call | tf_op jit(solution)/shard_map/pallas_call | solution.py:156
  76.4 0.8 %select_convert_fusion = bf16[256,512]{1,0:T(8,128)(2,1)} fusion(f32[256,512]{1,0:T(8,128)S(1)} %get-tuple-element.70, bf16[256,512]{1,0:T(8,128)(2,1)S(1)} %collective-permute-done.21, bf16[256,512]{1,0:T(8,128)(2,1)S(1)} %collective-permute-done.20, bf16[256,512]{1,0:T(8,128)(2,1)S(1)} %shard_map.116.refs_8_, pred[]{:T(512)S(6)} %eq.3), kind=kLoop, calls=%fused_computation | loop fusion | flops 917504 | bytes 1572865 | tf_op jit(solution)/shard_map/convert_element_type | solution.py:789
  (32 shorter events, 1.6 us)
Async XLA Ops:
  0.6 26.4 %collective-permute-start.5 = (bf16[1024,512]{1,0:T(8,128)(2,1)}, bf16[1024,512]{1,0:T(8,128)(2,1)S(1)}, u32[]{:S(2)}, u32[]{:S(2)}) collective-permute-start(bf16[1024,512]{1,0:T(8,128)(2,1)} %refs_2_.6), channel_id=1, source_target_pairs={{0,1},{1,0},{2,3},{3,2},{4,5},{5,4},{6,7},{7,6},{8,9},{9,8},{10,11... | collective-permute-start | bytes 3145736 | tf_op jit(solution)/shard_map/ppermute | solution.py:669
  3.6 25.2 %collective-permute-start.7 = (bf16[1024,512]{1,0:T(8,128)(2,1)}, bf16[1024,512]{1,0:T(8,128)(2,1)S(1)}, u32[]{:S(2)}, u32[]{:S(2)}) collective-permute-start(bf16[1024,512]{1,0:T(8,128)(2,1)} %refs_2_.6), channel_id=1, source_target_pairs={{0,2},{1,3},{2,0},{3,1},{4,6},{5,7},{6,4},{7,5},{8,10},{9,11},{10,... | collective-permute-start | bytes 3145736 | tf_op jit(solution)/shard_map/ppermute | solution.py:669
  9.3 1.4 %collective-permute-start = (bf16[528,128]{1,0:T(8,128)(2,1)S(1)}, bf16[528,128]{1,0:T(8,128)(2,1)S(1)}, u32[]{:S(2)}, u32[]{:S(2)}) collective-permute-start(bf16[528,128]{1,0:T(8,128)(2,1)S(1)} %get-tuple-element.41.refs_1_), channel_id=1, source_target_pairs={{0,4},{4,0},{8,12},{12,8},{16,20},{20,16},{24,28},{28,24},{1,5},{5... | collective-permute-start | bytes 405512 | tf_op jit(solution)/shard_map/ppermute | solution.py:625
  10.8 10.1 %collective-permute-start.1 = (bf16[272,128]{1,0:T(8,128)(2,1)S(1)}, bf16[272,128]{1,0:T(8,128)(2,1)S(1)}, u32[]{:S(2)}, u32[]{:S(2)}) collective-permute-start(bf16[272,128]{1,0:T(8,128)(2,1)S(1)} %shard_map.102.refs_5_), channel_id=1, source_target_pairs={{0,8},{4,12},{8,16},{12,20},{16,24},{20,28},{24,0},{28,4},{1,9},{5... | collective-permute-start | bytes 208904 | tf_op jit(solution)/shard_map/ppermute | solution.py:638
  12.5 8.5 %collective-permute-start.2 = (bf16[272,128]{1,0:T(8,128)(2,1)S(1)}, bf16[272,128]{1,0:T(8,128)(2,1)S(1)}, u32[]{:S(2)}, u32[]{:S(2)}) collective-permute-start(bf16[272,128]{1,0:T(8,128)(2,1)S(1)} %shard_map.102.refs_5_), channel_id=1, source_target_pairs={{0,16},{4,20},{8,24},{12,28},{16,0},{20,4},{24,8},{28,12},{1,17},{... | collective-permute-start | bytes 208904 | tf_op jit(solution)/shard_map/ppermute | solution.py:638
  15.1 5.9 %collective-permute-start.3 = (bf16[272,128]{1,0:T(8,128)(2,1)S(1)}, bf16[272,128]{1,0:T(8,128)(2,1)S(1)}, u32[]{:S(2)}, u32[]{:S(2)}) collective-permute-start(bf16[272,128]{1,0:T(8,128)(2,1)S(1)} %shard_map.102.refs_5_), channel_id=1, source_target_pairs={{0,24},{4,28},{8,0},{12,4},{16,8},{20,12},{24,16},{28,20},{1,25},{... | collective-permute-start | bytes 208904 | tf_op jit(solution)/shard_map/ppermute | solution.py:638
  21.1 1.3 %collective-permute-start.4 = (bf16[256,128]{1,0:T(8,128)(2,1)S(1)}, bf16[256,128]{1,0:T(8,128)(2,1)S(1)}, u32[]{:S(2)}, u32[]{:S(2)}) collective-permute-start(bf16[256,128]{1,0:T(8,128)(2,1)S(1)} %shard_map.104.refs_3_), channel_id=1, source_target_pairs={{0,4},{4,0},{8,12},{12,8},{16,20},{20,16},{24,28},{28,24},{1,5},{5... | collective-permute-start | bytes 196616 | tf_op jit(solution)/shard_map/ppermute | solution.py:625
  27.0 13.3 %collective-permute-start.6 = (bf16[1024,256]{1,0:T(8,128)(2,1)S(1)}, bf16[1024,256]{1,0:T(8,128)(2,1)S(1)}, u32[]{:S(2)}, u32[]{:S(2)}) collective-permute-start(bf16[1024,256]{1,0:T(8,128)(2,1)S(1)} %get-tuple-element.47), channel_id=1, source_target_pairs={{0,2},{1,3},{2,0},{3,1},{4,6},{5,7},{6,4},{7,5},{8,10},{9,11},{10,... | collective-permute-start | bytes 1572872 | tf_op jit(solution)/shard_map/ppermute | solution.py:669
  28.9 12.6 %collective-permute-start.8 = (bf16[1024,256]{1,0:T(8,128)(2,1)S(1)}, bf16[1024,256]{1,0:T(8,128)(2,1)S(1)}, u32[]{:S(2)}, u32[]{:S(2)}) collective-permute-start(bf16[1024,256]{1,0:T(8,128)(2,1)S(1)} %get-tuple-element.49), channel_id=1, source_target_pairs={{0,1},{1,0},{2,3},{3,2},{4,5},{5,4},{6,7},{7,6},{8,9},{9,8},{10,11... | collective-permute-start | bytes 1572872 | tf_op jit(solution)/shard_map/ppermute | solution.py:669
  36.2 1.6 %collective-permute-start.9 = (bf16[256,512]{1,0:T(8,128)(2,1)S(1)}, bf16[256,512]{1,0:T(8,128)(2,1)S(1)}, u32[]{:S(2)}, u32[]{:S(2)}) collective-permute-start(bf16[256,512]{1,0:T(8,128)(2,1)S(1)} %get-tuple-element.53.refs_4_), channel_id=1, source_target_pairs={{0,4},{4,0},{8,12},{12,8},{16,20},{20,16},{24,28},{28,24},{1,5},{5... | collective-permute-start | bytes 786440 | tf_op jit(solution)/shard_map/ppermute | solution.py:703
  36.2 1.9 %collective-permute-start.10 = (bf16[256,512]{1,0:T(8,128)(2,1)S(1)}, bf16[256,512]{1,0:T(8,128)(2,1)S(1)}, u32[]{:S(2)}, u32[]{:S(2)}) collective-permute-start(bf16[256,512]{1,0:T(8,128)(2,1)S(1)} %get-tuple-element.54), channel_id=1, source_target_pairs={{0,4},{4,0},{8,12},{12,8},{16,20},{20,16},{24,28},{28,24},{1,5},{5... | collective-permute-start | bytes 786440 | tf_op jit(solution)/shard_map/ppermute | solution.py:703
  36.7 1.8 %collective-permute-start.11 = (bf16[256,512]{1,0:T(8,128)(2,1)S(1)}, bf16[256,512]{1,0:T(8,128)(2,1)S(1)}, u32[]{:S(2)}, u32[]{:S(2)}) collective-permute-start(bf16[256,512]{1,0:T(8,128)(2,1)S(1)} %get-tuple-element.55), channel_id=1, source_target_pairs={{0,4},{4,0},{8,12},{12,8},{16,20},{20,16},{24,28},{28,24},{1,5},{5... | collective-permute-start | bytes 786440 | tf_op jit(solution)/shard_map/ppermute | solution.py:703
  38.7 7.8 %copy-start = (bf16[2,256,512]{2,1,0:T(8,128)(2,1)}, bf16[2,256,512]{2,1,0:T(8,128)(2,1)S(1)}, u32[]{:S(2)}) copy-start(bf16[2,256,512]{2,1,0:T(8,128)(2,1)S(1)} %get-tuple-element.56.refs_8_.refs_0_) | copy-start | bytes 1572868
  38.8 18.9 %collective-permute-start.12 = (bf16[2,256,512]{2,1,0:T(8,128)(2,1)S(1)}, bf16[2,256,512]{2,1,0:T(8,128)(2,1)S(1)}, u32[]{:S(2)}, u32[]{:S(2)}) collective-permute-start(bf16[2,256,512]{2,1,0:T(8,128)(2,1)S(1)} %get-tuple-element.59), channel_id=1, source_target_pairs={{0,8},{1,9},{2,10},{3,11},{4,12},{5,13},{6,14},{7,15},{8,0},{9,1},... | collective-permute-start | bytes 1572872 | tf_op jit(solution)/shard_map/ppermute | solution.py:615
  46.6 1.9 %collective-permute-start.13 = (bf16[256,512]{1,0:T(8,128)(2,1)S(1)}, bf16[256,512]{1,0:T(8,128)(2,1)S(1)}, u32[]{:S(2)}, u32[]{:S(2)}) collective-permute-start(bf16[256,512]{1,0:T(8,128)(2,1)S(1)} %get-tuple-element.61), channel_id=1, source_target_pairs={{0,4},{4,0},{8,12},{12,8},{16,20},{20,16},{24,28},{28,24},{1,5},{5... | collective-permute-start | bytes 786440 | tf_op jit(solution)/shard_map/ppermute | solution.py:703
  46.7 1.7 %collective-permute-start.14 = (bf16[528,128]{1,0:T(8,128)(2,1)S(1)}, bf16[528,128]{1,0:T(8,128)(2,1)S(1)}, u32[]{:S(2)}, u32[]{:S(2)}) collective-permute-start(bf16[528,128]{1,0:T(8,128)(2,1)S(1)} %get-tuple-element.63.refs_1_), channel_id=1, source_target_pairs={{0,4},{4,0},{8,12},{12,8},{16,20},{20,16},{24,28},{28,24},{1,5},{5... | collective-permute-start | bytes 405512 | tf_op jit(solution)/shard_map/ppermute | solution.py:625
  48.6 21.1 %collective-permute-start.19 = (bf16[256,512]{1,0:T(8,128)(2,1)S(1)}, bf16[256,512]{1,0:T(8,128)(2,1)S(1)}, u32[]{:S(2)}, u32[]{:S(2)}) collective-permute-start(bf16[256,512]{1,0:T(8,128)(2,1)S(1)} %shard_map.112.refs_2_.refs_6_.refs_10_.refs_5_.refs_0_), channel_id=1, source_target_pairs={{0,8},{2,10},{4,12},{6,14},{9,1},{11,3},{13,5},{15,7},{16,24},{18,... | collective-permute-start | bytes 786440 | tf_op jit(solution)/shard_map/ppermute | solution.py:615
  52.1 17.5 %collective-permute-start.15 = (bf16[272,128]{1,0:T(8,128)(2,1)S(1)}, bf16[272,128]{1,0:T(8,128)(2,1)S(1)}, u32[]{:S(2)}, u32[]{:S(2)}) collective-permute-start(bf16[272,128]{1,0:T(8,128)(2,1)S(1)} %shard_map.111.refs_2_), channel_id=1, source_target_pairs={{0,8},{4,12},{8,16},{12,20},{16,24},{20,28},{24,0},{28,4},{1,9},{5... | collective-permute-start | bytes 208904 | tf_op jit(solution)/shard_map/ppermute | solution.py:638
  52.1 17.5 %collective-permute-start.16 = (bf16[272,128]{1,0:T(8,128)(2,1)S(1)}, bf16[272,128]{1,0:T(8,128)(2,1)S(1)}, u32[]{:S(2)}, u32[]{:S(2)}) collective-permute-start(bf16[272,128]{1,0:T(8,128)(2,1)S(1)} %shard_map.111.refs_2_), channel_id=1, source_target_pairs={{0,16},{4,20},{8,24},{12,28},{16,0},{20,4},{24,8},{28,12},{1,17},{... | collective-permute-start | bytes 208904 | tf_op jit(solution)/shard_map/ppermute | solution.py:638
  54.8 14.8 %collective-permute-start.17 = (bf16[272,128]{1,0:T(8,128)(2,1)S(1)}, bf16[272,128]{1,0:T(8,128)(2,1)S(1)}, u32[]{:S(2)}, u32[]{:S(2)}) collective-permute-start(bf16[272,128]{1,0:T(8,128)(2,1)S(1)} %shard_map.111.refs_2_), channel_id=1, source_target_pairs={{0,24},{4,28},{8,0},{12,4},{16,8},{20,12},{24,16},{28,20},{1,25},{... | collective-permute-start | bytes 208904 | tf_op jit(solution)/shard_map/ppermute | solution.py:638
  58.9 17.5 %collective-permute-start.21 = (bf16[256,512]{1,0:T(8,128)(2,1)S(1)}, bf16[256,512]{1,0:T(8,128)(2,1)S(1)}, u32[]{:S(2)}, u32[]{:S(2)}) collective-permute-start(bf16[256,512]{1,0:T(8,128)(2,1)S(1)} %get-tuple-element.64.refs_8_), channel_id=1, source_target_pairs={{0,16},{2,18},{3,19},{4,20},{6,22},{7,23},{9,25},{10,26},{11,27},{... | collective-permute-start | bytes 786440 | tf_op jit(solution)/shard_map/ppermute | solution.py:615
  69.8 6.6 %collective-permute-start.20 = (bf16[256,512]{1,0:T(8,128)(2,1)S(1)}, bf16[256,512]{1,0:T(8,128)(2,1)S(1)}, u32[]{:S(2)}, u32[]{:S(2)}) collective-permute-start(bf16[256,512]{1,0:T(8,128)(2,1)S(1)} %shard_map.116.refs_8_), channel_id=1, source_target_pairs={{1,17},{5,21},{8,24},{12,28},{19,3},{23,7},{26,10},{30,14}} | collective-permute-start | bytes 786440 | tf_op jit(solution)/shard_map/ppermute | solution.py:615
  70.5 1.3 %collective-permute-start.18 = (bf16[256,128]{1,0:T(8,128)(2,1)S(1)}, bf16[256,128]{1,0:T(8,128)(2,1)S(1)}, u32[]{:S(2)}, u32[]{:S(2)}) collective-permute-start(bf16[256,128]{1,0:T(8,128)(2,1)S(1)} %shard_map.115.refs_2_.refs_3_), channel_id=1, source_target_pairs={{0,4},{4,0},{8,12},{12,8},{16,20},{20,16},{24,28},{28,24},{1,5},{5... | collective-permute-start | bytes 196616 | tf_op jit(solution)/shard_map/ppermute | solution.py:625

commit v5 on v4

--- a/solution.py
+++ b/solution.py
@@ -755,7 +755,6 @@
         last_arrived = hop(last, 1, (0, 2), chips, head_size)
         total, sent = line.call(
             fold_again_body, [(shape, F32), (shape, BF16)], kept, arrived, place=True,
-            fetch={0: (1, 0), 1: (1, 0)}, loose=(1,),
         )
         arrived = hop(sent, 2, (0, 2, 3), chips, head_size)
     query_grad, key_part, value_part = line.call(

time: 78.1 us -> 77 us (0.986)
  Pallas kernels: 37.5 us -> 36.5 us
    pallas_call x17, Pallas kernels: 37.5 us -> 36.5 us  [call(): pl.pallas_call(kernel, out_shape=shapes, in_specs=specs + [ANY] * more, o...]
  transfers between devices with their start and end apart: 22 -> 22, of which waited for: 9 -> 9; matrix products, arithmetic and copies ran while one was open for 0% -> 0% of each run, Pallas kernels for 49% -> 48%
where the time goes in v5:
time: 77 us; the launch traced here: 76.2 us
  Pallas kernels  36.5 us (47%)
  starting transfers between devices  28.7 us (37%)
  waiting for transfers between devices  9.23 us (12%)
  between operations  0.91 us (1%)
  other arithmetic  0.85 us (1%)
    pallas_call x17, Pallas kernels, call(): pl.pallas_call(kernel, out_shape=shapes, in_specs=specs + [ANY] * more, o...  36.5 us
    ppermute x6, starting transfers between devices, send(): lax.ppermute(message, 'seq', [(i, (i // 2 + k) % self.chips * 2 + i % 2)...  11.1 us
    ppermute x4, starting transfers between devices, hop(): return lax.ppermute(value, ('seq', 'head'), moves)  8.23 us
    ppermute x4, starting transfers between devices, on_device(): lax.ppermute(a, 'head', [(i, i ^ k) for i in range(head_size)])  7.91 us
    ppermute x4, waiting for transfers between devices, swap(): lax.ppermute(value, 'seq', [(i, i ^ 1) for i in range(2 * self.chips)])  5.02 us
    ppermute x4, waiting for transfers between devices, on_device(): lax.ppermute(a, 'head', [(i, i ^ k) for i in range(head_size)])  2.49 us
    ppermute x4, waiting for transfers between devices, on_device(): lax.ppermute(a, 'seq', [(i, i ^ 1) for i in range(2 * chips)])  1.7 us
  transfers between devices with their start and end apart: 22, of which 9 were waited for; matrix products, arithmetic and copies ran while one was open for 0% of the time, Pallas kernels for 48%

profile of v5, /device:TPU:0, one launch (start us, length us, event | category | flops | bytes accessed | tf_op | source)
XLA Modules:
  0.0 76.2 jit_solution(7026193182054906252)
XLA Ops:
  0.6 3.0 %collective-permute-start.5 = (bf16[1024,512]{1,0:T(8,128)(2,1)}, bf16[1024,512]{1,0:T(8,128)(2,1)S(1)}, u32[]{:S(2)}, u32[]{:S(2)}) collective-permute-start(bf16[1024,512]{1,0:T(8,128)(2,1)} %refs_2_.6), channel_id=1, source_target_pairs={{0,1},{1,0},{2,3},{3,2},{4,5},{5,4},{6,7},{7,6},{8,9},{9,8},{10,11... | collective-permute-start | bytes 3145736 | tf_op jit(solution)/shard_map/ppermute | solution.py:669
  3.6 1.5 %collective-permute-start.7 = (bf16[1024,512]{1,0:T(8,128)(2,1)}, bf16[1024,512]{1,0:T(8,128)(2,1)S(1)}, u32[]{:S(2)}, u32[]{:S(2)}) collective-permute-start(bf16[1024,512]{1,0:T(8,128)(2,1)} %refs_2_.6), channel_id=1, source_target_pairs={{0,2},{1,3},{2,0},{3,1},{4,6},{5,7},{6,4},{7,5},{8,10},{9,11},{10,... | collective-permute-start | bytes 3145736 | tf_op jit(solution)/shard_map/ppermute | solution.py:669
  5.2 4.2 %shard_map.101 = (f32[5,16,256]{2,1,0:T(8,128)S(1)}, f32[512,128]{1,0:T(8,128)S(1)}, bf16[528,128]{1,0:T(8,128)(2,1)S(1)}, bf16[2048,128]{1,0:T(8,128)(2,1)}) custom-call(bf16[1024,512]{1,0:T(8,128)(2,1)} %refs_0_.11, bf16[1024,512]{1,0:T(8,128)(2,1)} %refs_1_.9, f32[4,1024]{1,0:T(4,128)} %refs_2_.4), custom_call_target="tpu_custom_call" | custom-call | tf_op jit(solution)/shard_map/pallas_call | solution.py:156
  9.4 1.3 %collective-permute-done.refs_2_.refs_6_.refs_4_.refs_5_ = bf16[528,128]{1,0:T(8,128)(2,1)S(1)} collective-permute-done((bf16[528,128]{1,0:T(8,128)(2,1)S(1)}, bf16[528,128]{1,0:T(8,128)(2,1)S(1)}, u32[]{:S(2)}, u32[]{:S(2)}) %collective-permute-start) | collective-permute-done | bytes 135200 | tf_op jit(solution)/shard_map/ppermute | solution.py:625
  10.8 1.6 %collective-permute-start.1 = (bf16[272,128]{1,0:T(8,128)(2,1)S(1)}, bf16[272,128]{1,0:T(8,128)(2,1)S(1)}, u32[]{:S(2)}, u32[]{:S(2)}) collective-permute-start(bf16[272,128]{1,0:T(8,128)(2,1)S(1)} %shard_map.102.refs_5_), channel_id=1, source_target_pairs={{0,8},{4,12},{8,16},{12,20},{16,24},{20,28},{24,0},{28,4},{1,9},{5... | collective-permute-start | bytes 208904 | tf_op jit(solution)/shard_map/ppermute | solution.py:638
  12.5 2.6 %collective-permute-start.2 = (bf16[272,128]{1,0:T(8,128)(2,1)S(1)}, bf16[272,128]{1,0:T(8,128)(2,1)S(1)}, u32[]{:S(2)}, u32[]{:S(2)}) collective-permute-start(bf16[272,128]{1,0:T(8,128)(2,1)S(1)} %shard_map.102.refs_5_), channel_id=1, source_target_pairs={{0,16},{4,20},{8,24},{12,28},{16,0},{20,4},{24,8},{28,12},{1,17},{... | collective-permute-start | bytes 208904 | tf_op jit(solution)/shard_map/ppermute | solution.py:638
  15.1 1.3 %collective-permute-start.3 = (bf16[272,128]{1,0:T(8,128)(2,1)S(1)}, bf16[272,128]{1,0:T(8,128)(2,1)S(1)}, u32[]{:S(2)}, u32[]{:S(2)}) collective-permute-start(bf16[272,128]{1,0:T(8,128)(2,1)S(1)} %shard_map.102.refs_5_), channel_id=1, source_target_pairs={{0,24},{4,28},{8,0},{12,4},{16,8},{20,12},{24,16},{28,20},{1,25},{... | collective-permute-start | bytes 208904 | tf_op jit(solution)/shard_map/ppermute | solution.py:638
  16.4 4.6 %shard_map.103 = (f32[1024,512]{1,0:T(8,128)S(1)}, bf16[512,1024]{1,0:T(8,128)(2,1)}) custom-call(bf16[1024,512]{1,0:T(8,128)(2,1)} %refs_0_.10, bf16[1024,512]{1,0:T(8,128)(2,1)} %refs_0_.11, bf16[1024,512]{1,0:T(8,128)(2,1)} %refs_1_.9, f32[5,16,256]{2,1,0:T(8,128)S(1)} %get-tuple-element.38.refs_3_.refs_2_.refs_7_.refs_4_, ...), custom_call_target="tpu_custom_call" | custom-call | tf_op jit(solution)/shard_map/pallas_call | solution.py:156
  21.1 1.2 %collective-permute-done.4.refs_4_ = bf16[256,128]{1,0:T(8,128)(2,1)S(1)} collective-permute-done((bf16[256,128]{1,0:T(8,128)(2,1)S(1)}, bf16[256,128]{1,0:T(8,128)(2,1)S(1)}, u32[]{:S(2)}, u32[]{:S(2)}) %collective-permute-start.4) | collective-permute-done | bytes 65568 | tf_op jit(solution)/shard_map/ppermute | solution.py:625
  22.4 3.2 %shard_map.105 = (bf16[1024,512]{1,0:T(8,128)(2,1)}, f32[16,256]{1,0:T(8,128)S(1)}, f32[512,128]{1,0:T(8,128)S(1)}) custom-call(f32[1024,512]{1,0:T(8,128)S(1)} %get-tuple-element.42.refs_5_.refs_0_, bf16[1024,512]{1,0:T(8,128)(2,1)} %refs_0_.10, f32[5,16,256]{2,1,0:T(8,128)S(1)} %get-tuple-element.38.refs_3_.refs_2_.refs_7_.refs_4_, ...), custom_call_target="tpu_custom_call" | custom-call | tf_op jit(solution)/shard_map/pallas_call | solution.py:156
  25.6 1.4 %collective-permute-done.5.refs_0_.refs_3_ = bf16[1024,512]{1,0:T(8,128)(2,1)S(1)} collective-permute-done((bf16[1024,512]{1,0:T(8,128)(2,1)}, bf16[1024,512]{1,0:T(8,128)(2,1)S(1)}, u32[]{:S(2)}, u32[]{:S(2)}) %collective-permute-start.5) | collective-permute-done | bytes 1048608 | tf_op jit(solution)/shard_map/ppermute | solution.py:669
  27.0 1.8 %collective-permute-start.6 = (bf16[1024,256]{1,0:T(8,128)(2,1)S(1)}, bf16[1024,256]{1,0:T(8,128)(2,1)S(1)}, u32[]{:S(2)}, u32[]{:S(2)}) collective-permute-start(bf16[1024,256]{1,0:T(8,128)(2,1)S(1)} %get-tuple-element.47), channel_id=1, source_target_pairs={{0,2},{1,3},{2,0},{3,1},{4,6},{5,7},{6,4},{7,5},{8,10},{9,11},{10,... | collective-permute-start | bytes 1572872 | tf_op jit(solution)/shard_map/ppermute | solution.py:669
  28.9 1.6 %collective-permute-start.8 = (bf16[1024,256]{1,0:T(8,128)(2,1)S(1)}, bf16[1024,256]{1,0:T(8,128)(2,1)S(1)}, u32[]{:S(2)}, u32[]{:S(2)}) collective-permute-start(bf16[1024,256]{1,0:T(8,128)(2,1)S(1)} %get-tuple-element.49), channel_id=1, source_target_pairs={{0,1},{1,0},{2,3},{3,2},{4,5},{5,4},{6,7},{7,6},{8,9},{9,8},{10,11... | collective-permute-start | bytes 1572872 | tf_op jit(solution)/shard_map/ppermute | solution.py:669
  30.5 5.7 %shard_map.108 = (bf16[3,256,512]{2,1,0:T(8,128)(2,1)S(1)}, bf16[256,512]{1,0:T(8,128)(2,1)S(1)}, bf16[256,512]{1,0:T(8,128)(2,1)S(1)}, bf16[256,512]{1,0:T(8,128)(2,1)S(1)}, f32[1024,512]{1,0:T(8,128)S(1)}) custom-call(bf16[2048,512]{1,0:T(8,128)(2,1)} %refs_0_.9, bf16[1024,512]{1,0:T(8,128)(2,1)} %get-tuple-element.33.refs_1_, bf16[1024,512]{1,0:T(8,128)(2,1)} %refs_2_.6, ...), custom_call_target="tpu_custom_call" | custom-call | tf_op jit(solution)/shard_map/pallas_call | solution.py:156
  36.2 0.5 collective-permute-start.10
  36.8 0.9 %collective-permute-done.9.refs_1_ = bf16[256,512]{1,0:T(8,128)(2,1)S(1)} collective-permute-done((bf16[256,512]{1,0:T(8,128)(2,1)S(1)}, bf16[256,512]{1,0:T(8,128)(2,1)S(1)}, u32[]{:S(2)}, u32[]{:S(2)}) %collective-permute-start.9) | collective-permute-done | bytes 262176 | tf_op jit(solution)/shard_map/ppermute | solution.py:703
  37.8 0.4 collective-permute-done.10.refs_2_
  38.1 0.4 collective-permute-done.11.refs_3_
  38.7 1.6 %collective-permute-start.12 = (bf16[2,256,512]{2,1,0:T(8,128)(2,1)S(1)}, bf16[2,256,512]{2,1,0:T(8,128)(2,1)S(1)}, u32[]{:S(2)}, u32[]{:S(2)}) collective-permute-start(bf16[2,256,512]{2,1,0:T(8,128)(2,1)S(1)} %get-tuple-element.59), channel_id=1, source_target_pairs={{0,8},{1,9},{2,10},{3,11},{4,12},{5,13},{6,14},{7,15},{8,0},{9,1},... | collective-permute-start | bytes 1572872 | tf_op jit(solution)/shard_map/ppermute | solution.py:615
  40.4 1.1 %collective-permute-done.8.refs_3_ = bf16[1024,256]{1,0:T(8,128)(2,1)S(1)} collective-permute-done((bf16[1024,256]{1,0:T(8,128)(2,1)S(1)}, bf16[1024,256]{1,0:T(8,128)(2,1)S(1)}, u32[]{:S(2)}, u32[]{:S(2)}) %collective-permute-start.8) | collective-permute-done | bytes 524320 | tf_op jit(solution)/shard_map/ppermute | solution.py:669
  41.5 5.1 %shard_map.110 = (bf16[1024,512]{1,0:T(8,128)(2,1)S(1)}, f32[512,128]{1,0:T(8,128)S(1)}, bf16[528,128]{1,0:T(8,128)(2,1)S(1)}, bf16[2048,128]{1,0:T(8,128)(2,1)}...) custom-call(bf16[2048,512]{1,0:T(8,128)(2,1)} %refs_0_.9, bf16[1024,512]{1,0:T(8,128)(2,1)} %get-tuple-element.33.refs_1_, ...), custom_call_target="tpu_custom_call" | custom-call | tf_op jit(solution)/shard_map/pallas_call | solution.py:156
  46.7 0.5 collective-permute-start.14
  47.2 1.2 %collective-permute-done.14.refs_2_.refs_5_.refs_9_.refs_4_.refs_3_ = bf16[528,128]{1,0:T(8,128)(2,1)S(1)} collective-permute-done((bf16[528,128]{1,0:T(8,128)(2,1)S(1)}, bf16[528,128]{1,0:T(8,128)(2,1)S(1)}, u32[]{:S(2)}, u32[]{:S(2)}) %collective-permute-start.14) | collective-permute-done | bytes 135200 | tf_op jit(solution)/shard_map/ppermute | solution.py:625
  48.6 3.5 %collective-permute-start.19 = (bf16[256,512]{1,0:T(8,128)(2,1)S(1)}, bf16[256,512]{1,0:T(8,128)(2,1)S(1)}, u32[]{:S(2)}, u32[]{:S(2)}) collective-permute-start(bf16[256,512]{1,0:T(8,128)(2,1)S(1)} %shard_map.112.refs_2_.refs_6_.refs_10_.refs_5_.refs_0_), channel_id=1, source_target_pairs={{0,8},{2,10},{4,12},{6,14},{9,1},{11,3},{13,5},{15,7},{16,24},{18,... | collective-permute-start | bytes 786440 | tf_op jit(solution)/shard_map/ppermute | solution.py:615
  52.1 2.7 %collective-permute-start.16 = (bf16[272,128]{1,0:T(8,128)(2,1)S(1)}, bf16[272,128]{1,0:T(8,128)(2,1)S(1)}, u32[]{:S(2)}, u32[]{:S(2)}) collective-permute-start(bf16[272,128]{1,0:T(8,128)(2,1)S(1)} %shard_map.111.refs_2_), channel_id=1, source_target_pairs={{0,16},{4,20},{8,24},{12,28},{16,0},{20,4},{24,8},{28,12},{1,17},{... | collective-permute-start | bytes 208904 | tf_op jit(solution)/shard_map/ppermute | solution.py:638
  54.8 2.8 %collective-permute-start.17 = (bf16[272,128]{1,0:T(8,128)(2,1)S(1)}, bf16[272,128]{1,0:T(8,128)(2,1)S(1)}, u32[]{:S(2)}, u32[]{:S(2)}) collective-permute-start(bf16[272,128]{1,0:T(8,128)(2,1)S(1)} %shard_map.111.refs_2_), channel_id=1, source_target_pairs={{0,24},{4,28},{8,0},{12,4},{16,8},{20,12},{24,16},{28,20},{1,25},{... | collective-permute-start | bytes 208904 | tf_op jit(solution)/shard_map/ppermute | solution.py:638
  57.8 2.4 %collective-permute-start.21 = (bf16[256,512]{1,0:T(8,128)(2,1)S(1)}, bf16[256,512]{1,0:T(8,128)(2,1)S(1)}, u32[]{:S(2)}, u32[]{:S(2)}) collective-permute-start(bf16[256,512]{1,0:T(8,128)(2,1)S(1)} %get-tuple-element.64.refs_8_), channel_id=1, source_target_pairs={{0,16},{2,18},{3,19},{4,20},{6,22},{7,23},{9,25},{10,26},{11,27},{... | collective-permute-start | bytes 786440 | tf_op jit(solution)/shard_map/ppermute | solution.py:615
  60.2 8.3 %shard_map.114 = (bf16[1024,512]{1,0:T(8,128)(2,1)}, bf16[1024,512]{1,0:T(8,128)(2,1)}, bf16[1024,512]{1,0:T(8,128)(2,1)}) custom-call(bf16[1024,512]{1,0:T(8,128)(2,1)} %refs_0_.10, bf16[1024,512]{1,0:T(8,128)(2,1)} %refs_0_.11, bf16[1024,512]{1,0:T(8,128)(2,1)} %refs_1_.9, bf16[1024,512]{1,0:T(8,128)(2,1)S(1)} %get-tuple-element.57.refs_5_.refs_4_.refs_3_, ...), custom_call_target="tpu_custom_call" | custom-call | tf_op jit(solution)/shard_map/pallas_call | solution.py:156
  68.7 0.7 collective-permute-start.20
  69.5 1.2 %collective-permute-done.18.refs_4_ = bf16[256,128]{1,0:T(8,128)(2,1)S(1)} collective-permute-done((bf16[256,128]{1,0:T(8,128)(2,1)S(1)}, bf16[256,128]{1,0:T(8,128)(2,1)S(1)}, u32[]{:S(2)}, u32[]{:S(2)}) %collective-permute-start.18) | collective-permute-done | bytes 65568 | tf_op jit(solution)/shard_map/ppermute | solution.py:625
  70.7 4.6 %shard_map.117 = (bf16[1024,512]{1,0:T(8,128)(2,1)}, bf16[1024,512]{1,0:T(8,128)(2,1)}) custom-call(bf16[1024,512]{1,0:T(8,128)(2,1)} %refs_0_.11, bf16[1024,512]{1,0:T(8,128)(2,1)} %refs_1_.9, f32[5,16,256]{2,1,0:T(8,128)S(1)} %get-tuple-element.38.refs_3_.refs_2_.refs_7_.refs_4_, bf16[256,128]{1,0:T(8,128)(2,1)S(1)} %shard_map.115.refs_2_.refs_3_, ...), custom_call_target="tpu_custom_call" | custom-call | tf_op jit(solution)/shard_map/pallas_call | solution.py:156
  75.3 0.8 %select_convert_fusion = bf16[256,512]{1,0:T(8,128)(2,1)} fusion(f32[256,512]{1,0:T(8,128)S(1)} %get-tuple-element.70, bf16[256,512]{1,0:T(8,128)(2,1)S(1)} %collective-permute-done.21, bf16[256,512]{1,0:T(8,128)(2,1)S(1)} %collective-permute-done.20, bf16[256,512]{1,0:T(8,128)(2,1)S(1)} %shard_map.116.refs_8_, pred[]{:T(512)S(6)} %eq.3), kind=kLoop, calls=%fused_computation | loop fusion | flops 917504 | bytes 1572865 | tf_op jit(solution)/shard_map/convert_element_type | solution.py:788
  (30 shorter events, 1.4 us)
Async XLA Ops:
  0.6 26.4 %collective-permute-start.5 = (bf16[1024,512]{1,0:T(8,128)(2,1)}, bf16[1024,512]{1,0:T(8,128)(2,1)S(1)}, u32[]{:S(2)}, u32[]{:S(2)}) collective-permute-start(bf16[1024,512]{1,0:T(8,128)(2,1)} %refs_2_.6), channel_id=1, source_target_pairs={{0,1},{1,0},{2,3},{3,2},{4,5},{5,4},{6,7},{7,6},{8,9},{9,8},{10,11... | collective-permute-start | bytes 3145736 | tf_op jit(solution)/shard_map/ppermute | solution.py:669
  3.6 25.2 %collective-permute-start.7 = (bf16[1024,512]{1,0:T(8,128)(2,1)}, bf16[1024,512]{1,0:T(8,128)(2,1)S(1)}, u32[]{:S(2)}, u32[]{:S(2)}) collective-permute-start(bf16[1024,512]{1,0:T(8,128)(2,1)} %refs_2_.6), channel_id=1, source_target_pairs={{0,2},{1,3},{2,0},{3,1},{4,6},{5,7},{6,4},{7,5},{8,10},{9,11},{10,... | collective-permute-start | bytes 3145736 | tf_op jit(solution)/shard_map/ppermute | solution.py:669
  9.3 1.4 %collective-permute-start = (bf16[528,128]{1,0:T(8,128)(2,1)S(1)}, bf16[528,128]{1,0:T(8,128)(2,1)S(1)}, u32[]{:S(2)}, u32[]{:S(2)}) collective-permute-start(bf16[528,128]{1,0:T(8,128)(2,1)S(1)} %get-tuple-element.41.refs_1_), channel_id=1, source_target_pairs={{0,4},{4,0},{8,12},{12,8},{16,20},{20,16},{24,28},{28,24},{1,5},{5... | collective-permute-start | bytes 405512 | tf_op jit(solution)/shard_map/ppermute | solution.py:625
  10.8 10.1 %collective-permute-start.1 = (bf16[272,128]{1,0:T(8,128)(2,1)S(1)}, bf16[272,128]{1,0:T(8,128)(2,1)S(1)}, u32[]{:S(2)}, u32[]{:S(2)}) collective-permute-start(bf16[272,128]{1,0:T(8,128)(2,1)S(1)} %shard_map.102.refs_5_), channel_id=1, source_target_pairs={{0,8},{4,12},{8,16},{12,20},{16,24},{20,28},{24,0},{28,4},{1,9},{5... | collective-permute-start | bytes 208904 | tf_op jit(solution)/shard_map/ppermute | solution.py:638
  12.5 8.5 %collective-permute-start.2 = (bf16[272,128]{1,0:T(8,128)(2,1)S(1)}, bf16[272,128]{1,0:T(8,128)(2,1)S(1)}, u32[]{:S(2)}, u32[]{:S(2)}) collective-permute-start(bf16[272,128]{1,0:T(8,128)(2,1)S(1)} %shard_map.102.refs_5_), channel_id=1, source_target_pairs={{0,16},{4,20},{8,24},{12,28},{16,0},{20,4},{24,8},{28,12},{1,17},{... | collective-permute-start | bytes 208904 | tf_op jit(solution)/shard_map/ppermute | solution.py:638
  15.1 5.9 %collective-permute-start.3 = (bf16[272,128]{1,0:T(8,128)(2,1)S(1)}, bf16[272,128]{1,0:T(8,128)(2,1)S(1)}, u32[]{:S(2)}, u32[]{:S(2)}) collective-permute-start(bf16[272,128]{1,0:T(8,128)(2,1)S(1)} %shard_map.102.refs_5_), channel_id=1, source_target_pairs={{0,24},{4,28},{8,0},{12,4},{16,8},{20,12},{24,16},{28,20},{1,25},{... | collective-permute-start | bytes 208904 | tf_op jit(solution)/shard_map/ppermute | solution.py:638
  21.1 1.3 %collective-permute-start.4 = (bf16[256,128]{1,0:T(8,128)(2,1)S(1)}, bf16[256,128]{1,0:T(8,128)(2,1)S(1)}, u32[]{:S(2)}, u32[]{:S(2)}) collective-permute-start(bf16[256,128]{1,0:T(8,128)(2,1)S(1)} %shard_map.104.refs_3_), channel_id=1, source_target_pairs={{0,4},{4,0},{8,12},{12,8},{16,20},{20,16},{24,28},{28,24},{1,5},{5... | collective-permute-start | bytes 196616 | tf_op jit(solution)/shard_map/ppermute | solution.py:625
  27.0 13.3 %collective-permute-start.6 = (bf16[1024,256]{1,0:T(8,128)(2,1)S(1)}, bf16[1024,256]{1,0:T(8,128)(2,1)S(1)}, u32[]{:S(2)}, u32[]{:S(2)}) collective-permute-start(bf16[1024,256]{1,0:T(8,128)(2,1)S(1)} %get-tuple-element.47), channel_id=1, source_target_pairs={{0,2},{1,3},{2,0},{3,1},{4,6},{5,7},{6,4},{7,5},{8,10},{9,11},{10,... | collective-permute-start | bytes 1572872 | tf_op jit(solution)/shard_map/ppermute | solution.py:669
  28.9 12.6 %collective-permute-start.8 = (bf16[1024,256]{1,0:T(8,128)(2,1)S(1)}, bf16[1024,256]{1,0:T(8,128)(2,1)S(1)}, u32[]{:S(2)}, u32[]{:S(2)}) collective-permute-start(bf16[1024,256]{1,0:T(8,128)(2,1)S(1)} %get-tuple-element.49), channel_id=1, source_target_pairs={{0,1},{1,0},{2,3},{3,2},{4,5},{5,4},{6,7},{7,6},{8,9},{9,8},{10,11... | collective-permute-start | bytes 1572872 | tf_op jit(solution)/shard_map/ppermute | solution.py:669
  36.2 1.6 %collective-permute-start.9 = (bf16[256,512]{1,0:T(8,128)(2,1)S(1)}, bf16[256,512]{1,0:T(8,128)(2,1)S(1)}, u32[]{:S(2)}, u32[]{:S(2)}) collective-permute-start(bf16[256,512]{1,0:T(8,128)(2,1)S(1)} %get-tuple-element.53.refs_4_), channel_id=1, source_target_pairs={{0,4},{4,0},{8,12},{12,8},{16,20},{20,16},{24,28},{28,24},{1,5},{5... | collective-permute-start | bytes 786440 | tf_op jit(solution)/shard_map/ppermute | solution.py:703
  36.2 1.9 %collective-permute-start.10 = (bf16[256,512]{1,0:T(8,128)(2,1)S(1)}, bf16[256,512]{1,0:T(8,128)(2,1)S(1)}, u32[]{:S(2)}, u32[]{:S(2)}) collective-permute-start(bf16[256,512]{1,0:T(8,128)(2,1)S(1)} %get-tuple-element.54), channel_id=1, source_target_pairs={{0,4},{4,0},{8,12},{12,8},{16,20},{20,16},{24,28},{28,24},{1,5},{5... | collective-permute-start | bytes 786440 | tf_op jit(solution)/shard_map/ppermute | solution.py:703
  36.7 1.8 %collective-permute-start.11 = (bf16[256,512]{1,0:T(8,128)(2,1)S(1)}, bf16[256,512]{1,0:T(8,128)(2,1)S(1)}, u32[]{:S(2)}, u32[]{:S(2)}) collective-permute-start(bf16[256,512]{1,0:T(8,128)(2,1)S(1)} %get-tuple-element.55), channel_id=1, source_target_pairs={{0,4},{4,0},{8,12},{12,8},{16,20},{20,16},{24,28},{28,24},{1,5},{5... | collective-permute-start | bytes 786440 | tf_op jit(solution)/shard_map/ppermute | solution.py:703
  38.7 18.9 %collective-permute-start.12 = (bf16[2,256,512]{2,1,0:T(8,128)(2,1)S(1)}, bf16[2,256,512]{2,1,0:T(8,128)(2,1)S(1)}, u32[]{:S(2)}, u32[]{:S(2)}) collective-permute-start(bf16[2,256,512]{2,1,0:T(8,128)(2,1)S(1)} %get-tuple-element.59), channel_id=1, source_target_pairs={{0,8},{1,9},{2,10},{3,11},{4,12},{5,13},{6,14},{7,15},{8,0},{9,1},... | collective-permute-start | bytes 1572872 | tf_op jit(solution)/shard_map/ppermute | solution.py:615
  46.6 1.9 %collective-permute-start.13 = (bf16[256,512]{1,0:T(8,128)(2,1)S(1)}, bf16[256,512]{1,0:T(8,128)(2,1)S(1)}, u32[]{:S(2)}, u32[]{:S(2)}) collective-permute-start(bf16[256,512]{1,0:T(8,128)(2,1)S(1)} %get-tuple-element.61), channel_id=1, source_target_pairs={{0,4},{4,0},{8,12},{12,8},{16,20},{20,16},{24,28},{28,24},{1,5},{5... | collective-permute-start | bytes 786440 | tf_op jit(solution)/shard_map/ppermute | solution.py:703
  46.7 1.7 %collective-permute-start.14 = (bf16[528,128]{1,0:T(8,128)(2,1)S(1)}, bf16[528,128]{1,0:T(8,128)(2,1)S(1)}, u32[]{:S(2)}, u32[]{:S(2)}) collective-permute-start(bf16[528,128]{1,0:T(8,128)(2,1)S(1)} %get-tuple-element.63.refs_1_), channel_id=1, source_target_pairs={{0,4},{4,0},{8,12},{12,8},{16,20},{20,16},{24,28},{28,24},{1,5},{5... | collective-permute-start | bytes 405512 | tf_op jit(solution)/shard_map/ppermute | solution.py:625
  48.6 20.1 %collective-permute-start.19 = (bf16[256,512]{1,0:T(8,128)(2,1)S(1)}, bf16[256,512]{1,0:T(8,128)(2,1)S(1)}, u32[]{:S(2)}, u32[]{:S(2)}) collective-permute-start(bf16[256,512]{1,0:T(8,128)(2,1)S(1)} %shard_map.112.refs_2_.refs_6_.refs_10_.refs_5_.refs_0_), channel_id=1, source_target_pairs={{0,8},{2,10},{4,12},{6,14},{9,1},{11,3},{13,5},{15,7},{16,24},{18,... | collective-permute-start | bytes 786440 | tf_op jit(solution)/shard_map/ppermute | solution.py:615
  52.1 16.4 %collective-permute-start.15 = (bf16[272,128]{1,0:T(8,128)(2,1)S(1)}, bf16[272,128]{1,0:T(8,128)(2,1)S(1)}, u32[]{:S(2)}, u32[]{:S(2)}) collective-permute-start(bf16[272,128]{1,0:T(8,128)(2,1)S(1)} %shard_map.111.refs_2_), channel_id=1, source_target_pairs={{0,8},{4,12},{8,16},{12,20},{16,24},{20,28},{24,0},{28,4},{1,9},{5... | collective-permute-start | bytes 208904 | tf_op jit(solution)/shard_map/ppermute | solution.py:638
  52.1 16.4 %collective-permute-start.16 = (bf16[272,128]{1,0:T(8,128)(2,1)S(1)}, bf16[272,128]{1,0:T(8,128)(2,1)S(1)}, u32[]{:S(2)}, u32[]{:S(2)}) collective-permute-start(bf16[272,128]{1,0:T(8,128)(2,1)S(1)} %shard_map.111.refs_2_), channel_id=1, source_target_pairs={{0,16},{4,20},{8,24},{12,28},{16,0},{20,4},{24,8},{28,12},{1,17},{... | collective-permute-start | bytes 208904 | tf_op jit(solution)/shard_map/ppermute | solution.py:638
  54.8 13.7 %collective-permute-start.17 = (bf16[272,128]{1,0:T(8,128)(2,1)S(1)}, bf16[272,128]{1,0:T(8,128)(2,1)S(1)}, u32[]{:S(2)}, u32[]{:S(2)}) collective-permute-start(bf16[272,128]{1,0:T(8,128)(2,1)S(1)} %shard_map.111.refs_2_), channel_id=1, source_target_pairs={{0,24},{4,28},{8,0},{12,4},{16,8},{20,12},{24,16},{28,20},{1,25},{... | collective-permute-start | bytes 208904 | tf_op jit(solution)/shard_map/ppermute | solution.py:638
  57.8 17.5 %collective-permute-start.21 = (bf16[256,512]{1,0:T(8,128)(2,1)S(1)}, bf16[256,512]{1,0:T(8,128)(2,1)S(1)}, u32[]{:S(2)}, u32[]{:S(2)}) collective-permute-start(bf16[256,512]{1,0:T(8,128)(2,1)S(1)} %get-tuple-element.64.refs_8_), channel_id=1, source_target_pairs={{0,16},{2,18},{3,19},{4,20},{6,22},{7,23},{9,25},{10,26},{11,27},{... | collective-permute-start | bytes 786440 | tf_op jit(solution)/shard_map/ppermute | solution.py:615
  68.7 6.6 %collective-permute-start.20 = (bf16[256,512]{1,0:T(8,128)(2,1)S(1)}, bf16[256,512]{1,0:T(8,128)(2,1)S(1)}, u32[]{:S(2)}, u32[]{:S(2)}) collective-permute-start(bf16[256,512]{1,0:T(8,128)(2,1)S(1)} %shard_map.116.refs_8_), channel_id=1, source_target_pairs={{1,17},{5,21},{8,24},{12,28},{19,3},{23,7},{26,10},{30,14}} | collective-permute-start | bytes 786440 | tf_op jit(solution)/shard_map/ppermute | solution.py:615
  69.4 1.3 %collective-permute-start.18 = (bf16[256,128]{1,0:T(8,128)(2,1)S(1)}, bf16[256,128]{1,0:T(8,128)(2,1)S(1)}, u32[]{:S(2)}, u32[]{:S(2)}) collective-permute-start(bf16[256,128]{1,0:T(8,128)(2,1)S(1)} %shard_map.115.refs_2_.refs_3_), channel_id=1, source_target_pairs={{0,4},{4,0},{8,12},{12,8},{16,20},{20,16},{24,28},{28,24},{1,5},{5... | collective-permute-start | bytes 196616 | tf_op jit(solution)/shard_map/ppermute | solution.py:625

commit v6 on v5

--- a/solution.py
+++ b/solution.py
@@ -524,12 +524,17 @@
             tail = tails[:, r : r + 1]
             value_tail, key_tail = (value * tail).astype(BF16), (key * tail).astype(BF16)
         yield True
-        query_part = mm(turned, key, NN) + mm(grown, state, NT)
+        query_part = mm(
+            jnp.concatenate([turned, grown], 1), jnp.concatenate([key, state.T], 0), NN
+        )
+        if j < chunks - 1:
+            left = exits[at, :]
+            masked = jnp.concatenate([masked, value_tail], 1)
+            weight = jnp.concatenate([weight, key_tail], 1)
+            query = jnp.concatenate([query, left.T], 0)
+            grad = jnp.concatenate([grad, left], 0)
         key_part = mm(masked, query, NN)
         value_part = mm(weight, grad, NN)
-        if j < chunks - 1:
-            key_part = key_part + mm(value_tail, exits[at, :], NT)
-            value_part = value_part + mm(key_tail, exits[at, :], NN)
         yield True
         query_grad[rows, cols] = query_part.astype(BF16)
         key_grad[rows, cols] = key_part.astype(BF16)
@@ -661,6 +666,7 @@
     size = 256 if length % 256 == 0 else length
     chunks = length // size
     chips = seq_size // 2
+    half = max(1, heads // 2)
     near = head_size == 4 and chips == 4
     seq, head = lax.axis_index("seq"), lax.axis_index("head")
     turn = (seq // 2) ^ head
@@ -687,7 +693,7 @@
     forward.send()
     mixed, grown_rows = line.call(
         local_body, [(rows, F32), ((columns, length), BF16)], queries, keys, values, tables, states,
-        fetch={0: heads, 1: heads, 2: heads, 4: (heads, 0)}, store={1: (heads, 0)},
+        fetch={0: half, 1: half, 2: half, 4: (half, 0)}, store={1: (heads, 0)},
     )
     held.update(mixed=mixed)
     forward.join()
@@ -760,7 +766,7 @@
     query_grad, key_part, value_part = line.call(
         functools.partial(back_body, heads), [(rows, BF16), (rows, BF16), (rows, BF16)],
         queries, keys, values, mixed_grad, tables, incoming, states, exits,
-        fetch={0: heads, 1: heads, 2: heads, 6: (heads, 0), 7: (heads, 0)},
+        fetch={0: half, 1: half, 2: half, 6: (half, 0), 7: (half, 0)},
         store={i: heads for i in range(3)},
     )
     for name in ("mixed_grad", "incoming"):
@@ -774,7 +780,7 @@
         functools.partial(final_body, heads), [(rows, BF16)] * 2,
         keys, values, tables, *back.done(), key_part, value_part,
         scratch=[pltpu.VMEM((heads * width, width), F32)], place=True,
-        fetch={0: heads, 1: heads, 6: heads, 7: heads}, store={0: heads, 1: heads},
+        fetch={0: half, 1: half, 6: half, 7: half}, store={0: heads, 1: heads},
     )
     if near:
         weight_grad = jnp.where(

time: 77 us -> 76.6 us (level)
  no operation moved by 1% of the time
where the time goes in v6:
time: 76.6 us; the launch traced here: 75.7 us
  Pallas kernels  36 us (47%)
  starting transfers between devices  28.7 us (37%)
  waiting for transfers between devices  9.16 us (12%)
  between operations  0.91 us (1%)
  other arithmetic  0.85 us (1%)
    pallas_call x17, Pallas kernels, call(): pl.pallas_call(kernel, out_shape=shapes, in_specs=specs + [ANY] * more, o...  36 us
    ppermute x6, starting transfers between devices, send(): lax.ppermute(message, 'seq', [(i, (i // 2 + k) % self.chips * 2 + i % 2)...  11.1 us
    ppermute x4, starting transfers between devices, hop(): return lax.ppermute(value, ('seq', 'head'), moves)  8.23 us
    ppermute x4, starting transfers between devices, on_device(): lax.ppermute(a, 'head', [(i, i ^ k) for i in range(head_size)])  7.91 us
    ppermute x4, waiting for transfers between devices, swap(): lax.ppermute(value, 'seq', [(i, i ^ 1) for i in range(2 * self.chips)])  5.02 us
    ppermute x4, waiting for transfers between devices, on_device(): lax.ppermute(a, 'head', [(i, i ^ k) for i in range(head_size)])  2.42 us
    ppermute x4, waiting for transfers between devices, on_device(): lax.ppermute(a, 'seq', [(i, i ^ 1) for i in range(2 * chips)])  1.7 us
  transfers between devices with their start and end apart: 22, of which 9 were waited for; matrix products, arithmetic and copies ran while one was open for 0% of the time, Pallas kernels for 48%

profile of v6, /device:TPU:0, one launch (start us, length us, event | category | flops | bytes accessed | tf_op | source)
XLA Modules:
  0.0 75.7 jit_solution(14397607378620465009)
XLA Ops:
  0.6 3.0 %collective-permute-start.5 = (bf16[1024,512]{1,0:T(8,128)(2,1)}, bf16[1024,512]{1,0:T(8,128)(2,1)S(1)}, u32[]{:S(2)}, u32[]{:S(2)}) collective-permute-start(bf16[1024,512]{1,0:T(8,128)(2,1)} %refs_2_.6), channel_id=1, source_target_pairs={{0,1},{1,0},{2,3},{3,2},{4,5},{5,4},{6,7},{7,6},{8,9},{9,8},{10,11... | collective-permute-start | bytes 3145736 | tf_op jit(solution)/shard_map/ppermute | solution.py:675
  3.6 1.5 %collective-permute-start.7 = (bf16[1024,512]{1,0:T(8,128)(2,1)}, bf16[1024,512]{1,0:T(8,128)(2,1)S(1)}, u32[]{:S(2)}, u32[]{:S(2)}) collective-permute-start(bf16[1024,512]{1,0:T(8,128)(2,1)} %refs_2_.6), channel_id=1, source_target_pairs={{0,2},{1,3},{2,0},{3,1},{4,6},{5,7},{6,4},{7,5},{8,10},{9,11},{10,... | collective-permute-start | bytes 3145736 | tf_op jit(solution)/shard_map/ppermute | solution.py:675
  5.2 4.2 %shard_map.101 = (f32[5,16,256]{2,1,0:T(8,128)S(1)}, f32[512,128]{1,0:T(8,128)S(1)}, bf16[528,128]{1,0:T(8,128)(2,1)S(1)}, bf16[2048,128]{1,0:T(8,128)(2,1)}) custom-call(bf16[1024,512]{1,0:T(8,128)(2,1)} %refs_0_.11, bf16[1024,512]{1,0:T(8,128)(2,1)} %refs_1_.9, f32[4,1024]{1,0:T(4,128)} %refs_2_.4), custom_call_target="tpu_custom_call" | custom-call | tf_op jit(solution)/shard_map/pallas_call | solution.py:156
  9.4 1.3 %collective-permute-done.refs_2_.refs_6_.refs_4_.refs_5_ = bf16[528,128]{1,0:T(8,128)(2,1)S(1)} collective-permute-done((bf16[528,128]{1,0:T(8,128)(2,1)S(1)}, bf16[528,128]{1,0:T(8,128)(2,1)S(1)}, u32[]{:S(2)}, u32[]{:S(2)}) %collective-permute-start) | collective-permute-done | bytes 135200 | tf_op jit(solution)/shard_map/ppermute | solution.py:630
  10.8 1.6 %collective-permute-start.1 = (bf16[272,128]{1,0:T(8,128)(2,1)S(1)}, bf16[272,128]{1,0:T(8,128)(2,1)S(1)}, u32[]{:S(2)}, u32[]{:S(2)}) collective-permute-start(bf16[272,128]{1,0:T(8,128)(2,1)S(1)} %shard_map.102.refs_5_), channel_id=1, source_target_pairs={{0,8},{4,12},{8,16},{12,20},{16,24},{20,28},{24,0},{28,4},{1,9},{5... | collective-permute-start | bytes 208904 | tf_op jit(solution)/shard_map/ppermute | solution.py:643
  12.5 2.6 %collective-permute-start.2 = (bf16[272,128]{1,0:T(8,128)(2,1)S(1)}, bf16[272,128]{1,0:T(8,128)(2,1)S(1)}, u32[]{:S(2)}, u32[]{:S(2)}) collective-permute-start(bf16[272,128]{1,0:T(8,128)(2,1)S(1)} %shard_map.102.refs_5_), channel_id=1, source_target_pairs={{0,16},{4,20},{8,24},{12,28},{16,0},{20,4},{24,8},{28,12},{1,17},{... | collective-permute-start | bytes 208904 | tf_op jit(solution)/shard_map/ppermute | solution.py:643
  15.1 1.3 %collective-permute-start.3 = (bf16[272,128]{1,0:T(8,128)(2,1)S(1)}, bf16[272,128]{1,0:T(8,128)(2,1)S(1)}, u32[]{:S(2)}, u32[]{:S(2)}) collective-permute-start(bf16[272,128]{1,0:T(8,128)(2,1)S(1)} %shard_map.102.refs_5_), channel_id=1, source_target_pairs={{0,24},{4,28},{8,0},{12,4},{16,8},{20,12},{24,16},{28,20},{1,25},{... | collective-permute-start | bytes 208904 | tf_op jit(solution)/shard_map/ppermute | solution.py:643
  16.4 4.6 %shard_map.103 = (f32[1024,512]{1,0:T(8,128)S(1)}, bf16[512,1024]{1,0:T(8,128)(2,1)}) custom-call(bf16[1024,512]{1,0:T(8,128)(2,1)} %refs_0_.10, bf16[1024,512]{1,0:T(8,128)(2,1)} %refs_0_.11, bf16[1024,512]{1,0:T(8,128)(2,1)} %refs_1_.9, f32[5,16,256]{2,1,0:T(8,128)S(1)} %get-tuple-element.38.refs_3_.refs_2_.refs_7_.refs_4_, ...), custom_call_target="tpu_custom_call" | custom-call | tf_op jit(solution)/shard_map/pallas_call | solution.py:156
  21.2 1.2 %collective-permute-done.4.refs_4_ = bf16[256,128]{1,0:T(8,128)(2,1)S(1)} collective-permute-done((bf16[256,128]{1,0:T(8,128)(2,1)S(1)}, bf16[256,128]{1,0:T(8,128)(2,1)S(1)}, u32[]{:S(2)}, u32[]{:S(2)}) %collective-permute-start.4) | collective-permute-done | bytes 65568 | tf_op jit(solution)/shard_map/ppermute | solution.py:630
  22.5 3.2 %shard_map.105 = (bf16[1024,512]{1,0:T(8,128)(2,1)}, f32[16,256]{1,0:T(8,128)S(1)}, f32[512,128]{1,0:T(8,128)S(1)}) custom-call(f32[1024,512]{1,0:T(8,128)S(1)} %get-tuple-element.42.refs_5_.refs_0_, bf16[1024,512]{1,0:T(8,128)(2,1)} %refs_0_.10, f32[5,16,256]{2,1,0:T(8,128)S(1)} %get-tuple-element.38.refs_3_.refs_2_.refs_7_.refs_4_, ...), custom_call_target="tpu_custom_call" | custom-call | tf_op jit(solution)/shard_map/pallas_call | solution.py:156
  25.7 1.3 %collective-permute-done.5.refs_0_.refs_3_ = bf16[1024,512]{1,0:T(8,128)(2,1)S(1)} collective-permute-done((bf16[1024,512]{1,0:T(8,128)(2,1)}, bf16[1024,512]{1,0:T(8,128)(2,1)S(1)}, u32[]{:S(2)}, u32[]{:S(2)}) %collective-permute-start.5) | collective-permute-done | bytes 1048608 | tf_op jit(solution)/shard_map/ppermute | solution.py:675
  27.0 1.8 %collective-permute-start.6 = (bf16[1024,256]{1,0:T(8,128)(2,1)S(1)}, bf16[1024,256]{1,0:T(8,128)(2,1)S(1)}, u32[]{:S(2)}, u32[]{:S(2)}) collective-permute-start(bf16[1024,256]{1,0:T(8,128)(2,1)S(1)} %get-tuple-element.47), channel_id=1, source_target_pairs={{0,2},{1,3},{2,0},{3,1},{4,6},{5,7},{6,4},{7,5},{8,10},{9,11},{10,... | collective-permute-start | bytes 1572872 | tf_op jit(solution)/shard_map/ppermute | solution.py:675
  28.9 1.6 %collective-permute-start.8 = (bf16[1024,256]{1,0:T(8,128)(2,1)S(1)}, bf16[1024,256]{1,0:T(8,128)(2,1)S(1)}, u32[]{:S(2)}, u32[]{:S(2)}) collective-permute-start(bf16[1024,256]{1,0:T(8,128)(2,1)S(1)} %get-tuple-element.49), channel_id=1, source_target_pairs={{0,1},{1,0},{2,3},{3,2},{4,5},{5,4},{6,7},{7,6},{8,9},{9,8},{10,11... | collective-permute-start | bytes 1572872 | tf_op jit(solution)/shard_map/ppermute | solution.py:675
  30.5 5.7 %shard_map.108 = (bf16[3,256,512]{2,1,0:T(8,128)(2,1)S(1)}, bf16[256,512]{1,0:T(8,128)(2,1)S(1)}, bf16[256,512]{1,0:T(8,128)(2,1)S(1)}, bf16[256,512]{1,0:T(8,128)(2,1)S(1)}, f32[1024,512]{1,0:T(8,128)S(1)}) custom-call(bf16[2048,512]{1,0:T(8,128)(2,1)} %refs_0_.9, bf16[1024,512]{1,0:T(8,128)(2,1)} %get-tuple-element.33.refs_1_, bf16[1024,512]{1,0:T(8,128)(2,1)} %refs_2_.6, ...), custom_call_target="tpu_custom_call" | custom-call | tf_op jit(solution)/shard_map/pallas_call | solution.py:156
  36.2 0.5 collective-permute-start.10
  36.8 0.9 %collective-permute-done.9.refs_1_ = bf16[256,512]{1,0:T(8,128)(2,1)S(1)} collective-permute-done((bf16[256,512]{1,0:T(8,128)(2,1)S(1)}, bf16[256,512]{1,0:T(8,128)(2,1)S(1)}, u32[]{:S(2)}, u32[]{:S(2)}) %collective-permute-start.9) | collective-permute-done | bytes 262176 | tf_op jit(solution)/shard_map/ppermute | solution.py:709
  37.8 0.4 collective-permute-done.10.refs_2_
  38.1 0.4 collective-permute-done.11.refs_3_
  38.7 1.6 %collective-permute-start.12 = (bf16[2,256,512]{2,1,0:T(8,128)(2,1)S(1)}, bf16[2,256,512]{2,1,0:T(8,128)(2,1)S(1)}, u32[]{:S(2)}, u32[]{:S(2)}) collective-permute-start(bf16[2,256,512]{2,1,0:T(8,128)(2,1)S(1)} %get-tuple-element.59), channel_id=1, source_target_pairs={{0,8},{1,9},{2,10},{3,11},{4,12},{5,13},{6,14},{7,15},{8,0},{9,1},... | collective-permute-start | bytes 1572872 | tf_op jit(solution)/shard_map/ppermute | solution.py:620
  40.4 1.1 %collective-permute-done.8.refs_3_ = bf16[1024,256]{1,0:T(8,128)(2,1)S(1)} collective-permute-done((bf16[1024,256]{1,0:T(8,128)(2,1)S(1)}, bf16[1024,256]{1,0:T(8,128)(2,1)S(1)}, u32[]{:S(2)}, u32[]{:S(2)}) %collective-permute-start.8) | collective-permute-done | bytes 524320 | tf_op jit(solution)/shard_map/ppermute | solution.py:675
  41.5 5.1 %shard_map.110 = (bf16[1024,512]{1,0:T(8,128)(2,1)S(1)}, f32[512,128]{1,0:T(8,128)S(1)}, bf16[528,128]{1,0:T(8,128)(2,1)S(1)}, bf16[2048,128]{1,0:T(8,128)(2,1)}...) custom-call(bf16[2048,512]{1,0:T(8,128)(2,1)} %refs_0_.9, bf16[1024,512]{1,0:T(8,128)(2,1)} %get-tuple-element.33.refs_1_, ...), custom_call_target="tpu_custom_call" | custom-call | tf_op jit(solution)/shard_map/pallas_call | solution.py:156
  46.7 0.5 collective-permute-start.14
  47.2 1.2 %collective-permute-done.14.refs_2_.refs_5_.refs_9_.refs_4_.refs_3_ = bf16[528,128]{1,0:T(8,128)(2,1)S(1)} collective-permute-done((bf16[528,128]{1,0:T(8,128)(2,1)S(1)}, bf16[528,128]{1,0:T(8,128)(2,1)S(1)}, u32[]{:S(2)}, u32[]{:S(2)}) %collective-permute-start.14) | collective-permute-done | bytes 135200 | tf_op jit(solution)/shard_map/ppermute | solution.py:630
  48.6 3.5 %collective-permute-start.19 = (bf16[256,512]{1,0:T(8,128)(2,1)S(1)}, bf16[256,512]{1,0:T(8,128)(2,1)S(1)}, u32[]{:S(2)}, u32[]{:S(2)}) collective-permute-start(bf16[256,512]{1,0:T(8,128)(2,1)S(1)} %shard_map.112.refs_2_.refs_6_.refs_10_.refs_5_.refs_0_), channel_id=1, source_target_pairs={{0,8},{2,10},{4,12},{6,14},{9,1},{11,3},{13,5},{15,7},{16,24},{18,... | collective-permute-start | bytes 786440 | tf_op jit(solution)/shard_map/ppermute | solution.py:620
  52.1 2.7 %collective-permute-start.16 = (bf16[272,128]{1,0:T(8,128)(2,1)S(1)}, bf16[272,128]{1,0:T(8,128)(2,1)S(1)}, u32[]{:S(2)}, u32[]{:S(2)}) collective-permute-start(bf16[272,128]{1,0:T(8,128)(2,1)S(1)} %shard_map.111.refs_2_), channel_id=1, source_target_pairs={{0,16},{4,20},{8,24},{12,28},{16,0},{20,4},{24,8},{28,12},{1,17},{... | collective-permute-start | bytes 208904 | tf_op jit(solution)/shard_map/ppermute | solution.py:643
  54.8 2.8 %collective-permute-start.17 = (bf16[272,128]{1,0:T(8,128)(2,1)S(1)}, bf16[272,128]{1,0:T(8,128)(2,1)S(1)}, u32[]{:S(2)}, u32[]{:S(2)}) collective-permute-start(bf16[272,128]{1,0:T(8,128)(2,1)S(1)} %shard_map.111.refs_2_), channel_id=1, source_target_pairs={{0,24},{4,28},{8,0},{12,4},{16,8},{20,12},{24,16},{28,20},{1,25},{... | collective-permute-start | bytes 208904 | tf_op jit(solution)/shard_map/ppermute | solution.py:643
  57.8 2.4 %collective-permute-start.21 = (bf16[256,512]{1,0:T(8,128)(2,1)S(1)}, bf16[256,512]{1,0:T(8,128)(2,1)S(1)}, u32[]{:S(2)}, u32[]{:S(2)}) collective-permute-start(bf16[256,512]{1,0:T(8,128)(2,1)S(1)} %get-tuple-element.64.refs_8_), channel_id=1, source_target_pairs={{0,16},{2,18},{3,19},{4,20},{6,22},{7,23},{9,25},{10,26},{11,27},{... | collective-permute-start | bytes 786440 | tf_op jit(solution)/shard_map/ppermute | solution.py:620
  60.2 8.3 %shard_map.114 = (bf16[1024,512]{1,0:T(8,128)(2,1)}, bf16[1024,512]{1,0:T(8,128)(2,1)}, bf16[1024,512]{1,0:T(8,128)(2,1)}) custom-call(bf16[1024,512]{1,0:T(8,128)(2,1)} %refs_0_.10, bf16[1024,512]{1,0:T(8,128)(2,1)} %refs_0_.11, bf16[1024,512]{1,0:T(8,128)(2,1)} %refs_1_.9, bf16[1024,512]{1,0:T(8,128)(2,1)S(1)} %get-tuple-element.57.refs_5_.refs_4_.refs_3_, ...), custom_call_target="tpu_custom_call" | custom-call | tf_op jit(solution)/shard_map/pallas_call | solution.py:156
  68.7 0.7 collective-permute-start.20
  69.5 1.2 %collective-permute-done.18.refs_4_ = bf16[256,128]{1,0:T(8,128)(2,1)S(1)} collective-permute-done((bf16[256,128]{1,0:T(8,128)(2,1)S(1)}, bf16[256,128]{1,0:T(8,128)(2,1)S(1)}, u32[]{:S(2)}, u32[]{:S(2)}) %collective-permute-start.18) | collective-permute-done | bytes 65568 | tf_op jit(solution)/shard_map/ppermute | solution.py:630
  70.7 4.1 %shard_map.117 = (bf16[1024,512]{1,0:T(8,128)(2,1)}, bf16[1024,512]{1,0:T(8,128)(2,1)}) custom-call(bf16[1024,512]{1,0:T(8,128)(2,1)} %refs_0_.11, bf16[1024,512]{1,0:T(8,128)(2,1)} %refs_1_.9, f32[5,16,256]{2,1,0:T(8,128)S(1)} %get-tuple-element.38.refs_3_.refs_2_.refs_7_.refs_4_, bf16[256,128]{1,0:T(8,128)(2,1)S(1)} %shard_map.115.refs_2_.refs_3_, ...), custom_call_target="tpu_custom_call" | custom-call | tf_op jit(solution)/shard_map/pallas_call | solution.py:156
  74.8 0.8 %select_convert_fusion = bf16[256,512]{1,0:T(8,128)(2,1)} fusion(f32[256,512]{1,0:T(8,128)S(1)} %get-tuple-element.70, bf16[256,512]{1,0:T(8,128)(2,1)S(1)} %collective-permute-done.21, bf16[256,512]{1,0:T(8,128)(2,1)S(1)} %collective-permute-done.20, bf16[256,512]{1,0:T(8,128)(2,1)S(1)} %shard_map.116.refs_8_, pred[]{:T(512)S(6)} %eq.3), kind=kLoop, calls=%fused_computation | loop fusion | flops 917504 | bytes 1572865 | tf_op jit(solution)/shard_map/convert_element_type | solution.py:794
  (30 shorter events, 1.4 us)
Async XLA Ops:
  0.6 26.4 %collective-permute-start.5 = (bf16[1024,512]{1,0:T(8,128)(2,1)}, bf16[1024,512]{1,0:T(8,128)(2,1)S(1)}, u32[]{:S(2)}, u32[]{:S(2)}) collective-permute-start(bf16[1024,512]{1,0:T(8,128)(2,1)} %refs_2_.6), channel_id=1, source_target_pairs={{0,1},{1,0},{2,3},{3,2},{4,5},{5,4},{6,7},{7,6},{8,9},{9,8},{10,11... | collective-permute-start | bytes 3145736 | tf_op jit(solution)/shard_map/ppermute | solution.py:675
  3.6 25.2 %collective-permute-start.7 = (bf16[1024,512]{1,0:T(8,128)(2,1)}, bf16[1024,512]{1,0:T(8,128)(2,1)S(1)}, u32[]{:S(2)}, u32[]{:S(2)}) collective-permute-start(bf16[1024,512]{1,0:T(8,128)(2,1)} %refs_2_.6), channel_id=1, source_target_pairs={{0,2},{1,3},{2,0},{3,1},{4,6},{5,7},{6,4},{7,5},{8,10},{9,11},{10,... | collective-permute-start | bytes 3145736 | tf_op jit(solution)/shard_map/ppermute | solution.py:675
  9.3 1.4 %collective-permute-start = (bf16[528,128]{1,0:T(8,128)(2,1)S(1)}, bf16[528,128]{1,0:T(8,128)(2,1)S(1)}, u32[]{:S(2)}, u32[]{:S(2)}) collective-permute-start(bf16[528,128]{1,0:T(8,128)(2,1)S(1)} %get-tuple-element.41.refs_1_), channel_id=1, source_target_pairs={{0,4},{4,0},{8,12},{12,8},{16,20},{20,16},{24,28},{28,24},{1,5},{5... | collective-permute-start | bytes 405512 | tf_op jit(solution)/shard_map/ppermute | solution.py:630
  10.8 10.2 %collective-permute-start.1 = (bf16[272,128]{1,0:T(8,128)(2,1)S(1)}, bf16[272,128]{1,0:T(8,128)(2,1)S(1)}, u32[]{:S(2)}, u32[]{:S(2)}) collective-permute-start(bf16[272,128]{1,0:T(8,128)(2,1)S(1)} %shard_map.102.refs_5_), channel_id=1, source_target_pairs={{0,8},{4,12},{8,16},{12,20},{16,24},{20,28},{24,0},{28,4},{1,9},{5... | collective-permute-start | bytes 208904 | tf_op jit(solution)/shard_map/ppermute | solution.py:643
  12.5 8.6 %collective-permute-start.2 = (bf16[272,128]{1,0:T(8,128)(2,1)S(1)}, bf16[272,128]{1,0:T(8,128)(2,1)S(1)}, u32[]{:S(2)}, u32[]{:S(2)}) collective-permute-start(bf16[272,128]{1,0:T(8,128)(2,1)S(1)} %shard_map.102.refs_5_), channel_id=1, source_target_pairs={{0,16},{4,20},{8,24},{12,28},{16,0},{20,4},{24,8},{28,12},{1,17},{... | collective-permute-start | bytes 208904 | tf_op jit(solution)/shard_map/ppermute | solution.py:643
  15.1 6.0 %collective-permute-start.3 = (bf16[272,128]{1,0:T(8,128)(2,1)S(1)}, bf16[272,128]{1,0:T(8,128)(2,1)S(1)}, u32[]{:S(2)}, u32[]{:S(2)}) collective-permute-start(bf16[272,128]{1,0:T(8,128)(2,1)S(1)} %shard_map.102.refs_5_), channel_id=1, source_target_pairs={{0,24},{4,28},{8,0},{12,4},{16,8},{20,12},{24,16},{28,20},{1,25},{... | collective-permute-start | bytes 208904 | tf_op jit(solution)/shard_map/ppermute | solution.py:643
  21.1 1.3 %collective-permute-start.4 = (bf16[256,128]{1,0:T(8,128)(2,1)S(1)}, bf16[256,128]{1,0:T(8,128)(2,1)S(1)}, u32[]{:S(2)}, u32[]{:S(2)}) collective-permute-start(bf16[256,128]{1,0:T(8,128)(2,1)S(1)} %shard_map.104.refs_3_), channel_id=1, source_target_pairs={{0,4},{4,0},{8,12},{12,8},{16,20},{20,16},{24,28},{28,24},{1,5},{5... | collective-permute-start | bytes 196616 | tf_op jit(solution)/shard_map/ppermute | solution.py:630
  27.0 13.3 %collective-permute-start.6 = (bf16[1024,256]{1,0:T(8,128)(2,1)S(1)}, bf16[1024,256]{1,0:T(8,128)(2,1)S(1)}, u32[]{:S(2)}, u32[]{:S(2)}) collective-permute-start(bf16[1024,256]{1,0:T(8,128)(2,1)S(1)} %get-tuple-element.47), channel_id=1, source_target_pairs={{0,2},{1,3},{2,0},{3,1},{4,6},{5,7},{6,4},{7,5},{8,10},{9,11},{10,... | collective-permute-start | bytes 1572872 | tf_op jit(solution)/shard_map/ppermute | solution.py:675
  28.9 12.6 %collective-permute-start.8 = (bf16[1024,256]{1,0:T(8,128)(2,1)S(1)}, bf16[1024,256]{1,0:T(8,128)(2,1)S(1)}, u32[]{:S(2)}, u32[]{:S(2)}) collective-permute-start(bf16[1024,256]{1,0:T(8,128)(2,1)S(1)} %get-tuple-element.49), channel_id=1, source_target_pairs={{0,1},{1,0},{2,3},{3,2},{4,5},{5,4},{6,7},{7,6},{8,9},{9,8},{10,11... | collective-permute-start | bytes 1572872 | tf_op jit(solution)/shard_map/ppermute | solution.py:675
  36.2 1.6 %collective-permute-start.9 = (bf16[256,512]{1,0:T(8,128)(2,1)S(1)}, bf16[256,512]{1,0:T(8,128)(2,1)S(1)}, u32[]{:S(2)}, u32[]{:S(2)}) collective-permute-start(bf16[256,512]{1,0:T(8,128)(2,1)S(1)} %get-tuple-element.53.refs_4_), channel_id=1, source_target_pairs={{0,4},{4,0},{8,12},{12,8},{16,20},{20,16},{24,28},{28,24},{1,5},{5... | collective-permute-start | bytes 786440 | tf_op jit(solution)/shard_map/ppermute | solution.py:709
  36.2 1.9 %collective-permute-start.10 = (bf16[256,512]{1,0:T(8,128)(2,1)S(1)}, bf16[256,512]{1,0:T(8,128)(2,1)S(1)}, u32[]{:S(2)}, u32[]{:S(2)}) collective-permute-start(bf16[256,512]{1,0:T(8,128)(2,1)S(1)} %get-tuple-element.54), channel_id=1, source_target_pairs={{0,4},{4,0},{8,12},{12,8},{16,20},{20,16},{24,28},{28,24},{1,5},{5... | collective-permute-start | bytes 786440 | tf_op jit(solution)/shard_map/ppermute | solution.py:709
  36.7 1.8 %collective-permute-start.11 = (bf16[256,512]{1,0:T(8,128)(2,1)S(1)}, bf16[256,512]{1,0:T(8,128)(2,1)S(1)}, u32[]{:S(2)}, u32[]{:S(2)}) collective-permute-start(bf16[256,512]{1,0:T(8,128)(2,1)S(1)} %get-tuple-element.55), channel_id=1, source_target_pairs={{0,4},{4,0},{8,12},{12,8},{16,20},{20,16},{24,28},{28,24},{1,5},{5... | collective-permute-start | bytes 786440 | tf_op jit(solution)/shard_map/ppermute | solution.py:709
  38.7 18.9 %collective-permute-start.12 = (bf16[2,256,512]{2,1,0:T(8,128)(2,1)S(1)}, bf16[2,256,512]{2,1,0:T(8,128)(2,1)S(1)}, u32[]{:S(2)}, u32[]{:S(2)}) collective-permute-start(bf16[2,256,512]{2,1,0:T(8,128)(2,1)S(1)} %get-tuple-element.59), channel_id=1, source_target_pairs={{0,8},{1,9},{2,10},{3,11},{4,12},{5,13},{6,14},{7,15},{8,0},{9,1},... | collective-permute-start | bytes 1572872 | tf_op jit(solution)/shard_map/ppermute | solution.py:620
  46.6 1.9 %collective-permute-start.13 = (bf16[256,512]{1,0:T(8,128)(2,1)S(1)}, bf16[256,512]{1,0:T(8,128)(2,1)S(1)}, u32[]{:S(2)}, u32[]{:S(2)}) collective-permute-start(bf16[256,512]{1,0:T(8,128)(2,1)S(1)} %get-tuple-element.61), channel_id=1, source_target_pairs={{0,4},{4,0},{8,12},{12,8},{16,20},{20,16},{24,28},{28,24},{1,5},{5... | collective-permute-start | bytes 786440 | tf_op jit(solution)/shard_map/ppermute | solution.py:709
  46.7 1.7 %collective-permute-start.14 = (bf16[528,128]{1,0:T(8,128)(2,1)S(1)}, bf16[528,128]{1,0:T(8,128)(2,1)S(1)}, u32[]{:S(2)}, u32[]{:S(2)}) collective-permute-start(bf16[528,128]{1,0:T(8,128)(2,1)S(1)} %get-tuple-element.63.refs_1_), channel_id=1, source_target_pairs={{0,4},{4,0},{8,12},{12,8},{16,20},{20,16},{24,28},{28,24},{1,5},{5... | collective-permute-start | bytes 405512 | tf_op jit(solution)/shard_map/ppermute | solution.py:630
  48.6 20.0 %collective-permute-start.19 = (bf16[256,512]{1,0:T(8,128)(2,1)S(1)}, bf16[256,512]{1,0:T(8,128)(2,1)S(1)}, u32[]{:S(2)}, u32[]{:S(2)}) collective-permute-start(bf16[256,512]{1,0:T(8,128)(2,1)S(1)} %shard_map.112.refs_2_.refs_6_.refs_10_.refs_5_.refs_0_), channel_id=1, source_target_pairs={{0,8},{2,10},{4,12},{6,14},{9,1},{11,3},{13,5},{15,7},{16,24},{18,... | collective-permute-start | bytes 786440 | tf_op jit(solution)/shard_map/ppermute | solution.py:620
  52.1 16.4 %collective-permute-start.15 = (bf16[272,128]{1,0:T(8,128)(2,1)S(1)}, bf16[272,128]{1,0:T(8,128)(2,1)S(1)}, u32[]{:S(2)}, u32[]{:S(2)}) collective-permute-start(bf16[272,128]{1,0:T(8,128)(2,1)S(1)} %shard_map.111.refs_2_), channel_id=1, source_target_pairs={{0,8},{4,12},{8,16},{12,20},{16,24},{20,28},{24,0},{28,4},{1,9},{5... | collective-permute-start | bytes 208904 | tf_op jit(solution)/shard_map/ppermute | solution.py:643
  52.1 16.4 %collective-permute-start.16 = (bf16[272,128]{1,0:T(8,128)(2,1)S(1)}, bf16[272,128]{1,0:T(8,128)(2,1)S(1)}, u32[]{:S(2)}, u32[]{:S(2)}) collective-permute-start(bf16[272,128]{1,0:T(8,128)(2,1)S(1)} %shard_map.111.refs_2_), channel_id=1, source_target_pairs={{0,16},{4,20},{8,24},{12,28},{16,0},{20,4},{24,8},{28,12},{1,17},{... | collective-permute-start | bytes 208904 | tf_op jit(solution)/shard_map/ppermute | solution.py:643
  54.8 13.7 %collective-permute-start.17 = (bf16[272,128]{1,0:T(8,128)(2,1)S(1)}, bf16[272,128]{1,0:T(8,128)(2,1)S(1)}, u32[]{:S(2)}, u32[]{:S(2)}) collective-permute-start(bf16[272,128]{1,0:T(8,128)(2,1)S(1)} %shard_map.111.refs_2_), channel_id=1, source_target_pairs={{0,24},{4,28},{8,0},{12,4},{16,8},{20,12},{24,16},{28,20},{1,25},{... | collective-permute-start | bytes 208904 | tf_op jit(solution)/shard_map/ppermute | solution.py:643
  57.8 17.0 %collective-permute-start.21 = (bf16[256,512]{1,0:T(8,128)(2,1)S(1)}, bf16[256,512]{1,0:T(8,128)(2,1)S(1)}, u32[]{:S(2)}, u32[]{:S(2)}) collective-permute-start(bf16[256,512]{1,0:T(8,128)(2,1)S(1)} %get-tuple-element.64.refs_8_), channel_id=1, source_target_pairs={{0,16},{2,18},{3,19},{4,20},{6,22},{7,23},{9,25},{10,26},{11,27},{... | collective-permute-start | bytes 786440 | tf_op jit(solution)/shard_map/ppermute | solution.py:620
  68.7 6.1 %collective-permute-start.20 = (bf16[256,512]{1,0:T(8,128)(2,1)S(1)}, bf16[256,512]{1,0:T(8,128)(2,1)S(1)}, u32[]{:S(2)}, u32[]{:S(2)}) collective-permute-start(bf16[256,512]{1,0:T(8,128)(2,1)S(1)} %shard_map.116.refs_8_), channel_id=1, source_target_pairs={{1,17},{5,21},{8,24},{12,28},{19,3},{23,7},{26,10},{30,14}} | collective-permute-start | bytes 786440 | tf_op jit(solution)/shard_map/ppermute | solution.py:620
  69.4 1.3 %collective-permute-start.18 = (bf16[256,128]{1,0:T(8,128)(2,1)S(1)}, bf16[256,128]{1,0:T(8,128)(2,1)S(1)}, u32[]{:S(2)}, u32[]{:S(2)}) collective-permute-start(bf16[256,128]{1,0:T(8,128)(2,1)S(1)} %shard_map.115.refs_2_.refs_3_), channel_id=1, source_target_pairs={{0,4},{4,0},{8,12},{12,8},{16,20},{20,16},{24,28},{28,24},{1,5},{5... | collective-permute-start | bytes 196616 | tf_op jit(solution)/shard_map/ppermute | solution.py:630
